TPU v7x, 32 devices: a whole 2x2x4 slice. The times are simulated.
32 devices in a mesh: dp: 8 (over y, x, core), head: 4 (over z).
Axes of the slice: x: 2, y: 2, z: 4, core: 2. Of those that a mesh axis runs over, the one named last changes fastest.
Arguments:
- query_rows: bfloat16 [8, 512, 3072], P('dp', 'head'), may hold values from -6 to 6
- key_rows: bfloat16 [8, 512, 3072], P('dp', 'head'), may hold values from -6 to 6
- value_rows: bfloat16 [8, 512, 3072], P('dp', 'head'), may hold values from -6 to 6
- out_grad: bfloat16 [8, 512, 6144], P('dp', 'head'), may hold values from -6 to 6
- out_weight: bfloat16 [3072, 6144], P('head', 'dp'), may hold values from -0.109375 to 0.109375
- token_order: int32 [8, 512], P('dp'), may hold values from 0 to 511, as said below
- tile_index: int32 [8, 24, 4, 4], P('dp', 'head'), may hold values from 0 to 3, as said below
- tile_count: int32 [8, 24, 4], P('dp', 'head'), may hold values from 1 to 4, as said below
Outputs:
- attention: bfloat16 [8, 512, 3072], P('dp', None, 'head')
- query_grad: bfloat16 [8, 512, 3072], P('dp', 'head')
- key_grad: bfloat16 [8, 512, 3072], P('dp', 'head')
- value_grad: bfloat16 [8, 512, 3072], P('dp', 'head')
- weight_grad: bfloat16 [3072, 6144], P('head', 'dp')
Inputs may be any that keep to these rules, and one draw needn't show every extreme that they name: `token_order`: each clip's row is a permutation of the positions. `tile_index`: slot 0 of every list names the query cube itself; the entries of one list differ. Only the first tile_count[c, h, b] slots of list (c, h, b) are used.
All inputs are finite; a program needn't handle non-finite values.
Results may differ from a plain program's by a relative error of at most 0.015.
Values may be sent and summed in bfloat16 or wider, within the bound.
No kernel may reach another device: no remote copies, remote signals or barrier semaphores. Data moves between devices by JAX's collectives and lax.ppermute only.
A program may use at most 128 MiB of HBM per device.

v0:
```python
import functools
import math

import jax
import jax.numpy as jnp
from jax import lax
from jax.experimental import pallas as pl
from jax.experimental.pallas import tpu as pltpu
from jax.sharding import PartitionSpec as P

HEAD_DIM = 128
CUBE_TOKENS = 128
LANES = 128
CHUNKS = 3

masked_score = -1e30
scale = 1.0 / math.sqrt(HEAD_DIM)
log2_e = math.log2(math.e)

BF16 = jnp.bfloat16
F32 = jnp.float32
NT = (((1,), (1,)), ((), ()))
NN = (((1,), (0,)), ((), ()))


def dot(a, b, dims=NN):
    return lax.dot_general(a, b, dims, preferred_element_type=F32)


def params(limit_mib=48):
    return pltpu.CompilerParams(vmem_limit_bytes=limit_mib * 1024 * 1024)


def bit_reversed(count):
    bits = count.bit_length() - 1
    return [sum(((p >> i) & 1) << (bits - 1 - i) for i in range(bits)) for p in range(count)]


def pack_kernel(place, q_ref, k_ref, v_ref, *outs):
    width = outs[0].shape[2]
    for s, out in enumerate(outs):
        columns = pl.ds(pl.multiple_of(place[s] * width, LANES), width)
        for i, rows in enumerate((q_ref, k_ref, v_ref)):
            out[i] = rows[0, :, columns]


def pack(place, q, k, v):
    group = place.shape[0]
    rows, total = q.shape[1:]
    shape = jax.ShapeDtypeStruct((3, rows, total // group), BF16)
    return pl.pallas_call(
        pack_kernel,
        out_shape=[shape] * group,
        grid_spec=pltpu.PrefetchScalarGridSpec(
            num_scalar_prefetch=1,
            in_specs=[pl.BlockSpec(memory_space=pltpu.VMEM)] * 3,
            out_specs=[pl.BlockSpec(memory_space=pltpu.VMEM)] * group,
        ),
        compiler_params=params(),
    )(place, q, k, v)


def unpack_kernel(group, place, *refs):
    parts, outs = refs[:group], refs[group:]
    width = parts[0].shape[2]
    for s, part in enumerate(parts):
        columns = pl.ds(pl.multiple_of(place[s] * width, LANES), width)
        for i, out in enumerate(outs):
            out[0, :, columns] = part[i]


def unpack(place, parts):
    group = place.shape[0]
    _, rows, width = parts[0].shape
    shape = jax.ShapeDtypeStruct((1, rows, width * group), BF16)
    return pl.pallas_call(
        functools.partial(unpack_kernel, group),
        out_shape=[shape] * 3,
        grid_spec=pltpu.PrefetchScalarGridSpec(
            num_scalar_prefetch=1,
            in_specs=[pl.BlockSpec(memory_space=pltpu.VMEM)] * group,
            out_specs=[pl.BlockSpec(memory_space=pltpu.VMEM)] * 3,
        ),
        compiler_params=params(),
    )(place, *parts)


def forward_kernel(group, place, order_ref, bias_ref, *refs):
    parts = refs[:group]
    att_ref, att_t_ref, weight_ref, q_t_ref, k_ref, v_ref, cube_ref, q_ref = refs[group:]
    rows = parts[0].shape[1]
    total = q_ref.shape[0]

    @pl.when(pl.program_id(0) == 0)
    def _():
        token = lax.broadcasted_iota(jnp.int32, (total, total), 0)
        onehot = jnp.where(token == order_ref[...], 1.0, 0.0).astype(BF16)
        position = lax.broadcasted_iota(jnp.int32, (total, LANES), 0)
        cube = lax.broadcasted_iota(jnp.int32, (total, LANES), 1)
        block = jnp.where(lax.div(position, CUBE_TOKENS) == cube, 1.0, 0.0).astype(BF16)
        cube_ref[...] = dot(onehot, block).astype(BF16)

    for s, part in enumerate(parts):
        here = pl.ds(pl.multiple_of(place[s] * rows, rows), rows)
        q_ref[here, :] = part[0]
        k_ref[here, :] = part[1]
        v_ref[here, :] = part[2]
    cubes = cube_ref[...]
    q, k, v = q_ref[...], k_ref[...], v_ref[...]
    bias = dot(cubes, bias_ref[0]).astype(BF16)
    scores = dot(
        jnp.concatenate([q, bias], axis=1), jnp.concatenate([k, cubes], axis=1), NT
    ) * (scale * log2_e)
    raised = jnp.exp2(scores - jnp.max(scores, axis=1, keepdims=True))
    weights = (raised * (1.0 / jnp.sum(raised, axis=1, keepdims=True))).astype(BF16)
    weight_ref[0] = weights
    output = dot(weights, v)
    att_ref[...] = output.astype(BF16)
    att_t_ref[...] = output.T.astype(BF16)
    q_t_ref[...] = q.astype(F32).T.astype(BF16)


def forward(place, order, bias, parts):
    group = place.shape[0]
    _, rows, width = parts[0].shape
    total = rows * group
    heads = width // HEAD_DIM
    column = pl.BlockSpec((total, HEAD_DIM), lambda h, *_: (0, h))
    row = pl.BlockSpec((HEAD_DIM, total), lambda h, *_: (h, 0))
    return pl.pallas_call(
        functools.partial(forward_kernel, group),
        out_shape=[
            jax.ShapeDtypeStruct((total, width), BF16),
            jax.ShapeDtypeStruct((width, total), BF16),
            jax.ShapeDtypeStruct((heads, total, total), BF16),
            jax.ShapeDtypeStruct((width, total), BF16),
            jax.ShapeDtypeStruct((total, width), BF16),
            jax.ShapeDtypeStruct((total, width), BF16),
        ],
        grid_spec=pltpu.PrefetchScalarGridSpec(
            num_scalar_prefetch=1,
            grid=(heads,),
            in_specs=[
                pl.BlockSpec((1, total), lambda h, *_: (0, 0)),
                pl.BlockSpec((1, LANES, LANES), lambda h, *_: (h, 0, 0)),
            ]
            + [pl.BlockSpec((3, rows, HEAD_DIM), lambda h, *_: (0, 0, h))] * group,
            out_specs=[
                column,
                row,
                pl.BlockSpec((1, total, total), lambda h, *_: (h, 0, 0)),
                row,
                column,
                column,
            ],
            scratch_shapes=[
                pltpu.VMEM((total, LANES), BF16),
                pltpu.VMEM((total, HEAD_DIM), BF16),
            ],
        ),
        compiler_params=params(),
    )(place, order, bias, *parts)


def backward_kernel(group, place, g_ref, att_ref, weight_ref, q_t_ref, k_ref, v_ref, *refs):
    outs, held = refs[:group], refs[group]
    rows = outs[0].shape[1]
    grad = g_ref[...]
    weights = weight_ref[0]
    grad_float = grad.astype(F32)
    delta = jnp.sum(grad_float * att_ref[...].astype(F32), axis=1, keepdims=True)
    diff = (weights.astype(F32) * (dot(grad, v_ref[...], NT) - delta)).astype(BF16)
    held[0] = (dot(diff, k_ref[...]) * scale).astype(BF16)
    held[1] = (dot(q_t_ref[...], diff) * scale).T.astype(BF16)
    held[2] = dot(grad_float.T.astype(BF16), weights).T.astype(BF16)
    for s, out in enumerate(outs):
        here = pl.ds(pl.multiple_of(place[s] * rows, rows), rows)
        out[...] = held[:, here, :]


def backward(place, grad, att, weights, q_t, k, v):
    group = place.shape[0]
    total, width = grad.shape
    rows = total // group
    heads = width // HEAD_DIM
    column = pl.BlockSpec((total, HEAD_DIM), lambda h, *_: (0, h))
    row = pl.BlockSpec((HEAD_DIM, total), lambda h, *_: (h, 0))
    return pl.pallas_call(
        functools.partial(backward_kernel, group),
        out_shape=[jax.ShapeDtypeStruct((3, rows, width), BF16)] * group,
        grid_spec=pltpu.PrefetchScalarGridSpec(
            num_scalar_prefetch=1,
            grid=(heads,),
            in_specs=[
                column,
                column,
                pl.BlockSpec((1, total, total), lambda h, *_: (h, 0, 0)),
                row,
                column,
                column,
            ],
            out_specs=[pl.BlockSpec((3, rows, HEAD_DIM), lambda h, *_: (0, 0, h))] * group,
            scratch_shapes=[pltpu.VMEM((3, total, HEAD_DIM), BF16)],
        ),
        compiler_params=params(),
    )(place, grad, att, weights, q_t, k, v)


def project_kernel(count, blocks, rows_ref, *refs):
    weights, before, out = refs[:count], refs[count:-1], refs[-1]
    width = weights[0].shape[1]
    total = before[0][...] if before else None
    for p, weight in enumerate(weights):
        columns = pl.ds(pl.multiple_of(blocks[p] * width, LANES), width)
        term = dot(rows_ref[:, columns], weight[...], NT)
        total = term if total is None else total + term
    out[...] = total.astype(out.dtype)


def project(blocks, rows, weights, chunk, before, dtype):
    count = len(weights)
    tokens, width = rows.shape[0], rows.shape[1] // count
    heads = weights[0].shape[0]
    before = [] if before is None else [before]
    whole = pl.BlockSpec((tokens, heads), lambda i, *_: (0, 0))
    return pl.pallas_call(
        functools.partial(project_kernel, count),
        out_shape=jax.ShapeDtypeStruct((tokens, heads), dtype),
        grid_spec=pltpu.PrefetchScalarGridSpec(
            num_scalar_prefetch=1,
            grid=(1,),
            in_specs=[pl.BlockSpec(rows.shape, lambda i, *_: (0, 0))]
            + [pl.BlockSpec((heads, width), lambda i, *_: (0, chunk))] * count
            + [whole] * len(before),
            out_specs=whole,
        ),
        compiler_params=params(),
    )(blocks, rows, *weights, *before)


def outer_kernel(blocks, att_t_ref, rows_ref, keep_ref, send_ref):
    half, _, width = keep_ref.shape
    att_t = att_t_ref[...]
    for p in range(2 * half):
        columns = pl.ds(pl.multiple_of(blocks[p] * width, LANES), width)
        out = keep_ref if p < half else send_ref
        out[p % half] = dot(att_t, rows_ref[:, columns]).astype(BF16)


def outer(blocks, att_t, rows):
    count = blocks.shape[0]
    heads, width = att_t.shape[0], rows.shape[1] // count
    shape = jax.ShapeDtypeStruct((count // 2, heads, width), BF16)
    return pl.pallas_call(
        outer_kernel,
        out_shape=[shape] * 2,
        grid_spec=pltpu.PrefetchScalarGridSpec(
            num_scalar_prefetch=1,
            in_specs=[pl.BlockSpec(memory_space=pltpu.VMEM)] * 2,
            out_specs=[pl.BlockSpec(memory_space=pltpu.VMEM)] * 2,
        ),
        compiler_params=params(),
    )(blocks, att_t, rows)


def swap(value, axis, size, mask):
    return lax.ppermute(value, axis, [(i, i ^ mask) for i in range(size)])


def scatter_sum(keep, send, dp):
    steps = dp.bit_length() - 1
    kept = keep.astype(F32)
    for step in range(steps):
        arrived = swap(send, "dp", dp, 1 << step).astype(F32)
        kept = kept + arrived
        if step < steps - 1:
            half = kept.shape[0] // 2
            send, kept = kept[half:].astype(BF16), kept[:half]
    return kept[0].astype(BF16)


def gather_weight(weight, dp):
    held = [weight]
    mask = dp // 2
    while mask:
        held = held + [swap(part, "dp", dp, mask) for part in held]
        mask //= 2
    return held


def local(
    dp,
    group,
    query_rows,
    key_rows,
    value_rows,
    out_grad,
    out_weight,
    token_order,
    tile_index,
    tile_count,
):
    tokens_here, model = out_grad.shape[1:]
    part = model // dp // CHUNKS
    place = jnp.bitwise_xor(lax.axis_index("head"), jnp.arange(group, dtype=jnp.int32))
    blocks = jnp.bitwise_xor(lax.axis_index("dp"), jnp.array(bit_reversed(dp), jnp.int32))

    packed = pack(place, query_rows, key_rows, value_rows)
    parts = [packed[0]] + [swap(packed[s], "head", group, s) for s in range(1, group)]

    pieces = out_grad.reshape(tokens_here, dp, CHUNKS, part)
    gathered = [
        lax.all_gather(
            pieces[:, :, j].reshape(tokens_here, dp * part), "head", axis=0, tiled=True
        )
        for j in range(CHUNKS)
    ]
    weights_full = gather_weight(out_weight, dp)

    tiles, counts = tile_index[0], tile_count[0]
    heads, cubes, slots = tiles.shape
    used = jnp.arange(slots, dtype=jnp.int32) < counts[:, :, None]
    listed = tiles[..., None] == jnp.arange(LANES, dtype=jnp.int32)
    allowed = jnp.any(listed & used[..., None], axis=2)
    bias = jnp.where(allowed, 0.0, masked_score).astype(BF16)
    bias = jnp.pad(bias, ((0, 0), (0, LANES - cubes), (0, 0)))

    att, att_t, weights, q_t, k, v = forward(place, token_order, bias, parts)

    grad = None
    sums = []
    for j in range(CHUNKS):
        last = j == CHUNKS - 1
        grad = project(blocks, gathered[j], weights_full, j, grad, BF16 if last else F32)
        sums.append(scatter_sum(*outer(blocks, att_t, gathered[j]), dp))

    back = backward(place, grad, att, weights, q_t, k, v)
    back = [back[0]] + [swap(back[s], "head", group, s) for s in range(1, group)]
    query_back, key_back, value_back = unpack(place, back)
    return (att[None], query_back, key_back, value_back, jnp.concatenate(sums, axis=1))


def solution(mesh):
    placed = (
        P("dp", "head", None),
        P("dp", "head", None),
        P("dp", "head", None),
        P("dp", "head", None),
        P("head", "dp"),
        P("dp", None),
        P("dp", "head", None, None),
        P("dp", "head", None),
    )
    return jax.shard_map(
        functools.partial(local, mesh.shape["dp"], mesh.shape["head"]),
        mesh=mesh,
        in_specs=placed,
        out_specs=(
            P("dp", None, "head"),
            P("dp", "head", None),
            P("dp", "head", None),
            P("dp", "head", None),
            P("head", "dp"),
        ),
        check_vma=False,
    )
```

profile of v0, /device:TPU:9, one launch (start us, length us, event | category | flops | bytes accessed | tf_op | source)
XLA Modules:
  0.0 311.7 jit_solution(9014144846376222281)
XLA Ops:
  7.2 1.9 copy.27
  13.3 1.3 collective-permute-start.3
  14.6 1.2 collective-permute-start.4
  15.8 1.1 copy-done.12
  17.0 1.1 copy-done.13
  18.1 1.1 copy-done.14
  19.2 1.7 shard_map.128
  22.7 1.6 collective-permute-start.6
  24.3 2.3 collective-permute-start.1
  26.7 46.6 %collective-permute-done.refs_1_ = bf16[3,128,768]{2,1,0:T(8,128)(2,1)} collective-permute-done((bf16[3,128,768]{2,1,0:T(8,128)(2,1)}, bf16[3,128,768]{2,1,0:T(8,128)(2,1)}, u32[]{:S(2)}, u32[]{:S(2)}) %collective-permute-start) | collective-permute-done | bytes 589856 | tf_op jit(solution)/shard_map/ppermute | solution.py:267
  73.3 3.0 collective-permute-start.2
  76.3 1.4 copy.25
  78.6 2.0 collective-permute-start.8
  81.2 26.5 %collective-permute-done.2.refs_3_ = bf16[3,128,768]{2,1,0:T(8,128)(2,1)} collective-permute-done((bf16[3,128,768]{2,1,0:T(8,128)(2,1)}, bf16[3,128,768]{2,1,0:T(8,128)(2,1)}, u32[]{:S(2)}, u32[]{:S(2)}) %collective-permute-start.2) | collective-permute-done | bytes 589856 | tf_op jit(solution)/shard_map/ppermute | solution.py:267
  107.7 1.1 copy-done.22
  108.8 9.0 %shard_map.129 = (bf16[512,768]{1,0:T(8,128)(2,1)}, bf16[768,512]{1,0:T(8,128)(2,1)S(1)}, bf16[6,512,512]{2,1,0:T(8,128)(2,1)}, bf16[768,512]{1,0:T(8,128)(2,1)S...) custom-call(s32[4]{0:T(128)S(1)} %iota_xor_fusion.place, s32[1,512]{1,0:T(1,128)S(1)} %copy-done.23, ...), custom_call_target="tpu_custom_call" | custom-call | tf_op jit(solution)/shard_map/pallas_call | solution.py:130
  121.3 1.6 copy-done.1
  122.9 1.1 copy-done.5
  124.1 3.5 %shard_map.135 = (bf16[4,768,256]{2,1,0:T(8,128)(2,1)S(1)}, bf16[4,768,256]{2,1,0:T(8,128)(2,1)}) custom-call(s32[8]{0:T(128)S(1)} %broadcast_xor_fusion.blocks, bf16[768,512]{1,0:T(8,128)(2,1)S(1)} %copy-done.5, bf16[512,2048]{1,0:T(8,128)(2,1)S(1)} %copy-done.1), custom_call_target="tpu_custom_call" | custom-call | tf_op jit(solution)/shard_map/pallas_call | solution.py:254
  127.5 1.2 copy-done.10
  129.1 13.5 %all-gather.6.cloned.1.call-done.rows_ref = bf16[512,2048]{1,0:T(8,128)(2,1)} async-done(((bf16[128,2048]{1,0:T(8,128)(2,1)}), bf16[512,2048]{1,0:T(8,128)(2,1)}) %all-gather.6.cloned.1.call-update) | async-done | bytes 2097168 | tf_op jit(solution)/shard_map/all_gather | solution.py:313
  142.6 1.6 copy-done.2
  144.2 1.1 copy-done.6
  145.3 3.5 %shard_map.136 = (bf16[4,768,256]{2,1,0:T(8,128)(2,1)S(1)}, bf16[4,768,256]{2,1,0:T(8,128)(2,1)}) custom-call(s32[8]{0:T(128)S(1)} %broadcast_xor_fusion.blocks, bf16[768,512]{1,0:T(8,128)(2,1)S(1)} %copy-done.6, bf16[512,2048]{1,0:T(8,128)(2,1)S(1)} %copy-done.2), custom_call_target="tpu_custom_call" | custom-call | tf_op jit(solution)/shard_map/pallas_call | solution.py:254
  148.9 1.1 copy-done.8
  151.5 37.4 %all-gather.4.cloned.1.call-done.rows_ref = bf16[512,2048]{1,0:T(8,128)(2,1)} async-done(((bf16[128,2048]{1,0:T(8,128)(2,1)}), bf16[512,2048]{1,0:T(8,128)(2,1)}) %all-gather.4.cloned.1.call-update) | async-done | bytes 2097168 | tf_op jit(solution)/shard_map/all_gather | solution.py:313
  188.9 1.6 copy-done.3
  190.5 1.1 copy-done.7
  191.6 2.3 shard_map.137
  195.0 5.8 %shard_map.130.refs_8_ = f32[512,768]{1,0:T(8,128)} custom-call(s32[8]{0:T(128)S(1)} %broadcast_xor_fusion.blocks, bf16[512,2048]{1,0:T(8,128)(2,1)} %all-gather.8.cloned.1.call-done.rows_ref, bf16[768,768]{1,0:T(8,128)(2,1)S(1)} %copy-done, bf16[768,768]{1,0:T(8,128)(2,1)S(1)} %collective-permute-done.3.refs_1_, ...), custom_call_target="tpu_custom_call" | custom-call | tf_op jit(solution)/shard_map/pallas_call | solution.py:226
  200.8 6.4 %shard_map.131.refs_8_ = f32[512,768]{1,0:T(8,128)} custom-call(s32[8]{0:T(128)S(1)} %broadcast_xor_fusion.blocks, bf16[512,2048]{1,0:T(8,128)(2,1)} %all-gather.6.cloned.1.call-done.rows_ref, bf16[768,768]{1,0:T(8,128)(2,1)S(1)} %copy-done, bf16[768,768]{1,0:T(8,128)(2,1)S(1)} %collective-permute-done.3.refs_1_, ...), custom_call_target="tpu_custom_call" | custom-call | tf_op jit(solution)/shard_map/pallas_call | solution.py:226
  207.2 5.2 %shard_map.132.g_ref = bf16[512,768]{1,0:T(8,128)(2,1)S(1)} custom-call(s32[8]{0:T(128)S(1)} %broadcast_xor_fusion.blocks, bf16[512,2048]{1,0:T(8,128)(2,1)} %all-gather.4.cloned.1.call-done.rows_ref, bf16[768,768]{1,0:T(8,128)(2,1)S(1)} %copy-done, bf16[768,768]{1,0:T(8,128)(2,1)S(1)} %collective-permute-done.3.refs_1_, ...), custom_call_target="tpu_custom_call" | custom-call | tf_op jit(solution)/shard_map/pallas_call | solution.py:226
  212.4 7.7 %shard_map.133 = (bf16[3,128,768]{2,1,0:T(8,128)(2,1)S(1)}, bf16[3,128,768]{2,1,0:T(8,128)(2,1)S(1)}, bf16[3,128,768]{2,1,0:T(8,128)(2,1)S(1)}, bf16[3,128,768]{2,1,0:T(8,128)(2,1)S(1)}) custom-call(s32[4]{0:T(128)S(1)} %iota_xor_fusion.place, bf16[512,768]{1,0:T(8,128)(2,1)S(1)} %shard_map.132.g_ref, bf16[512,768]{1,0:T(8,128)(2,1)S(1)} %copy-done.15, ...), custom_call_target="tpu_custom_call" | custom-call | tf_op jit(solution)/shard_map/pallas_call | solution.py:188
  220.1 2.0 collective-permute-start.10
  223.4 1.8 convert_add_fusion.2
  225.2 1.2 collective-permute-start.14
  226.5 1.7 convert_add_fusion.1
  228.3 1.2 collective-permute-start.17
  229.6 1.8 convert_add_fusion
  231.4 15.7 %collective-permute-done.10.refs_1_ = bf16[3,128,768]{2,1,0:T(8,128)(2,1)S(1)} collective-permute-done((bf16[3,128,768]{2,1,0:T(8,128)(2,1)S(1)}, bf16[3,128,768]{2,1,0:T(8,128)(2,1)S(1)}, u32[]{:S(2)}, u32[]{:S(2)}) %collective-permute-start.10) | collective-permute-done | bytes 589856 | tf_op jit(solution)/shard_map/ppermute | solution.py:267
  249.0 25.8 %collective-permute-done.12.refs_3_ = bf16[3,128,768]{2,1,0:T(8,128)(2,1)S(1)} collective-permute-done((bf16[3,128,768]{2,1,0:T(8,128)(2,1)S(1)}, bf16[3,128,768]{2,1,0:T(8,128)(2,1)S(1)}, u32[]{:S(2)}, u32[]{:S(2)}) %collective-permute-start.12) | collective-permute-done | bytes 589856 | tf_op jit(solution)/shard_map/ppermute | solution.py:267
  274.9 2.1 shard_map.134
  277.2 1.2 collective-permute-start.15
  279.3 1.2 collective-permute-start.21
  280.5 6.7 %collective-permute-done.15 = bf16[1,768,256]{2,1,0:T(8,128)(2,1)S(1)} collective-permute-done((bf16[1,768,256]{2,1,0:T(8,128)(2,1)S(1)}, bf16[1,768,256]{2,1,0:T(8,128)(2,1)S(1)}, u32[]{:S(2)}, u32[]{:S(2)}) %collective-permute-start.15) | collective-permute-done | bytes 393248 | tf_op jit(solution)/shard_map/ppermute | solution.py:267
  287.3 8.3 %collective-permute-done.18 = bf16[1,768,256]{2,1,0:T(8,128)(2,1)S(1)} collective-permute-done((bf16[1,768,256]{2,1,0:T(8,128)(2,1)S(1)}, bf16[1,768,256]{2,1,0:T(8,128)(2,1)S(1)}, u32[]{:S(2)}, u32[]{:S(2)}) %collective-permute-start.18) | collective-permute-done | bytes 393248 | tf_op jit(solution)/shard_map/ppermute | solution.py:267
  295.7 8.3 %collective-permute-done.21 = bf16[1,768,256]{2,1,0:T(8,128)(2,1)S(1)} collective-permute-done((bf16[1,768,256]{2,1,0:T(8,128)(2,1)S(1)}, bf16[1,768,256]{2,1,0:T(8,128)(2,1)S(1)}, u32[]{:S(2)}, u32[]{:S(2)}) %collective-permute-start.21) | collective-permute-done | bytes 393248 | tf_op jit(solution)/shard_map/ppermute | solution.py:267
  304.1 1.1 pad_maximum_fusion
  (102 shorter events, 19.1 us)
Async XLA Ops:
  7.2 114.1 %all-gather.8.cloned.1.call-start = ((), (), s32[]{:S(2)}) async-start(), calls=%async_computation.2 | async-start | bytes 2621440 | tf_op jit(solution)/shard_map/all_gather | solution.py:313
  10.1 1.1 copy-start.27
  11.1 131.5 %all-gather.6.cloned.1.call-start = ((), (), s32[]{:S(2)}) async-start(), calls=%async_computation.1 | async-start | bytes 2621440 | tf_op jit(solution)/shard_map/all_gather | solution.py:313
  11.1 2.2 copy-start
  12.2 176.7 %all-gather.4.cloned.1.call-start = ((), (), s32[]{:S(2)}) async-start(), calls=%async_computation | async-start | bytes 2621440 | tf_op jit(solution)/shard_map/all_gather | solution.py:313
  13.3 13.3 %copy-start.28 = (s32[1,6,4]{1,2,0:T(4,128)S(1)}, s32[1,6,4]{1,2,0:T(4,128)}, u32[]{:S(2)}) copy-start(s32[1,6,4]{1,2,0:T(4,128)} %param.16) | copy-start | bytes 292
  13.3 94.5 %copy-start.23 = (s32[1,512]{1,0:T(1,128)S(1)}, s32[1,512]{1,0:T(1,128)}, u32[]{:S(2)}) copy-start(s32[1,512]{1,0:T(1,128)} %order_ref.1) | copy-start | bytes 6148
  13.3 62.9 %collective-permute-start.3 = (bf16[768,768]{1,0:T(8,128)(2,1)S(1)}, bf16[768,768]{1,0:T(8,128)(2,1)S(1)}, u32[]{:S(2)}, u32[]{:S(2)}) collective-permute-start(bf16[768,768]{1,0:T(8,128)(2,1)S(1)} %copy-done), channel_id=1, source_target_pairs={{0,16},{4,20},{8,24},{12,28},{16,0},{20,4},{24,8},{28,12},{1,17},{... | collective-permute-start | bytes 3538952 | tf_op jit(solution)/shard_map/ppermute | solution.py:267
  14.6 64.0 %collective-permute-start.4 = (bf16[768,768]{1,0:T(8,128)(2,1)S(1)}, bf16[768,768]{1,0:T(8,128)(2,1)S(1)}, u32[]{:S(2)}, u32[]{:S(2)}) collective-permute-start(bf16[768,768]{1,0:T(8,128)(2,1)S(1)} %copy-done), channel_id=1, source_target_pairs={{0,8},{4,12},{8,0},{12,4},{16,24},{20,28},{24,16},{28,20},{1,9},{5... | collective-permute-start | bytes 3538952 | tf_op jit(solution)/shard_map/ppermute | solution.py:267
  15.8 1.1 copy-start.12
  17.0 1.1 copy-start.13
  18.1 1.1 copy-start.14
  22.6 50.7 %collective-permute-start = (bf16[3,128,768]{2,1,0:T(8,128)(2,1)}, bf16[3,128,768]{2,1,0:T(8,128)(2,1)}, u32[]{:S(2)}, u32[]{:S(2)}) collective-permute-start(bf16[3,128,768]{2,1,0:T(8,128)(2,1)} %get-tuple-element.29), channel_id=1, source_target_pairs={{0,1},{1,0},{2,3},{3,2},{4,5},{5,4},{6,7},{7,6},{8,9},{9,8},{10,11... | collective-permute-start | bytes 1769480 | tf_op jit(solution)/shard_map/ppermute | solution.py:267
  22.7 128.2 %collective-permute-start.6 = (bf16[768,768]{1,0:T(8,128)(2,1)S(1)}, bf16[768,768]{1,0:T(8,128)(2,1)}, u32[]{:S(2)}, u32[]{:S(2)}) collective-permute-start(bf16[768,768]{1,0:T(8,128)(2,1)S(1)} %copy-done), channel_id=1, source_target_pairs={{0,4},{4,0},{8,12},{12,8},{16,20},{20,16},{24,28},{28,24},{1,5},{5... | collective-permute-start | bytes 3538952 | tf_op jit(solution)/shard_map/ppermute | solution.py:267
  24.3 56.9 %collective-permute-start.1 = (bf16[3,128,768]{2,1,0:T(8,128)(2,1)}, bf16[3,128,768]{2,1,0:T(8,128)(2,1)}, u32[]{:S(2)}, u32[]{:S(2)}) collective-permute-start(bf16[3,128,768]{2,1,0:T(8,128)(2,1)} %get-tuple-element.30), channel_id=1, source_target_pairs={{0,2},{1,3},{2,0},{3,1},{4,6},{5,7},{6,4},{7,5},{8,10},{9,11},{10,... | collective-permute-start | bytes 1769480 | tf_op jit(solution)/shard_map/ppermute | solution.py:267
  73.3 34.4 %collective-permute-start.2 = (bf16[3,128,768]{2,1,0:T(8,128)(2,1)}, bf16[3,128,768]{2,1,0:T(8,128)(2,1)}, u32[]{:S(2)}, u32[]{:S(2)}) collective-permute-start(bf16[3,128,768]{2,1,0:T(8,128)(2,1)} %copy-done.24), channel_id=1, source_target_pairs={{0,3},{1,2},{2,1},{3,0},{4,7},{5,6},{6,5},{7,4},{8,11},{9,10},{10,... | collective-permute-start | bytes 1769480 | tf_op jit(solution)/shard_map/ppermute | solution.py:267
  76.2 74.7 %collective-permute-start.5 = (bf16[768,768]{1,0:T(8,128)(2,1)S(1)}, bf16[768,768]{1,0:T(8,128)(2,1)}, u32[]{:S(2)}, u32[]{:S(2)}) collective-permute-start(bf16[768,768]{1,0:T(8,128)(2,1)S(1)} %collective-permute-done.3.refs_1_), channel_id=1, source_target_pairs={{0,8},{4,12},{8,0},{12,4},{16,24},{20,28},{24,16},{28,20},{1,9},{5... | collective-permute-start | bytes 3538952 | tf_op jit(solution)/shard_map/ppermute | solution.py:267
  78.6 115.4 %collective-permute-start.8 = (bf16[768,768]{1,0:T(8,128)(2,1)S(1)}, bf16[768,768]{1,0:T(8,128)(2,1)}, u32[]{:S(2)}, u32[]{:S(2)}) collective-permute-start(bf16[768,768]{1,0:T(8,128)(2,1)S(1)} %collective-permute-done.4.refs_2_), channel_id=1, source_target_pairs={{0,4},{4,0},{8,12},{12,8},{16,20},{20,16},{24,28},{28,24},{1,5},{5... | collective-permute-start | bytes 3538952 | tf_op jit(solution)/shard_map/ppermute | solution.py:267
  107.7 1.1 copy-start.22
  121.3 1.6 copy-start.1
  122.9 1.1 copy-start.5
  127.5 1.2 copy-start.10
  128.7 94.1 %collective-permute-start.13 = (bf16[4,768,256]{2,1,0:T(8,128)(2,1)}, bf16[4,768,256]{2,1,0:T(8,128)(2,1)}, u32[]{:S(2)}, u32[]{:S(2)}) collective-permute-start(bf16[4,768,256]{2,1,0:T(8,128)(2,1)} %get-tuple-element.46), channel_id=1, source_target_pairs={{0,4},{4,0},{8,12},{12,8},{16,20},{20,16},{24,28},{28,24},{1,5},{5... | collective-permute-start | bytes 4718600 | tf_op jit(solution)/shard_map/ppermute | solution.py:267
  142.6 1.6 copy-start.2
  144.2 1.1 copy-start.6
  148.9 1.1 copy-start.8
  150.0 75.2 %collective-permute-start.16 = (bf16[4,768,256]{2,1,0:T(8,128)(2,1)}, bf16[4,768,256]{2,1,0:T(8,128)(2,1)}, u32[]{:S(2)}, u32[]{:S(2)}) collective-permute-start(bf16[4,768,256]{2,1,0:T(8,128)(2,1)} %get-tuple-element.48), channel_id=1, source_target_pairs={{0,4},{4,0},{8,12},{12,8},{16,20},{20,16},{24,28},{28,24},{1,5},{5... | collective-permute-start | bytes 4718600 | tf_op jit(solution)/shard_map/ppermute | solution.py:267
  151.0 44.0 %collective-permute-start.7 = (bf16[768,768]{1,0:T(8,128)(2,1)S(1)}, bf16[768,768]{1,0:T(8,128)(2,1)}, u32[]{:S(2)}, u32[]{:S(2)}) collective-permute-start(bf16[768,768]{1,0:T(8,128)(2,1)S(1)} %collective-permute-done.3.refs_1_), channel_id=1, source_target_pairs={{0,4},{4,0},{8,12},{12,8},{16,20},{20,16},{24,28},{28,24},{1,5},{5... | collective-permute-start | bytes 3538952 | tf_op jit(solution)/shard_map/ppermute | solution.py:267
  151.0 44.0 %collective-permute-start.9 = (bf16[768,768]{1,0:T(8,128)(2,1)}, bf16[768,768]{1,0:T(8,128)(2,1)}, u32[]{:S(2)}, u32[]{:S(2)}) collective-permute-start(bf16[768,768]{1,0:T(8,128)(2,1)} %collective-permute-done.5.refs_3_), channel_id=1, source_target_pairs={{0,4},{4,0},{8,12},{12,8},{16,20},{20,16},{24,28},{28,24},{1,5},{5... | collective-permute-start | bytes 3538952 | tf_op jit(solution)/shard_map/ppermute | solution.py:267
  188.9 1.6 copy-start.3
  190.5 1.1 copy-start.7
  194.0 34.4 %collective-permute-start.19 = (bf16[4,768,256]{2,1,0:T(8,128)(2,1)S(1)}, bf16[4,768,256]{2,1,0:T(8,128)(2,1)}, u32[]{:S(2)}, u32[]{:S(2)}) collective-permute-start(bf16[4,768,256]{2,1,0:T(8,128)(2,1)S(1)} %get-tuple-element.50), channel_id=1, source_target_pairs={{0,4},{4,0},{8,12},{12,8},{16,20},{20,16},{24,28},{28,24},{1,5},{5... | collective-permute-start | bytes 4718600 | tf_op jit(solution)/shard_map/ppermute | solution.py:267
  207.2 5.2 %copy-start.15 = (bf16[512,768]{1,0:T(8,128)(2,1)S(1)}, bf16[512,768]{1,0:T(8,128)(2,1)}, u32[]{:S(2)}) copy-start(bf16[512,768]{1,0:T(8,128)(2,1)} %get-tuple-element.32.att_ref) | copy-start | bytes 2359300
  207.2 5.2 %copy-start.17 = (bf16[768,512]{1,0:T(8,128)(2,1)S(1)}, bf16[768,512]{1,0:T(8,128)(2,1)}, u32[]{:S(2)}) copy-start(bf16[768,512]{1,0:T(8,128)(2,1)} %copy-done.16) | copy-start | bytes 2359300
  207.2 5.2 %copy-start.19 = (bf16[512,768]{1,0:T(8,128)(2,1)S(1)}, bf16[512,768]{1,0:T(8,128)(2,1)}, u32[]{:S(2)}) copy-start(bf16[512,768]{1,0:T(8,128)(2,1)} %copy-done.18) | copy-start | bytes 2359300
  212.4 10.9 %copy-start.11 = (bf16[4,768,256]{2,1,0:T(8,128)(2,1)S(1)}, bf16[4,768,256]{2,1,0:T(8,128)(2,1)}, u32[]{:S(2)}) copy-start(bf16[4,768,256]{2,1,0:T(8,128)(2,1)} %copy-done.10) | copy-start | bytes 4718596
  220.1 26.9 %collective-permute-start.10 = (bf16[3,128,768]{2,1,0:T(8,128)(2,1)S(1)}, bf16[3,128,768]{2,1,0:T(8,128)(2,1)S(1)}, u32[]{:S(2)}, u32[]{:S(2)}) collective-permute-start(bf16[3,128,768]{2,1,0:T(8,128)(2,1)S(1)} %get-tuple-element.38), channel_id=1, source_target_pairs={{0,1},{1,0},{2,3},{3,2},{4,5},{5,4},{6,7},{7,6},{8,9},{9,8},{10,11... | collective-permute-start | bytes 1769480 | tf_op jit(solution)/shard_map/ppermute | solution.py:267
  222.1 27.0 %collective-permute-start.11 = (bf16[3,128,768]{2,1,0:T(8,128)(2,1)S(1)}, bf16[3,128,768]{2,1,0:T(8,128)(2,1)S(1)}, u32[]{:S(2)}, u32[]{:S(2)}) collective-permute-start(bf16[3,128,768]{2,1,0:T(8,128)(2,1)S(1)} %get-tuple-element.39), channel_id=1, source_target_pairs={{0,2},{1,3},{2,0},{3,1},{4,6},{5,7},{6,4},{7,5},{8,10},{9,11},{10,... | collective-permute-start | bytes 1769480 | tf_op jit(solution)/shard_map/ppermute | solution.py:267
  222.8 52.0 %collective-permute-start.12 = (bf16[3,128,768]{2,1,0:T(8,128)(2,1)S(1)}, bf16[3,128,768]{2,1,0:T(8,128)(2,1)S(1)}, u32[]{:S(2)}, u32[]{:S(2)}) collective-permute-start(bf16[3,128,768]{2,1,0:T(8,128)(2,1)S(1)} %get-tuple-element.40), channel_id=1, source_target_pairs={{0,3},{1,2},{2,1},{3,0},{4,7},{5,6},{6,5},{7,4},{8,11},{9,10},{10,... | collective-permute-start | bytes 1769480 | tf_op jit(solution)/shard_map/ppermute | solution.py:267
  225.1 1.4 copy-start.9
  225.2 51.7 %collective-permute-start.14 = (bf16[2,768,256]{2,1,0:T(8,128)(2,1)S(1)}, bf16[2,768,256]{2,1,0:T(8,128)(2,1)S(1)}, u32[]{:S(2)}, u32[]{:S(2)}) collective-permute-start(bf16[2,768,256]{2,1,0:T(8,128)(2,1)S(1)} %slice.107), channel_id=1, source_target_pairs={{0,8},{4,12},{8,0},{12,4},{16,24},{20,28},{24,16},{28,20},{1,9},{5... | collective-permute-start | bytes 2359304 | tf_op jit(solution)/shard_map/ppermute | solution.py:267
  228.3 50.0 %collective-permute-start.17 = (bf16[2,768,256]{2,1,0:T(8,128)(2,1)S(1)}, bf16[2,768,256]{2,1,0:T(8,128)(2,1)S(1)}, u32[]{:S(2)}, u32[]{:S(2)}) collective-permute-start(bf16[2,768,256]{2,1,0:T(8,128)(2,1)S(1)} %slice.106), channel_id=1, source_target_pairs={{0,8},{4,12},{8,0},{12,4},{16,24},{20,28},{24,16},{28,20},{1,9},{5... | collective-permute-start | bytes 2359304 | tf_op jit(solution)/shard_map/ppermute | solution.py:267
  231.3 43.5 %copy-start.25 = (f32[4,768,256]{2,1,0:T(8,128)}, f32[4,768,256]{2,1,0:T(8,128)S(1)}, u32[]{:S(2)}) copy-start(f32[4,768,256]{2,1,0:T(8,128)S(1)} %convert_add_fusion) | copy-start | bytes 9437188
  247.1 31.9 %collective-permute-start.20 = (bf16[2,768,256]{2,1,0:T(8,128)(2,1)S(1)}, bf16[2,768,256]{2,1,0:T(8,128)(2,1)S(1)}, u32[]{:S(2)}, u32[]{:S(2)}) collective-permute-start(bf16[2,768,256]{2,1,0:T(8,128)(2,1)S(1)} %slice.105), channel_id=1, source_target_pairs={{0,8},{4,12},{8,0},{12,4},{16,24},{20,28},{24,16},{28,20},{1,9},{5... | collective-permute-start | bytes 2359304 | tf_op jit(solution)/shard_map/ppermute | solution.py:267
  277.2 1.9 copy-start.26
  277.2 10.0 %collective-permute-start.15 = (bf16[1,768,256]{2,1,0:T(8,128)(2,1)S(1)}, bf16[1,768,256]{2,1,0:T(8,128)(2,1)S(1)}, u32[]{:S(2)}, u32[]{:S(2)}) collective-permute-start(bf16[1,768,256]{2,1,0:T(8,128)(2,1)S(1)} %slice.110), channel_id=1, source_target_pairs={{0,16},{4,20},{8,24},{12,28},{16,0},{20,4},{24,8},{28,12},{1,17},{... | collective-permute-start | bytes 1179656 | tf_op jit(solution)/shard_map/ppermute | solution.py:267
  278.6 17.0 %collective-permute-start.18 = (bf16[1,768,256]{2,1,0:T(8,128)(2,1)S(1)}, bf16[1,768,256]{2,1,0:T(8,128)(2,1)S(1)}, u32[]{:S(2)}, u32[]{:S(2)}) collective-permute-start(bf16[1,768,256]{2,1,0:T(8,128)(2,1)S(1)} %slice.109), channel_id=1, source_target_pairs={{0,16},{4,20},{8,24},{12,28},{16,0},{20,4},{24,8},{28,12},{1,17},{... | collective-permute-start | bytes 1179656 | tf_op jit(solution)/shard_map/ppermute | solution.py:267
  279.3 24.7 %collective-permute-start.21 = (bf16[1,768,256]{2,1,0:T(8,128)(2,1)S(1)}, bf16[1,768,256]{2,1,0:T(8,128)(2,1)S(1)}, u32[]{:S(2)}, u32[]{:S(2)}) collective-permute-start(bf16[1,768,256]{2,1,0:T(8,128)(2,1)S(1)} %slice.108), channel_id=1, source_target_pairs={{0,16},{4,20},{8,24},{12,28},{16,0},{20,4},{24,8},{28,12},{1,17},{... | collective-permute-start | bytes 1179656 | tf_op jit(solution)/shard_map/ppermute | solution.py:267
  (6 other events, 5.1 us)
Sparse Core Ops, SparseCore 0:
  11.2 71.3 all-gather.7
  84.2 58.3 all-gather.5
  144.2 44.6 all-gather.3
where the time goes:
time: 314 us; the launch traced here: 312 us
  waiting for transfers between devices  190 us (61%)
  Pallas kernels  47.2 us (15%)
  local copies, waits for them, and re-layouts  28.1 us (9%)
  starting transfers between devices  24 us (8%)
  between operations  14.1 us (4%)
  other arithmetic  8.7 us (3%)
    ppermute x22, waiting for transfers between devices, swap(): return lax.ppermute(value, axis, [(i, i ^ mask) for i in range(size)])  139 us
    all_gather x3, waiting for transfers between devices, local(): lax.all_gather(pieces[:, :, j].reshape(tokens_here, dp * part), 'head', a...  50.9 us
    ppermute x22, starting transfers between devices, swap(): return lax.ppermute(value, axis, [(i, i ^ mask) for i in range(size)])  23.9 us
    unnamed x59, local copies, waits for them, and re-layouts  22.2 us
    pallas_call x3, Pallas kernels, project(): pl.pallas_call(functools.partial(project_kernel, count), out_shape=jax.Sh...  17.4 us
    pallas_call x3, Pallas kernels, outer(): pl.pallas_call(outer_kernel, out_shape=[shape] * 2, grid_spec=pltpu.Prefe...  9.35 us
    pallas_call x1, Pallas kernels, forward(): pl.pallas_call(functools.partial(forward_kernel, group), out_shape=[jax.S...  8.97 us
    pallas_call x1, Pallas kernels, backward(): pl.pallas_call(functools.partial(backward_kernel, group), out_shape=[jax....  7.68 us
  transfers between devices with their start and end apart: 25, of which 10 were waited for; matrix products, arithmetic and copies ran while one was open for 4% of the time, Pallas kernels for 15%

commit v1 on v0

v1 whole, which is shorter than its diff:
```python
import functools
import math

import jax
import jax.numpy as jnp
from jax import lax
from jax.experimental import pallas as pl
from jax.experimental.pallas import tpu as pltpu
from jax.sharding import PartitionSpec as P

HEAD_DIM = 128
CUBE_TOKENS = 128
LANES = 128

masked_score = -1e30
scale = 1.0 / math.sqrt(HEAD_DIM)
log2_e = math.log2(math.e)

BF16 = jnp.bfloat16
F32 = jnp.float32
NT = (((1,), (1,)), ((), ()))
NN = (((1,), (0,)), ((), ()))


def chunk_widths(columns):
    return [columns // 3] * 3


def light():
    return pl.CostEstimate(flops=1, bytes_accessed=1, transcendentals=0)


def whole(shape):
    return pl.BlockSpec(shape, lambda *_: (0,) * len(shape))


def awaited(after):
    return [pl.BlockSpec(memory_space=pl.ANY)] * len(after)


def dot(a, b, dims=NN):
    return lax.dot_general(a, b, dims, preferred_element_type=F32)


def params(limit_mib=60):
    return pltpu.CompilerParams(vmem_limit_bytes=limit_mib * 1024 * 1024)


def tables(group, here):
    partner = jnp.bitwise_xor(here, jnp.arange(group, dtype=jnp.int32))
    if group != 4:
        return jnp.concatenate([partner, partner, jnp.arange(group, dtype=jnp.int32)])
    middle = jnp.logical_or(here == 1, here == 2)
    slots = jnp.where(middle, jnp.array([0, 1, 3, 2], jnp.int32), jnp.arange(4, dtype=jnp.int32))
    return jnp.concatenate([partner, slots, jnp.bitwise_xor(here, slots)])


def slot(table, s):
    return table[table.shape[0] // 3 + s]


def owner(table, t):
    return table[table.shape[0] // 3 * 2 + t]


def pack_kernel(group, table, *refs):
    ins, outs = refs[: 3 * group], refs[-group:]
    for s, out in enumerate(outs):
        for i in range(3):
            out[i] = ins[3 * s + i][0]


def pack(table, q, k, v, after=()):
    group = table.shape[0] // 3
    rows, total = q.shape[1:]
    shape = (3, rows, total // group)
    in_specs = []
    for s in range(group):
        in_specs += [
            pl.BlockSpec((1, rows, total // group), lambda i, t, s=s: (0, 0, t[s]))
        ] * 3
    return pl.pallas_call(
        functools.partial(pack_kernel, group),
        out_shape=[jax.ShapeDtypeStruct(shape, BF16)] * group,
        grid_spec=pltpu.PrefetchScalarGridSpec(
            num_scalar_prefetch=1,
            grid=(1,),
            in_specs=in_specs + awaited(after),
            out_specs=[whole(shape)] * group,
        ),
        cost_estimate=light(),
        compiler_params=params(),
    )(table, *[q, k, v] * group, *after)


def split_kernel(dp, g_ref, *outs):
    columns = g_ref.shape[2] // dp
    before = 0
    for out in outs:
        part = out.shape[1] // dp
        for d in range(dp):
            start = d * columns + before
            out[:, d * part : (d + 1) * part] = g_ref[0, :, start : start + part]
        before += part


def split(g, dp):
    shapes = [(g.shape[1], width * dp) for width in chunk_widths(g.shape[2] // dp)]
    return pl.pallas_call(
        functools.partial(split_kernel, dp),
        out_shape=[jax.ShapeDtypeStruct(shape, BF16) for shape in shapes],
        grid=(1,),
        in_specs=[whole(g.shape)],
        out_specs=[whole(shape) for shape in shapes],
        cost_estimate=light(),
        compiler_params=params(),
    )(g)


def join_kernel(a_ref, b_ref, *refs):
    out = refs[-1]
    out[: a_ref.shape[0]] = a_ref[...]
    out[a_ref.shape[0] :] = b_ref[...]


def join(a, b, after=()):
    shape = (a.shape[0] + b.shape[0],) + a.shape[1:]
    return pl.pallas_call(
        join_kernel,
        out_shape=jax.ShapeDtypeStruct(shape, a.dtype),
        grid=(1,),
        in_specs=[whole(a.shape), whole(b.shape)] + awaited(after),
        out_specs=whole(shape),
        cost_estimate=light(),
        compiler_params=params(),
    )(a, b, *after)


def hold_kernel(*refs):
    pass


def hold(value, after):
    return pl.pallas_call(
        hold_kernel,
        out_shape=jax.ShapeDtypeStruct(value.shape, value.dtype),
        in_specs=awaited([value, *after]),
        out_specs=pl.BlockSpec(memory_space=pl.ANY),
        input_output_aliases={0: 0},
        cost_estimate=light(),
        compiler_params=params(),
    )(value, *after)


def unpack_kernel(group, place, *refs):
    parts, outs = refs[:group], refs[-3:]
    width = parts[0].shape[2]
    for s, part in enumerate(parts):
        columns = pl.ds(pl.multiple_of(place[s] * width, LANES), width)
        for i, out in enumerate(outs):
            out[0, :, columns] = part[i]


def unpack(place, parts, after=()):
    group = place.shape[0] // 3
    _, rows, width = parts[0].shape
    shape = jax.ShapeDtypeStruct((1, rows, width * group), BF16)
    return pl.pallas_call(
        functools.partial(unpack_kernel, group),
        out_shape=[shape] * 3,
        grid_spec=pltpu.PrefetchScalarGridSpec(
            num_scalar_prefetch=1,
            grid=(1,),
            in_specs=[whole(part.shape) for part in parts] + awaited(after),
            out_specs=[whole(shape.shape)] * 3,
        ),
        cost_estimate=light(),
        compiler_params=params(),
    )(place, *parts, *after)


def forward_kernel(group, table, order_ref, bias_ref, *refs):
    parts = refs[:group]
    att_ref, att_t_ref, weight_ref, q_t_ref, k_ref, v_ref, cube_ref, q_ref = refs[-8:]
    rows = parts[0].shape[1]
    total = q_ref.shape[0]

    @pl.when(pl.program_id(0) == 0)
    def _():
        position = lax.broadcasted_iota(jnp.int32, (total, LANES), 0)
        cube = lax.broadcasted_iota(jnp.int32, (total, LANES), 1)
        block = jnp.where(lax.div(position, CUBE_TOKENS) == cube, 1.0, 0.0).astype(BF16)
        for t in range(group):
            token = lax.broadcasted_iota(jnp.int32, (rows, total), 0) + owner(table, t) * rows
            onehot = jnp.where(token == order_ref[...], 1.0, 0.0).astype(BF16)
            cube_ref[t * rows : (t + 1) * rows, :] = dot(onehot, block).astype(BF16)

    for s, part in enumerate(parts):
        here = pl.ds(pl.multiple_of(slot(table, s) * rows, rows), rows)
        q_ref[here, :] = part[0]
        k_ref[here, :] = part[1]
        v_ref[here, :] = part[2]
    cubes = cube_ref[...]
    q, k, v = q_ref[...], k_ref[...], v_ref[...]
    bias = dot(cubes, bias_ref[0]).astype(BF16)
    scores = dot(
        jnp.concatenate([q, bias], axis=1), jnp.concatenate([k, cubes], axis=1), NT
    ) * (scale * log2_e)
    raised = jnp.exp2(scores - jnp.max(scores, axis=1, keepdims=True))
    weights = (raised * (1.0 / jnp.sum(raised, axis=1, keepdims=True))).astype(BF16)
    weight_ref[0] = weights
    output = dot(weights, v)
    for t in range(group):
        here = pl.ds(pl.multiple_of(owner(table, t) * rows, rows), rows)
        att_ref[here, :] = output[t * rows : (t + 1) * rows].astype(BF16)
    att_t_ref[...] = output.T.astype(BF16)
    q_t_ref[...] = q.astype(F32).T.astype(BF16)


def forward(table, order, bias, parts, after=()):
    group = len(parts)
    _, rows, width = parts[0].shape
    total = rows * group
    heads = width // HEAD_DIM
    column = pl.BlockSpec((total, HEAD_DIM), lambda h, *_: (0, h))
    row = pl.BlockSpec((HEAD_DIM, total), lambda h, *_: (h, 0))
    return pl.pallas_call(
        functools.partial(forward_kernel, group),
        out_shape=[
            jax.ShapeDtypeStruct((total, width), BF16),
            jax.ShapeDtypeStruct((width, total), BF16),
            jax.ShapeDtypeStruct((heads, total, total), BF16),
            jax.ShapeDtypeStruct((width, total), BF16),
            jax.ShapeDtypeStruct((total, width), BF16),
            jax.ShapeDtypeStruct((total, width), BF16),
        ],
        grid_spec=pltpu.PrefetchScalarGridSpec(
            num_scalar_prefetch=1,
            grid=(heads,),
            in_specs=[
                pl.BlockSpec((1, total), lambda h, *_: (0, 0)),
                pl.BlockSpec((1, LANES, LANES), lambda h, *_: (h, 0, 0)),
            ]
            + [pl.BlockSpec((3, rows, HEAD_DIM), lambda h, *_: (0, 0, h))] * group
            + awaited(after),
            out_specs=[
                column,
                row,
                pl.BlockSpec((1, total, total), lambda h, *_: (h, 0, 0)),
                row,
                column,
                column,
            ],
            scratch_shapes=[
                pltpu.VMEM((total, LANES), BF16),
                pltpu.VMEM((total, HEAD_DIM), BF16),
            ],
        ),
        cost_estimate=light(),
        compiler_params=params(),
    )(table, order, bias, *parts, *after)


def backward_kernel(
    group, passed, table, g_ref, att_ref, weight_ref, q_t_ref, k_ref, v_ref, *refs
):
    outs, held = refs[passed : passed + group], refs[-1]
    rows = outs[0].shape[1]
    grad = g_ref[...]
    weights = weight_ref[0]
    grad_float = grad.astype(F32)
    att = jnp.concatenate(
        [
            att_ref[pl.ds(pl.multiple_of(owner(table, t) * rows, rows), rows), :]
            for t in range(group)
        ],
        axis=0,
    )
    delta = jnp.sum(grad_float * att.astype(F32), axis=1, keepdims=True)
    diff = (weights.astype(F32) * (dot(grad, v_ref[...], NT) - delta)).astype(BF16)
    held[0] = (dot(diff, k_ref[...]) * scale).astype(BF16)
    held[1] = (dot(q_t_ref[...], diff) * scale).T.astype(BF16)
    held[2] = dot(grad_float.T.astype(BF16), weights).T.astype(BF16)
    for s, out in enumerate(outs):
        here = pl.ds(pl.multiple_of(slot(table, s) * rows, rows), rows)
        out[...] = held[:, here, :]


def backward(table, grad, att, weights, q_t, k, v, passed):
    group = table.shape[0] // 3
    total, width = grad.shape
    rows = total // group
    heads = width // HEAD_DIM
    column = pl.BlockSpec((total, HEAD_DIM), lambda h, *_: (0, h))
    row = pl.BlockSpec((HEAD_DIM, total), lambda h, *_: (h, 0))
    return pl.pallas_call(
        functools.partial(backward_kernel, group, len(passed)),
        out_shape=[jax.ShapeDtypeStruct((3, rows, width), BF16)] * group
        + [jax.ShapeDtypeStruct(x.shape, x.dtype) for x in passed],
        grid_spec=pltpu.PrefetchScalarGridSpec(
            num_scalar_prefetch=1,
            grid=(heads,),
            in_specs=[
                column,
                column,
                pl.BlockSpec((1, total, total), lambda h, *_: (h, 0, 0)),
                row,
                column,
                column,
            ]
            + awaited(passed),
            out_specs=[pl.BlockSpec((3, rows, HEAD_DIM), lambda h, *_: (0, 0, h))] * group
            + awaited(passed),
            scratch_shapes=[pltpu.VMEM((3, total, HEAD_DIM), BF16)],
        ),
        input_output_aliases={7 + i: group + i for i in range(len(passed))},
        cost_estimate=light(),
        compiler_params=params(),
    )(table, grad, att, weights, q_t, k, v, *passed)


def block_rows(refs, columns):
    if len(refs) == 1:
        return refs[0][:, columns]
    own, near, inner, outer = refs
    return jnp.concatenate(
        [own[:, columns], near[:, columns], inner[:, columns] + outer[:, columns]], axis=0
    )


def block_columns(blocks, p, width):
    return pl.ds(pl.multiple_of(blocks[p] * width, LANES), width)


def project_kernel(count, pieces, first, *refs):
    weights, refs = refs[:pieces], refs[pieces:]
    rows, out = refs[:count], refs[-1]
    dp, _, unit = weights[0].shape
    part = unit * pieces
    total = None if first else refs[count][...]
    for p in range(dp):
        weight = jnp.concatenate([w[p] for w in weights], axis=1)
        term = dot(block_rows(rows, slice(p * part, (p + 1) * part)), weight, NT)
        total = term if total is None else total + term
    out[...] = total.astype(out.dtype)


def project(rows, weights, start, before, dtype, after=()):
    dp, heads, _ = weights.shape
    part = rows[0].shape[1] // dp
    unit = math.gcd(start, part)
    tokens = sum(r.shape[0] for r in rows[:3])
    before = [] if before is None else [before]
    at = range(start // unit, (start + part) // unit)
    return pl.pallas_call(
        functools.partial(project_kernel, len(rows), len(at), not before),
        out_shape=jax.ShapeDtypeStruct((tokens, heads), dtype),
        grid=(1,),
        in_specs=[pl.BlockSpec((dp, heads, unit), lambda i, c=c: (0, 0, c)) for c in at]
        + [whole(r.shape) for r in rows]
        + [whole(x.shape) for x in before]
        + awaited(after),
        out_specs=whole((tokens, heads)),
        cost_estimate=light(),
        compiler_params=params(),
    )(*[weights] * len(at), *rows, *before, *after)


def outer_kernel(count, blocks, att_t_ref, *refs):
    rows, (keep_ref, send_ref) = refs[:count], refs[-2:]
    half, _, part = keep_ref.shape
    att_t = att_t_ref[...]
    for p in range(2 * half):
        out = keep_ref if p < half else send_ref
        here = block_rows(rows, block_columns(blocks, p, part))
        out[p % half] = dot(att_t, here).astype(BF16)


def outer(blocks, att_t, rows, start, width, buffers=()):
    half = blocks.shape[0] // 2
    heads = att_t.shape[0]
    part = rows[0].shape[1] // (2 * half)
    first = 2 + len(rows)
    return pl.pallas_call(
        functools.partial(outer_kernel, len(rows)),
        out_shape=[jax.ShapeDtypeStruct((half, heads, width), BF16)] * 2,
        grid_spec=pltpu.PrefetchScalarGridSpec(
            num_scalar_prefetch=1,
            grid=(1,),
            in_specs=[whole(att_t.shape)] + [whole(r.shape) for r in rows] + awaited(buffers),
            out_specs=[pl.BlockSpec((half, heads, part), lambda i, b: (0, 0, start // part))] * 2,
        ),
        input_output_aliases={first + i: i for i in range(len(buffers))},
        cost_estimate=light(),
        compiler_params=params(),
    )(blocks, att_t, *rows, *buffers)


def swap(value, axis, size, mask):
    return lax.ppermute(value, axis, [(i, i ^ mask) for i in range(size)])


def half_order(masks):
    order = [0]
    for mask in reversed(masks):
        order = order + [mask ^ r for r in order]
    return order


def fold(state, dp):
    kept, send, masks = state
    if not masks:
        return state
    kept = kept.astype(F32) + swap(send, "dp", dp, masks[0]).astype(F32)
    half = kept.shape[0] // 2
    if half == 0:
        kept = kept[0].astype(BF16)
        return kept, kept, masks[1:]
    return kept[:half], kept[half:].astype(BF16), masks[1:]


def gather_rows(own, near, group, both=None, held=()):
    if group != 4:
        return [lax.all_gather(own, "head", axis=0, tiled=True)]
    inner = lax.ppermute(join(own, near) if both is None else both, "head", [(1, 2), (2, 1)])
    if held:
        inner = hold(inner, held)
    outer = lax.ppermute(inner, "head", [(1, 0), (2, 3)])
    return [own, near, inner, outer]


def local(
    dp,
    group,
    query_rows,
    key_rows,
    value_rows,
    out_grad,
    out_weight,
    token_order,
    tile_index,
    tile_count,
):
    table = tables(group, lax.axis_index("head"))
    up = [1 << i for i in range(dp.bit_length() - 1)]
    masks = [up, up[:1] + up[:0:-1]]
    widths = chunk_widths(out_weight.shape[1])

    def blocks(order):
        return jnp.bitwise_xor(lax.axis_index("dp"), jnp.array(half_order(order), jnp.int32))

    packed = pack(table, query_rows, key_rows, value_rows)
    parts = [packed[0]] + [swap(packed[s], "head", group, s) for s in range(1, group)]
    pieces = split(out_grad, dp)
    nears = [swap(own, "head", group, 1) for own in pieces] if group == 4 else pieces
    both = join(pieces[0], nears[0], after=parts[1:])
    weights_full = lax.all_gather(out_weight, "dp", axis=0)

    tiles, counts = tile_index[0], tile_count[0]
    heads, cubes, slots = tiles.shape
    used = jnp.arange(slots, dtype=jnp.int32) < counts[:, :, None]
    listed = tiles[..., None] == jnp.arange(LANES, dtype=jnp.int32)
    allowed = jnp.any(listed & used[..., None], axis=2)
    bias = jnp.where(allowed, 0.0, masked_score).astype(BF16)
    bias = jnp.pad(bias, ((0, 0), (0, LANES - cubes), (0, 0)))

    att, att_t, weights, q_t, k, v = forward(table, token_order, bias, parts, after=[both])
    sums_to = widths[0] + widths[1]
    first = gather_rows(pieces[0], nears[0], group, both)
    grad = project(first, weights_full, 0, None, F32)
    state = outer(blocks(masks[0]), att_t, first, 0, sums_to)
    second = gather_rows(pieces[1], nears[1], group, join(pieces[1], nears[1], after=[att_t]))
    third = gather_rows(pieces[2], nears[2], group, None, held=[grad, state[0]])
    grad = project(second, weights_full, widths[0], grad, F32)
    state = outer(blocks(masks[0]), att_t, second, widths[0], sums_to, state)
    other = outer(blocks(masks[1]), att_t, third, 0, widths[2])
    grad = project(
        third, weights_full, widths[0] + widths[1], grad, BF16, after=[state[0], other[0]]
    )
    *back, keep, send, other_keep, other_send = backward(
        table, grad, att, weights, q_t, k, v, [*state, *other]
    )
    states = [(keep, send, masks[0]), (other_keep, other_send, masks[1])]
    while any(masks for _, _, masks in states):
        states = [fold(state, dp) for state in states]
    back = [back[0]] + [swap(back[s], "head", group, s) for s in range(1, group)]
    query_back, key_back, value_back = unpack(table, back)
    sums = [kept for kept, _, _ in states]
    return (att[None], query_back, key_back, value_back, jnp.concatenate(sums, axis=1))


def solution(mesh):
    placed = (
        P("dp", "head", None),
        P("dp", "head", None),
        P("dp", "head", None),
        P("dp", "head", None),
        P("head", "dp"),
        P("dp", None),
        P("dp", "head", None, None),
        P("dp", "head", None),
    )
    return jax.shard_map(
        functools.partial(local, mesh.shape["dp"], mesh.shape["head"]),
        mesh=mesh,
        in_specs=placed,
        out_specs=(
            P("dp", None, "head"),
            P("dp", "head", None),
            P("dp", "head", None),
            P("dp", "head", None),
            P("head", "dp"),
        ),
        check_vma=False,
    )
```

time: 314 us -> 275 us (0.88)
  waiting for transfers between devices: 190 us -> 136 us
  Pallas kernels: 47.2 us -> 71 us
  local copies, waits for them, and re-layouts: 28.1 us -> 8.67 us
  starting transfers between devices: 24 us -> 32.2 us
    all_gather x3 -> x1, waiting for transfers between devices: 50.9 us -> 0.01 us  [local(): weights_full = lax.all_gather(out_weight, 'dp', axis=0)]
    ppermute x22 -> x15, waiting for transfers between devices: 139 us -> 108 us  [swap(): return lax.ppermute(value, axis, [(i, i ^ mask) for i in range(size)])]
    ppermute x0 -> x6, waiting for transfers between devices: none -> 27.5 us  [the longest x3 21.2 us: gather_rows(): lax.ppermute(join(own, near) if both is None else both, 'head', [(1, 2),...]
    pallas_call x8 -> x13, Pallas kernels: 36.2 us -> 57.7 us  [the longest x3 18.4 us: project(): pl.pallas_call(functools.partial(project_kernel, len(rows), len(at), not...]
    unnamed x59 -> x40, local copies, waits for them, and re-layouts: 22.2 us -> 6.58 us
    ppermute x0 -> x6, starting transfers between devices: none -> 13.7 us  [the longest x3 7.96 us: gather_rows(): lax.ppermute(join(own, near) if both is None else both, 'head', [(1, 2),...]
    ppermute x22 -> x15, starting transfers between devices: 23.9 us -> 18.4 us  [swap(): return lax.ppermute(value, axis, [(i, i ^ mask) for i in range(size)])]
  transfers between devices with their start and end apart: 25 -> 22, of which waited for: 10 -> 9; matrix products, arithmetic and copies ran while one was open for 4% -> 4% of each run, Pallas kernels for 15% -> 18%
where the time goes in v1:
time: 275 us; the launch traced here: 273 us
  waiting for transfers between devices  136 us (49%)
  Pallas kernels  71 us (26%)
  starting transfers between devices  32.2 us (12%)
  between operations  14.3 us (5%)
  other arithmetic  10.2 us (4%)
  local copies, waits for them, and re-layouts  8.67 us (3%)
    ppermute x15, waiting for transfers between devices, swap(): return lax.ppermute(value, axis, [(i, i ^ mask) for i in range(size)])  108 us
    ppermute x3, waiting for transfers between devices, gather_rows(): lax.ppermute(join(own, near) if both is None else both, 'head', [(1, 2),...  21.2 us
    ppermute x15, starting transfers between devices, swap(): return lax.ppermute(value, axis, [(i, i ^ mask) for i in range(size)])  18.4 us
    pallas_call x3, Pallas kernels, project(): pl.pallas_call(functools.partial(project_kernel, len(rows), len(at), not...  18.4 us
    pallas_call x3, Pallas kernels, outer(): pl.pallas_call(functools.partial(outer_kernel, len(rows)), out_shape=[jax...  17.4 us
    pallas_call x1, Pallas kernels, forward(): pl.pallas_call(functools.partial(forward_kernel, group), out_shape=[jax.S...  9.48 us
    pallas_call x1, Pallas kernels, backward(): pl.pallas_call(functools.partial(backward_kernel, group, len(passed)), ou...  8.81 us
    ppermute x3, starting transfers between devices, gather_rows(): lax.ppermute(join(own, near) if both is None else both, 'head', [(1, 2),...  7.96 us
  transfers between devices with their start and end apart: 22, of which 9 were waited for; matrix products, arithmetic and copies ran while one was open for 4% of the time, Pallas kernels for 18%

profile of v1, /device:TPU:9, one launch (start us, length us, event | category | flops | bytes accessed | tf_op | source)
XLA Modules:
  0.0 272.9 jit_solution(14026135643679572017)
XLA Ops:
  9.2 3.8 %shard_map.155 = (bf16[3,128,768]{2,1,0:T(8,128)(2,1)}, bf16[3,128,768]{2,1,0:T(8,128)(2,1)}, bf16[3,128,768]{2,1,0:T(8,128)(2,1)}, bf16[3,128,768]{2,1,0:T(8,128)(2,1)}) custom-call(s32[12]{0:T(128)} %pad_add_fusion.table.place, bf16[1,128,3072]{2,1,0:T(8,128)(2,1)} %refs_9_.1, bf16[1,128,3072]{2,1,0:T(8,128)(2,1)} %refs_10_.1, ...), custom_call_target="tpu_custom_call" | custom-call | flops 1 | bytes 1 | tf_op jit(solution)/shard_map/pallas_call | solution.py:82
  13.1 2.5 collective-permute-start.1
  15.7 2.6 shard_map.156
  18.4 1.0 collective-permute-start.3
  19.4 44.8 %collective-permute-done.3.b_ref.refs_2_.refs_1_ = bf16[128,2048]{1,0:T(8,128)(2,1)S(1)} collective-permute-done((bf16[128,2048]{1,0:T(8,128)(2,1)}, bf16[128,2048]{1,0:T(8,128)(2,1)S(1)}, u32[]{:S(2)}, u32[]{:S(2)}) %collective-permute-start.3) | collective-permute-done | bytes 524320 | tf_op jit(solution)/shard_map/ppermute | solution.py:400
  64.2 2.3 collective-permute-done.2.refs_2_.refs_3_
  66.5 0.8 copy-done.12
  67.3 2.2 shard_map.157.refs_4_
  69.6 3.2 %collective-permute-start.6 = (bf16[256,2048]{1,0:T(8,128)(2,1)}, bf16[256,2048]{1,0:T(8,128)(2,1)}, u32[]{:S(2)}, u32[]{:S(2)}) collective-permute-start(bf16[256,2048]{1,0:T(8,128)(2,1)} %shard_map.157.refs_4_), channel_id=1, source_target_pairs={{1,2},{2,1},{5,6},{6,5},{9,10},{10,9},{13,14},{14,13},{17,18},{18,... | collective-permute-start | bytes 3145736 | tf_op jit(solution)/shard_map/ppermute | solution.py:425
  72.9 1.4 collective-permute-start.9
  75.5 9.5 %shard_map.158 = (bf16[512,768]{1,0:T(8,128)(2,1)}, bf16[768,512]{1,0:T(8,128)(2,1)}, bf16[6,512,512]{2,1,0:T(8,128)(2,1)}, bf16[768,512]{1,0:T(8,128)(2,1)}, bf...) custom-call(s32[12]{0:T(128)} %pad_add_fusion.table.place, s32[1,512]{1,0:T(1,128)} %order_ref.1, ...), custom_call_target="tpu_custom_call" | custom-call | flops 1 | bytes 1 | tf_op jit(solution)/shard_map/pallas_call | solution.py:227
  84.9 10.7 %collective-permute-done.9.b_ref.refs_2_.refs_1_ = bf16[128,2048]{1,0:T(8,128)(2,1)S(1)} collective-permute-done((bf16[128,2048]{1,0:T(8,128)(2,1)S(1)}, bf16[128,2048]{1,0:T(8,128)(2,1)S(1)}, u32[]{:S(2)}, u32[]{:S(2)}) %collective-permute-start.9) | collective-permute-done | bytes 524320 | tf_op jit(solution)/shard_map/ppermute | solution.py:400
  96.4 2.3 shard_map.163
  98.6 2.0 collective-permute-start.10
  100.7 1.9 collective-permute-start.7
  102.5 0.8 copy-done.6
  103.4 2.2 shard_map.159
  105.6 2.8 %collective-permute-start.5 = (bf16[256,2048]{1,0:T(8,128)(2,1)}, bf16[256,2048]{1,0:T(8,128)(2,1)S(1)}, u32[]{:S(2)}, u32[]{:S(2)}) collective-permute-start(bf16[256,2048]{1,0:T(8,128)(2,1)} %shard_map.159), channel_id=1, source_target_pairs={{1,2},{2,1},{5,6},{6,5},{9,10},{10,9},{13,14},{14,13},{17,18},{18,... | collective-permute-start | bytes 3145736 | tf_op jit(solution)/shard_map/ppermute | solution.py:425
  108.9 13.8 %collective-permute-done.10.refs_3_.refs_2_ = bf16[256,2048]{1,0:T(8,128)(2,1)} collective-permute-done((bf16[256,2048]{1,0:T(8,128)(2,1)}, bf16[256,2048]{1,0:T(8,128)(2,1)}, u32[]{:S(2)}, u32[]{:S(2)}) %collective-permute-start.10) | collective-permute-done | bytes 1048608 | tf_op jit(solution)/shard_map/ppermute | solution.py:425
  122.7 2.3 collective-permute-start.11
  124.9 1.0 copy-done.8
  126.0 5.8 %shard_map.161 = (bf16[4,768,512]{2,1,0:T(8,128)(2,1)}, bf16[4,768,512]{2,1,0:T(8,128)(2,1)}) custom-call(s32[8]{0:T(128)} %broadcast_xor_fusion.1.blocks, bf16[768,512]{1,0:T(8,128)(2,1)} %get-tuple-element.42.att_t_ref.refs_0_, bf16[128,2048]{1,0:T(8,128)(2,1)} %get-tuple-element.39.a_ref.refs_1_.refs_0_, bf16[128,2048]{1,0:T(8,128)(2,1)} %copy-done.3, ...), custom_call_target="tpu_custom_call" | custom-call | flops 1 | bytes 1 | tf_op jit(solution)/shard_map/pallas_call | solution.py:384
  131.8 5.9 %shard_map.160.refs_1_.refs_5_ = f32[512,768]{1,0:T(8,128)} custom-call(bf16[8,768,768]{2,1,0:T(8,128)(2,1)} %bitcast.8, bf16[128,2048]{1,0:T(8,128)(2,1)} %get-tuple-element.39.a_ref.refs_1_.refs_0_, bf16[128,2048]{1,0:T(8,128)(2,1)} %copy-done.3, bf16[256,2048]{1,0:T(8,128)(2,1)} %collective-permute-done.6.refs_3_.refs_2_, bf16[256,2048]{1,0:T(8,128)(2,1)} %copy-done.8), custom_call_target="tpu_custom_call" | custom-call | flops 1 | bytes 1 | tf_op jit(solution)/shard_map/pallas_call | solution.py:355
  137.7 7.4 %collective-permute-done.5.refs_0_ = bf16[256,2048]{1,0:T(8,128)(2,1)S(1)} collective-permute-done((bf16[256,2048]{1,0:T(8,128)(2,1)}, bf16[256,2048]{1,0:T(8,128)(2,1)S(1)}, u32[]{:S(2)}, u32[]{:S(2)}) %collective-permute-start.5) | collective-permute-done | bytes 1048608 | tf_op jit(solution)/shard_map/ppermute | solution.py:425
  145.0 1.0 copy-done.1
  146.0 1.7 collective-permute-start.8
  148.2 6.4 %shard_map.164.refs_5_ = f32[512,768]{1,0:T(8,128)} custom-call(bf16[8,768,768]{2,1,0:T(8,128)(2,1)} %bitcast.9, bf16[128,2048]{1,0:T(8,128)(2,1)} %get-tuple-element.44.a_ref.refs_1_.refs_0_, bf16[128,2048]{1,0:T(8,128)(2,1)} %copy-done.7, bf16[256,2048]{1,0:T(8,128)(2,1)} %collective-permute-done.10.refs_3_.refs_2_, ...), custom_call_target="tpu_custom_call" | custom-call | flops 1 | bytes 1 | tf_op jit(solution)/shard_map/pallas_call | solution.py:355
  154.6 5.8 %shard_map.165 = (bf16[4,768,512]{2,1,0:T(8,128)(2,1)}, bf16[4,768,512]{2,1,0:T(8,128)(2,1)}) custom-call(s32[8]{0:T(128)} %broadcast_xor_fusion.1.blocks, bf16[768,512]{1,0:T(8,128)(2,1)} %get-tuple-element.42.att_t_ref.refs_0_, bf16[128,2048]{1,0:T(8,128)(2,1)} %get-tuple-element.44.a_ref.refs_1_.refs_0_, ...), custom_call_target="tpu_custom_call", output_to_operand_aliasing={{0}: (6, {}), {1}: (7, {})} | custom-call | flops 1 | bytes 1 | tf_op jit(solution)/shard_map/pallas_call | solution.py:384
  160.4 6.3 %collective-permute-done.8.refs_3_.refs_4_ = bf16[256,2048]{1,0:T(8,128)(2,1)S(1)} collective-permute-done((bf16[256,2048]{1,0:T(8,128)(2,1)}, bf16[256,2048]{1,0:T(8,128)(2,1)S(1)}, u32[]{:S(2)}, u32[]{:S(2)}) %collective-permute-start.8) | collective-permute-done | bytes 1048608 | tf_op jit(solution)/shard_map/ppermute | solution.py:428
  166.7 1.0 copy-done.9
  167.7 5.8 %shard_map.166 = (bf16[4,768,256]{2,1,0:T(8,128)(2,1)}, bf16[4,768,256]{2,1,0:T(8,128)(2,1)}) custom-call(s32[8]{0:T(128)} %broadcast_xor_fusion.blocks, bf16[768,512]{1,0:T(8,128)(2,1)} %get-tuple-element.42.att_t_ref.refs_0_, bf16[128,2048]{1,0:T(8,128)(2,1)} %get-tuple-element.41.a_ref.refs_0_.refs_1_, bf16[128,2048]{1,0:T(8,128)(2,1)} %copy-done.6, ...), custom_call_target="tpu_custom_call" | custom-call | flops 1 | bytes 1 | tf_op jit(solution)/shard_map/pallas_call | solution.py:384
  173.4 6.1 %shard_map.167.g_ref = bf16[512,768]{1,0:T(8,128)(2,1)} custom-call(bf16[8,768,768]{2,1,0:T(8,128)(2,1)} %bitcast.10, bf16[128,2048]{1,0:T(8,128)(2,1)} %get-tuple-element.41.a_ref.refs_0_.refs_1_, bf16[128,2048]{1,0:T(8,128)(2,1)} %copy-done.6, bf16[256,2048]{1,0:T(8,128)(2,1)} %shard_map.162.refs_2_.refs_3_, bf16[256,2048]{1,0:T(8,128)(2,1)} %copy-done.9, ...), custom_call_target="tpu_custom_call" | custom-call | flops 1 | bytes 1 | tf_op jit(solution)/shard_map/pallas_call | solution.py:355
  179.6 8.8 %shard_map.168 = (bf16[3,128,768]{2,1,0:T(8,128)(2,1)}, bf16[3,128,768]{2,1,0:T(8,128)(2,1)}, bf16[3,128,768]{2,1,0:T(8,128)(2,1)}, bf16[3,128,768]{2,1,0:T(8,12...) custom-call(s32[12]{0:T(128)} %pad_add_fusion.table.place, ...), custom_call_target="tpu_custom_call", output_to_operand_aliasing={{4}: (7, {}), {5}: (8, {}), {6}: (9, {}), {7}: (10, {})} | custom-call | flops 1 | bytes 1 | tf_op jit(solution)/shard_map/pallas_call | solution.py:296
  188.4 4.4 %collective-permute-start.15 = (bf16[4,768,512]{2,1,0:T(8,128)(2,1)}, bf16[4,768,512]{2,1,0:T(8,128)(2,1)S(1)}, u32[]{:S(2)}, u32[]{:S(2)}) collective-permute-start(bf16[4,768,512]{2,1,0:T(8,128)(2,1)} %get-tuple-element.62), channel_id=1, source_target_pairs={{0,4},{4,0},{8,12},{12,8},{16,20},{20,16},{24,28},{28,24},{1,5},{5... | collective-permute-start | bytes 9437192 | tf_op jit(solution)/shard_map/ppermute | solution.py:400
  192.9 5.4 %collective-permute-done.15 = bf16[4,768,512]{2,1,0:T(8,128)(2,1)S(1)} collective-permute-done((bf16[4,768,512]{2,1,0:T(8,128)(2,1)}, bf16[4,768,512]{2,1,0:T(8,128)(2,1)S(1)}, u32[]{:S(2)}, u32[]{:S(2)}) %collective-permute-start.15) | collective-permute-done | bytes 3145760 | tf_op jit(solution)/shard_map/ppermute | solution.py:400
  198.3 2.8 %convert_add_fusion = f32[4,768,512]{2,1,0:T(8,128)S(1)} fusion(bf16[4,768,512]{2,1,0:T(8,128)(2,1)S(1)} %collective-permute-done.15, bf16[4,768,512]{2,1,0:T(8,128)(2,1)} %get-tuple-element.61), kind=kLoop, calls=%fused_computation | loop fusion | flops 4718592 | bytes 12582912 | tf_op jit(solution)/shard_map/add | solution.py:414
  201.3 1.3 collective-permute-start.16
  203.1 1.4 collective-permute-start.19
  204.5 2.1 collective-permute-start.12
  207.8 29.2 %collective-permute-done.16 = bf16[2,768,512]{2,1,0:T(8,128)(2,1)S(1)} collective-permute-done((bf16[2,768,512]{2,1,0:T(8,128)(2,1)S(1)}, bf16[2,768,512]{2,1,0:T(8,128)(2,1)S(1)}, u32[]{:S(2)}, u32[]{:S(2)}) %collective-permute-start.16) | collective-permute-done | bytes 1572896 | tf_op jit(solution)/shard_map/ppermute | solution.py:400
  237.7 1.4 collective-permute-start.17
  239.3 1.2 copy-done.2
  241.3 1.2 collective-permute-start.20
  242.5 15.9 %collective-permute-done.14.refs_3_ = bf16[3,128,768]{2,1,0:T(8,128)(2,1)} collective-permute-done((bf16[3,128,768]{2,1,0:T(8,128)(2,1)S(1)}, bf16[3,128,768]{2,1,0:T(8,128)(2,1)}, u32[]{:S(2)}, u32[]{:S(2)}) %collective-permute-start.14) | collective-permute-done | bytes 589856 | tf_op jit(solution)/shard_map/ppermute | solution.py:400
  258.4 3.8 %shard_map.169 = (bf16[1,128,3072]{2,1,0:T(8,128)(2,1)}, bf16[1,128,3072]{2,1,0:T(8,128)(2,1)}, bf16[1,128,3072]{2,1,0:T(8,128)(2,1)}) custom-call(s32[12]{0:T(128)} %pad_add_fusion.table.place, bf16[3,128,768]{2,1,0:T(8,128)(2,1)} %get-tuple-element.54.refs_0_, bf16[3,128,768]{2,1,0:T(8,128)(2,1)} %collective-permute-done.12.refs_1_, ...), custom_call_target="tpu_custom_call" | custom-call | flops 1 | bytes 1 | tf_op jit(solution)/shard_map/pallas_call | solution.py:168
  262.2 1.3 fusion.3
  263.6 1.4 fusion.1
  264.9 1.1 pad_maximum_fusion
  (74 shorter events, 8.9 us)
Async XLA Ops:
  7.2 124.6 %all-gather.3.cloned.1.call-start = ((), (), s32[]{:S(2)}) async-start(), calls=%async_computation | async-start | bytes 10616832 | tf_op jit(solution)/shard_map/all_gather | solution.py:457
  13.1 51.1 %collective-permute-start = (bf16[3,128,768]{2,1,0:T(8,128)(2,1)}, bf16[3,128,768]{2,1,0:T(8,128)(2,1)S(1)}, u32[]{:S(2)}, u32[]{:S(2)}) collective-permute-start(bf16[3,128,768]{2,1,0:T(8,128)(2,1)} %get-tuple-element.36), channel_id=1, source_target_pairs={{0,1},{1,0},{2,3},{3,2},{4,5},{5,4},{6,7},{7,6},{8,9},{9,8},{10,11... | collective-permute-start | bytes 1769480 | tf_op jit(solution)/shard_map/ppermute | solution.py:400
  13.1 51.1 %collective-permute-start.1 = (bf16[3,128,768]{2,1,0:T(8,128)(2,1)}, bf16[3,128,768]{2,1,0:T(8,128)(2,1)S(1)}, u32[]{:S(2)}, u32[]{:S(2)}) collective-permute-start(bf16[3,128,768]{2,1,0:T(8,128)(2,1)} %get-tuple-element.37), channel_id=1, source_target_pairs={{0,2},{1,3},{2,0},{3,1},{4,6},{5,7},{6,4},{7,5},{8,10},{9,11},{10,... | collective-permute-start | bytes 1769480 | tf_op jit(solution)/shard_map/ppermute | solution.py:400
  15.5 58.8 %copy-start.14 = (s32[1,6,4]{1,2,0:T(4,128)S(1)}, s32[1,6,4]{1,2,0:T(4,128)}, u32[]{:S(2)}) copy-start(s32[1,6,4]{1,2,0:T(4,128)} %param.19) | copy-start | bytes 292
  15.5 58.9 %copy-start.13 = (s32[1,6,4,4]{1,3,2,0:T(4,128)S(1)}, s32[1,6,4,4]{1,3,2,0:T(4,128)}, u32[]{:S(2)}) copy-start(s32[1,6,4,4]{1,3,2,0:T(4,128)} %param.18) | copy-start | bytes 1156
  15.5 50.9 %collective-permute-start.2 = (bf16[3,128,768]{2,1,0:T(8,128)(2,1)}, bf16[3,128,768]{2,1,0:T(8,128)(2,1)S(1)}, u32[]{:S(2)}, u32[]{:S(2)}) collective-permute-start(bf16[3,128,768]{2,1,0:T(8,128)(2,1)} %get-tuple-element.38), channel_id=1, source_target_pairs={{0,3},{1,2},{2,1},{3,0},{4,7},{5,6},{6,5},{7,4},{8,11},{9,10},{10,... | collective-permute-start | bytes 1769480 | tf_op jit(solution)/shard_map/ppermute | solution.py:400
  18.4 54.4 %copy-start.4 = (bf16[128,2048]{1,0:T(8,128)(2,1)S(1)}, bf16[128,2048]{1,0:T(8,128)(2,1)}, u32[]{:S(2)}) copy-start(bf16[128,2048]{1,0:T(8,128)(2,1)} %get-tuple-element.41.a_ref.refs_0_.refs_1_) | copy-start | bytes 1572868
  18.4 54.5 %copy-start.5 = (bf16[128,2048]{1,0:T(8,128)(2,1)S(1)}, bf16[128,2048]{1,0:T(8,128)(2,1)}, u32[]{:S(2)}) copy-start(bf16[128,2048]{1,0:T(8,128)(2,1)} %get-tuple-element.44.a_ref.refs_1_.refs_0_) | copy-start | bytes 1572868
  18.4 45.8 %collective-permute-start.3 = (bf16[128,2048]{1,0:T(8,128)(2,1)}, bf16[128,2048]{1,0:T(8,128)(2,1)S(1)}, u32[]{:S(2)}, u32[]{:S(2)}) collective-permute-start(bf16[128,2048]{1,0:T(8,128)(2,1)} %get-tuple-element.39.a_ref.refs_1_.refs_0_), channel_id=1, source_target_pairs={{0,1},{1,0},{2,3},{3,2},{4,5},{5,4},{6,7},{7,6},{8,9},{9,8},{10,11... | collective-permute-start | bytes 1572872 | tf_op jit(solution)/shard_map/ppermute | solution.py:400
  64.2 2.3 copy-start.3
  64.2 2.3 copy-start.10
  64.2 2.3 copy-start.11
  66.5 0.8 copy-start.12
  69.6 31.1 %collective-permute-start.6 = (bf16[256,2048]{1,0:T(8,128)(2,1)}, bf16[256,2048]{1,0:T(8,128)(2,1)}, u32[]{:S(2)}, u32[]{:S(2)}) collective-permute-start(bf16[256,2048]{1,0:T(8,128)(2,1)} %shard_map.157.refs_4_), channel_id=1, source_target_pairs={{1,2},{2,1},{5,6},{6,5},{9,10},{10,9},{13,14},{14,13},{17,18},{18,... | collective-permute-start | bytes 3145736 | tf_op jit(solution)/shard_map/ppermute | solution.py:425
  72.8 29.8 %collective-permute-start.4 = (bf16[128,2048]{1,0:T(8,128)(2,1)S(1)}, bf16[128,2048]{1,0:T(8,128)(2,1)S(1)}, u32[]{:S(2)}, u32[]{:S(2)}) collective-permute-start(bf16[128,2048]{1,0:T(8,128)(2,1)S(1)} %copy-done.4), channel_id=1, source_target_pairs={{0,1},{1,0},{2,3},{3,2},{4,5},{5,4},{6,7},{7,6},{8,9},{9,8},{10,11... | collective-permute-start | bytes 1572872 | tf_op jit(solution)/shard_map/ppermute | solution.py:400
  72.9 22.7 %collective-permute-start.9 = (bf16[128,2048]{1,0:T(8,128)(2,1)S(1)}, bf16[128,2048]{1,0:T(8,128)(2,1)S(1)}, u32[]{:S(2)}, u32[]{:S(2)}) collective-permute-start(bf16[128,2048]{1,0:T(8,128)(2,1)S(1)} %copy-done.5), channel_id=1, source_target_pairs={{0,1},{1,0},{2,3},{3,2},{4,5},{5,4},{6,7},{7,6},{8,9},{9,8},{10,11... | collective-permute-start | bytes 1572872 | tf_op jit(solution)/shard_map/ppermute | solution.py:400
  95.6 0.8 copy-start.7
  96.4 12.0 %copy-start.19 = (s32[8]{0:T(128)S(1)}, s32[8]{0:T(128)}, u32[]{:S(2)}) copy-start(s32[8]{0:T(128)} %constant.29.clone) | copy-start | bytes 100
  98.6 24.0 %collective-permute-start.10 = (bf16[256,2048]{1,0:T(8,128)(2,1)}, bf16[256,2048]{1,0:T(8,128)(2,1)}, u32[]{:S(2)}, u32[]{:S(2)}) collective-permute-start(bf16[256,2048]{1,0:T(8,128)(2,1)} %shard_map.163), channel_id=1, source_target_pairs={{1,2},{2,1},{5,6},{6,5},{9,10},{10,9},{13,14},{14,13},{17,18},{18,... | collective-permute-start | bytes 3145736 | tf_op jit(solution)/shard_map/ppermute | solution.py:425
  100.7 24.3 %collective-permute-start.7 = (bf16[256,2048]{1,0:T(8,128)(2,1)}, bf16[256,2048]{1,0:T(8,128)(2,1)S(1)}, u32[]{:S(2)}, u32[]{:S(2)}) collective-permute-start(bf16[256,2048]{1,0:T(8,128)(2,1)} %collective-permute-done.6.refs_3_.refs_2_), channel_id=1, source_target_pairs={{1,0},{2,3},{5,4},{6,7},{9,8},{10,11},{13,12},{14,15},{17,16},{18,... | collective-permute-start | bytes 3145736 | tf_op jit(solution)/shard_map/ppermute | solution.py:428
  102.5 0.8 copy-start.6
  105.6 39.4 %collective-permute-start.5 = (bf16[256,2048]{1,0:T(8,128)(2,1)}, bf16[256,2048]{1,0:T(8,128)(2,1)S(1)}, u32[]{:S(2)}, u32[]{:S(2)}) collective-permute-start(bf16[256,2048]{1,0:T(8,128)(2,1)} %shard_map.159), channel_id=1, source_target_pairs={{1,2},{2,1},{5,6},{6,5},{9,10},{10,9},{13,14},{14,13},{17,18},{18,... | collective-permute-start | bytes 3145736 | tf_op jit(solution)/shard_map/ppermute | solution.py:425
  122.7 25.5 %collective-permute-start.11 = (bf16[256,2048]{1,0:T(8,128)(2,1)}, bf16[256,2048]{1,0:T(8,128)(2,1)}, u32[]{:S(2)}, u32[]{:S(2)}) collective-permute-start(bf16[256,2048]{1,0:T(8,128)(2,1)} %collective-permute-done.10.refs_3_.refs_2_), channel_id=1, source_target_pairs={{1,0},{2,3},{5,4},{6,7},{9,8},{10,11},{13,12},{14,15},{17,16},{18,... | collective-permute-start | bytes 3145736 | tf_op jit(solution)/shard_map/ppermute | solution.py:428
  124.9 1.0 copy-start.8
  145.0 1.0 copy-start.1
  146.0 1.7 copy-start.18
  146.0 20.7 %collective-permute-start.8 = (bf16[256,2048]{1,0:T(8,128)(2,1)}, bf16[256,2048]{1,0:T(8,128)(2,1)S(1)}, u32[]{:S(2)}, u32[]{:S(2)}) collective-permute-start(bf16[256,2048]{1,0:T(8,128)(2,1)} %shard_map.162.refs_2_.refs_3_), channel_id=1, source_target_pairs={{1,0},{2,3},{5,4},{6,7},{9,8},{10,11},{13,12},{14,15},{17,16},{18,... | collective-permute-start | bytes 3145736 | tf_op jit(solution)/shard_map/ppermute | solution.py:428
  166.7 1.0 copy-start.9
  188.4 9.9 %collective-permute-start.15 = (bf16[4,768,512]{2,1,0:T(8,128)(2,1)}, bf16[4,768,512]{2,1,0:T(8,128)(2,1)S(1)}, u32[]{:S(2)}, u32[]{:S(2)}) collective-permute-start(bf16[4,768,512]{2,1,0:T(8,128)(2,1)} %get-tuple-element.62), channel_id=1, source_target_pairs={{0,4},{4,0},{8,12},{12,8},{16,20},{20,16},{24,28},{28,24},{1,5},{5... | collective-permute-start | bytes 9437192 | tf_op jit(solution)/shard_map/ppermute | solution.py:400
  192.8 9.8 %collective-permute-start.18 = (bf16[4,768,256]{2,1,0:T(8,128)(2,1)}, bf16[4,768,256]{2,1,0:T(8,128)(2,1)S(1)}, u32[]{:S(2)}, u32[]{:S(2)}) collective-permute-start(bf16[4,768,256]{2,1,0:T(8,128)(2,1)} %get-tuple-element.64), channel_id=1, source_target_pairs={{0,4},{4,0},{8,12},{12,8},{16,20},{20,16},{24,28},{28,24},{1,5},{5... | collective-permute-start | bytes 4718600 | tf_op jit(solution)/shard_map/ppermute | solution.py:400
  201.1 1.5 copy-start
  201.3 35.7 %collective-permute-start.16 = (bf16[2,768,512]{2,1,0:T(8,128)(2,1)S(1)}, bf16[2,768,512]{2,1,0:T(8,128)(2,1)S(1)}, u32[]{:S(2)}, u32[]{:S(2)}) collective-permute-start(bf16[2,768,512]{2,1,0:T(8,128)(2,1)S(1)} %slice.60), channel_id=1, source_target_pairs={{0,8},{4,12},{8,0},{12,4},{16,24},{20,28},{24,16},{28,20},{1,9},{5... | collective-permute-start | bytes 4718600 | tf_op jit(solution)/shard_map/ppermute | solution.py:400
  202.6 1.8 copy-start.17
  202.6 4.0 %copy-start.16 = (bf16[3,128,768]{2,1,0:T(8,128)(2,1)S(1)}, bf16[3,128,768]{2,1,0:T(8,128)(2,1)}, u32[]{:S(2)}) copy-start(bf16[3,128,768]{2,1,0:T(8,128)(2,1)} %get-tuple-element.56) | copy-start | bytes 1769476
  202.6 4.5 %copy-start.15 = (bf16[3,128,768]{2,1,0:T(8,128)(2,1)S(1)}, bf16[3,128,768]{2,1,0:T(8,128)(2,1)}, u32[]{:S(2)}) copy-start(bf16[3,128,768]{2,1,0:T(8,128)(2,1)} %get-tuple-element.57) | copy-start | bytes 1769476
  203.1 36.1 %collective-permute-start.19 = (bf16[2,768,256]{2,1,0:T(8,128)(2,1)S(1)}, bf16[2,768,256]{2,1,0:T(8,128)(2,1)S(1)}, u32[]{:S(2)}, u32[]{:S(2)}) collective-permute-start(bf16[2,768,256]{2,1,0:T(8,128)(2,1)S(1)} %slice.61), channel_id=1, source_target_pairs={{0,16},{4,20},{8,24},{12,28},{16,0},{20,4},{24,8},{28,12},{1,17},{... | collective-permute-start | bytes 2359304 | tf_op jit(solution)/shard_map/ppermute | solution.py:400
  204.5 38.0 %collective-permute-start.12 = (bf16[3,128,768]{2,1,0:T(8,128)(2,1)S(1)}, bf16[3,128,768]{2,1,0:T(8,128)(2,1)}, u32[]{:S(2)}, u32[]{:S(2)}) collective-permute-start(bf16[3,128,768]{2,1,0:T(8,128)(2,1)S(1)} %copy-done.17), channel_id=1, source_target_pairs={{0,1},{1,0},{2,3},{3,2},{4,5},{5,4},{6,7},{7,6},{8,9},{9,8},{10,11... | collective-permute-start | bytes 1769480 | tf_op jit(solution)/shard_map/ppermute | solution.py:400
  206.6 35.9 %collective-permute-start.13 = (bf16[3,128,768]{2,1,0:T(8,128)(2,1)S(1)}, bf16[3,128,768]{2,1,0:T(8,128)(2,1)}, u32[]{:S(2)}, u32[]{:S(2)}) collective-permute-start(bf16[3,128,768]{2,1,0:T(8,128)(2,1)S(1)} %copy-done.16), channel_id=1, source_target_pairs={{0,2},{1,3},{2,0},{3,1},{4,6},{5,7},{6,4},{7,5},{8,10},{9,11},{10,... | collective-permute-start | bytes 1769480 | tf_op jit(solution)/shard_map/ppermute | solution.py:400
  207.2 51.2 %collective-permute-start.14 = (bf16[3,128,768]{2,1,0:T(8,128)(2,1)S(1)}, bf16[3,128,768]{2,1,0:T(8,128)(2,1)}, u32[]{:S(2)}, u32[]{:S(2)}) collective-permute-start(bf16[3,128,768]{2,1,0:T(8,128)(2,1)S(1)} %copy-done.15), channel_id=1, source_target_pairs={{0,3},{1,2},{2,1},{3,0},{4,7},{5,6},{6,5},{7,4},{8,11},{9,10},{10,... | collective-permute-start | bytes 1769480 | tf_op jit(solution)/shard_map/ppermute | solution.py:400
  237.7 25.8 %collective-permute-start.17 = (bf16[1,768,512]{2,1,0:T(8,128)(2,1)S(1)}, bf16[1,768,512]{2,1,0:T(8,128)(2,1)}, u32[]{:S(2)}, u32[]{:S(2)}) collective-permute-start(bf16[1,768,512]{2,1,0:T(8,128)(2,1)S(1)} %slice.62), channel_id=1, source_target_pairs={{0,16},{4,20},{8,24},{12,28},{16,0},{20,4},{24,8},{28,12},{1,17},{... | collective-permute-start | bytes 2359304 | tf_op jit(solution)/shard_map/ppermute | solution.py:400
  239.3 1.2 copy-start.2
  241.3 20.9 %collective-permute-start.20 = (bf16[1,768,256]{2,1,0:T(8,128)(2,1)}, bf16[1,768,256]{2,1,0:T(8,128)(2,1)}, u32[]{:S(2)}, u32[]{:S(2)}) collective-permute-start(bf16[1,768,256]{2,1,0:T(8,128)(2,1)} %slice.63), channel_id=1, source_target_pairs={{0,8},{4,12},{8,0},{12,4},{16,24},{20,28},{24,16},{28,20},{1,9},{5... | collective-permute-start | bytes 1179656 | tf_op jit(solution)/shard_map/ppermute | solution.py:400
Sparse Core Ops, SparseCore 0:
  9.9 60.4 all-gather.2

commit v2 on v1

--- a/solution.py
+++ b/solution.py
@@ -152,31 +152,55 @@
     )(value, *after)
 
 
-def unpack_kernel(group, place, *refs):
-    parts, outs = refs[:group], refs[-3:]
+def unpack_first_kernel(partners, place, *refs):
+    parts, outs = refs[: len(partners)], refs[-3:]
     width = parts[0].shape[2]
-    for s, part in enumerate(parts):
+    for s, part in zip(partners, parts):
         columns = pl.ds(pl.multiple_of(place[s] * width, LANES), width)
         for i, out in enumerate(outs):
             out[0, :, columns] = part[i]
 
 
-def unpack(place, parts, after=()):
+def unpack_last_kernel(count, place, *refs):
+    for s, part in enumerate(refs[:count]):
+
+        @pl.when(pl.program_id(0) == s)
+        def _(part=part):
+            for i, out in enumerate(refs[-3:]):
+                out[0] = part[i]
+
+
+def unpack(place, parts):
     group = place.shape[0] // 3
     _, rows, width = parts[0].shape
     shape = jax.ShapeDtypeStruct((1, rows, width * group), BF16)
-    return pl.pallas_call(
-        functools.partial(unpack_kernel, group),
+    early = group // 2
+    outs = pl.pallas_call(
+        functools.partial(unpack_first_kernel, range(early)),
         out_shape=[shape] * 3,
         grid_spec=pltpu.PrefetchScalarGridSpec(
             num_scalar_prefetch=1,
             grid=(1,),
-            in_specs=[whole(part.shape) for part in parts] + awaited(after),
+            in_specs=[whole(part.shape) for part in parts[:early]],
             out_specs=[whole(shape.shape)] * 3,
         ),
         cost_estimate=light(),
         compiler_params=params(),
-    )(place, *parts, *after)
+    )(place, *parts[:early])
+    late = parts[early:]
+    return pl.pallas_call(
+        functools.partial(unpack_last_kernel, len(late)),
+        out_shape=[shape] * 3,
+        grid_spec=pltpu.PrefetchScalarGridSpec(
+            num_scalar_prefetch=1,
+            grid=(len(late),),
+            in_specs=[whole(part.shape) for part in late] + awaited(outs),
+            out_specs=[pl.BlockSpec((1, rows, width), lambda i, t: (0, 0, t[early + i]))] * 3,
+        ),
+        input_output_aliases={1 + len(late) + i: i for i in range(3)},
+        cost_estimate=light(),
+        compiler_params=params(),
+    )(place, *late, *outs)
 
 
 def forward_kernel(group, table, order_ref, bias_ref, *refs):
@@ -262,9 +286,10 @@
 
 
 def backward_kernel(
-    group, passed, table, g_ref, att_ref, weight_ref, q_t_ref, k_ref, v_ref, *refs
+    group, chains, table, g_ref, att_ref, weight_ref, q_t_ref, k_ref, v_ref, *refs
 ):
-    outs, held = refs[passed : passed + group], refs[-1]
+    sums, refs = refs[: 2 * chains], refs[2 * chains :]
+    outs, folded, held = refs[:group], refs[group:-1], refs[-1]
     rows = outs[0].shape[1]
     grad = g_ref[...]
     weights = weight_ref[0]
@@ -284,19 +309,30 @@
     for s, out in enumerate(outs):
         here = pl.ds(pl.multiple_of(slot(table, s) * rows, rows), rows)
         out[...] = held[:, here, :]
-
-
-def backward(table, grad, att, weights, q_t, k, v, passed):
+    for c in range(chains):
+        keep_ref, arrived_ref = sums[2 * c : 2 * c + 2]
+        kept_ref, send_ref = folded[2 * c : 2 * c + 2]
+        half = kept_ref.shape[0]
+        kept_ref[...] = keep_ref[:half] + arrived_ref[:half]
+        send_ref[...] = keep_ref[half:] + arrived_ref[half:]
+
+
+def backward(table, grad, att, weights, q_t, k, v, sums):
     group = table.shape[0] // 3
     total, width = grad.shape
     rows = total // group
     heads = width // HEAD_DIM
     column = pl.BlockSpec((total, HEAD_DIM), lambda h, *_: (0, h))
     row = pl.BlockSpec((HEAD_DIM, total), lambda h, *_: (h, 0))
-    return pl.pallas_call(
-        functools.partial(backward_kernel, group, len(passed)),
-        out_shape=[jax.ShapeDtypeStruct((3, rows, width), BF16)] * group
-        + [jax.ShapeDtypeStruct(x.shape, x.dtype) for x in passed],
+    sum_shapes, sum_specs, half_shapes, half_specs = [], [], [], []
+    for keep, _ in sums:
+        count, _, columns = keep.shape
+        sum_specs += [pl.BlockSpec((count, HEAD_DIM, columns), lambda h, *_: (0, h, 0))] * 2
+        half_specs += [pl.BlockSpec((count // 2, HEAD_DIM, columns), lambda h, *_: (0, h, 0))] * 2
+        half_shapes += [jax.ShapeDtypeStruct((count // 2, width, columns), BF16)] * 2
+    outs = pl.pallas_call(
+        functools.partial(backward_kernel, group, len(sums)),
+        out_shape=[jax.ShapeDtypeStruct((3, rows, width), BF16)] * group + half_shapes,
         grid_spec=pltpu.PrefetchScalarGridSpec(
             num_scalar_prefetch=1,
             grid=(heads,),
@@ -308,15 +344,16 @@
                 column,
                 column,
             ]
-            + awaited(passed),
+            + sum_specs,
             out_specs=[pl.BlockSpec((3, rows, HEAD_DIM), lambda h, *_: (0, 0, h))] * group
-            + awaited(passed),
+            + half_specs,
             scratch_shapes=[pltpu.VMEM((3, total, HEAD_DIM), BF16)],
         ),
-        input_output_aliases={7 + i: group + i for i in range(len(passed))},
-        cost_estimate=light(),
-        compiler_params=params(),
-    )(table, grad, att, weights, q_t, k, v, *passed)
+        cost_estimate=light(),
+        compiler_params=params(),
+    )(table, grad, att, weights, q_t, k, v, *[x for pair in sums for x in pair])
+    back, halves = outs[:group], outs[group:]
+    return list(back), [halves[2 * c : 2 * c + 2] for c in range(len(sums))]
 
 
 def block_rows(refs, columns):
@@ -366,34 +403,40 @@
     )(*[weights] * len(at), *rows, *before, *after)
 
 
-def outer_kernel(count, blocks, att_t_ref, *refs):
-    rows, (keep_ref, send_ref) = refs[:count], refs[-2:]
-    half, _, part = keep_ref.shape
+def outer_kernel(count, start, passed, blocks, att_t_ref, *refs):
+    rows = refs[:count]
+    keep_ref, send_ref = refs[len(refs) - 2 - passed : len(refs) - passed]
+    half, _, width = keep_ref.shape
+    part = rows[0].shape[1] // (2 * half)
     att_t = att_t_ref[...]
     for p in range(2 * half):
         out = keep_ref if p < half else send_ref
-        here = block_rows(rows, block_columns(blocks, p, part))
-        out[p % half] = dot(att_t, here).astype(BF16)
-
-
-def outer(blocks, att_t, rows, start, width, buffers=()):
+        columns = pl.ds(pl.multiple_of(blocks[p] * part + start, LANES), width)
+        out[p % half] = dot(att_t, block_rows(rows, columns)).astype(BF16)
+
+
+def outer(blocks, att_t, rows, start, width, place, total, buffers=(), passed=()):
     half = blocks.shape[0] // 2
     heads = att_t.shape[0]
-    part = rows[0].shape[1] // (2 * half)
     first = 2 + len(rows)
-    return pl.pallas_call(
-        functools.partial(outer_kernel, len(rows)),
-        out_shape=[jax.ShapeDtypeStruct((half, heads, width), BF16)] * 2,
+    handed = list(buffers) + list(passed)
+    outs = [jax.ShapeDtypeStruct((half, heads, total), BF16)] * 2
+    aliases = {first + i: i for i in range(len(buffers))}
+    aliases |= {first + len(buffers) + i: 2 + i for i in range(len(passed))}
+    return pl.pallas_call(
+        functools.partial(outer_kernel, len(rows), start, len(passed)),
+        out_shape=outs + [jax.ShapeDtypeStruct(x.shape, x.dtype) for x in passed],
         grid_spec=pltpu.PrefetchScalarGridSpec(
             num_scalar_prefetch=1,
             grid=(1,),
-            in_specs=[whole(att_t.shape)] + [whole(r.shape) for r in rows] + awaited(buffers),
-            out_specs=[pl.BlockSpec((half, heads, part), lambda i, b: (0, 0, start // part))] * 2,
-        ),
-        input_output_aliases={first + i: i for i in range(len(buffers))},
-        cost_estimate=light(),
-        compiler_params=params(),
-    )(blocks, att_t, *rows, *buffers)
+            in_specs=[whole(att_t.shape)] + [whole(r.shape) for r in rows] + awaited(handed),
+            out_specs=[pl.BlockSpec((half, heads, width), lambda i, b: (0, 0, place // width))] * 2
+            + awaited(passed),
+        ),
+        input_output_aliases=aliases,
+        cost_estimate=light(),
+        compiler_params=params(),
+    )(blocks, att_t, *rows, *handed)
 
 
 def swap(value, axis, size, mask):
@@ -465,28 +508,36 @@
     bias = jnp.pad(bias, ((0, 0), (0, LANES - cubes), (0, 0)))
 
     att, att_t, weights, q_t, k, v = forward(table, token_order, bias, parts, after=[both])
-    sums_to = widths[0] + widths[1]
+    part = widths[0]
+    cut = part // 2 if part % (2 * LANES) == 0 else 0
+    order, other_order = blocks(masks[0]), blocks(masks[1])
     first = gather_rows(pieces[0], nears[0], group, both)
     grad = project(first, weights_full, 0, None, F32)
-    state = outer(blocks(masks[0]), att_t, first, 0, sums_to)
+    state = outer(order, att_t, first, 0, part, 0, part + cut)
     second = gather_rows(pieces[1], nears[1], group, join(pieces[1], nears[1], after=[att_t]))
-    third = gather_rows(pieces[2], nears[2], group, None, held=[grad, state[0]])
-    grad = project(second, weights_full, widths[0], grad, F32)
-    state = outer(blocks(masks[0]), att_t, second, widths[0], sums_to, state)
-    other = outer(blocks(masks[1]), att_t, third, 0, widths[2])
-    grad = project(
-        third, weights_full, widths[0] + widths[1], grad, BF16, after=[state[0], other[0]]
+    third = gather_rows(pieces[2], nears[2], group, held=[grad, state[0]])
+    grad = project(second, weights_full, part, grad, F32)
+    if cut:
+        state = outer(order, att_t, second, 0, cut, part, part + cut, state)
+    rest = part - cut
+    other = outer(other_order, att_t, second, cut, rest, part, part + rest)
+    *other, keep, send, grad = outer(
+        other_order, att_t, third, 0, part, 0, part + rest, other, passed=[*state, grad]
     )
-    *back, keep, send, other_keep, other_send = backward(
-        table, grad, att, weights, q_t, k, v, [*state, *other]
+    grad = project(third, weights_full, 2 * part, grad, BF16, after=[other[0], keep])
+    arrived = swap(send, "dp", dp, masks[0][0])
+    other_arrived = swap(other[1], "dp", dp, masks[1][0])
+    back, halves = backward(
+        table, grad, att, weights, q_t, k, v, [(keep, arrived), (other[0], other_arrived)]
     )
-    states = [(keep, send, masks[0]), (other_keep, other_send, masks[1])]
+    states = [(*half, mask[1:]) for half, mask in zip(halves, masks)]
     while any(masks for _, _, masks in states):
         states = [fold(state, dp) for state in states]
     back = [back[0]] + [swap(back[s], "head", group, s) for s in range(1, group)]
+    low, high = [kept for kept, _, _ in states]
+    total = jnp.concatenate([low, high[:, part:], high[:, :part]], axis=1)
     query_back, key_back, value_back = unpack(table, back)
-    sums = [kept for kept, _, _ in states]
-    return (att[None], query_back, key_back, value_back, jnp.concatenate(sums, axis=1))
+    return (att[None], query_back, key_back, value_back, total)
 
 
 def solution(mesh):

time: 275 us -> 270 us (0.982)
  waiting for transfers between devices: 136 us -> 123 us
  Pallas kernels: 71 us -> 82.4 us
    pallas_call x5 -> x7, Pallas kernels: 30 us -> 41.5 us  [the longest x4 22.8 us: outer(): pl.pallas_call(functools.partial(outer_kernel, len(rows), start, len(pass...]
    ppermute x15, waiting for transfers between devices: 108 us -> 100 us  [swap(): return lax.ppermute(value, axis, [(i, i ^ mask) for i in range(size)])]
    ppermute x3, waiting for transfers between devices: 6.35 us -> 0.01 us  [gather_rows(): outer = lax.ppermute(inner, 'head', [(1, 0), (2, 3)])]
  transfers between devices with their start and end apart: 22 -> 22, of which waited for: 9 -> 10; matrix products, arithmetic and copies ran while one was open for 4% -> 3% of each run, Pallas kernels for 18% -> 24%
where the time goes in v2:
time: 270 us; the launch traced here: 269 us
  waiting for transfers between devices  123 us (46%)
  Pallas kernels  82.4 us (31%)
  starting transfers between devices  32.4 us (12%)
  between operations  14.3 us (5%)
  local copies, waits for them, and re-layouts  9.31 us (3%)
  other arithmetic  8.09 us (3%)
    ppermute x15, waiting for transfers between devices, swap(): return lax.ppermute(value, axis, [(i, i ^ mask) for i in range(size)])  100 us
    pallas_call x4, Pallas kernels, outer(): pl.pallas_call(functools.partial(outer_kernel, len(rows), start, len(pass...  22.8 us
    ppermute x3, waiting for transfers between devices, gather_rows(): lax.ppermute(join(own, near) if both is None else both, 'head', [(1, 2),...  22.1 us
    ppermute x15, starting transfers between devices, swap(): return lax.ppermute(value, axis, [(i, i ^ mask) for i in range(size)])  18.6 us
    pallas_call x3, Pallas kernels, project(): pl.pallas_call(functools.partial(project_kernel, len(rows), len(at), not...  18.3 us
    pallas_call x1, Pallas kernels, backward(): pl.pallas_call(functools.partial(backward_kernel, group, len(sums)), out_...  12.3 us
    pallas_call x1, Pallas kernels, forward(): pl.pallas_call(functools.partial(forward_kernel, group), out_shape=[jax.S...  9.47 us
    ppermute x3, starting transfers between devices, gather_rows(): lax.ppermute(join(own, near) if both is None else both, 'head', [(1, 2),...  8.46 us
  transfers between devices with their start and end apart: 22, of which 10 were waited for; matrix products, arithmetic and copies ran while one was open for 3% of the time, Pallas kernels for 24%

profile of v2, /device:TPU:9, one launch (start us, length us, event | category | flops | bytes accessed | tf_op | source)
XLA Modules:
  0.0 269.4 jit_solution(6490843369997561988)
XLA Ops:
  9.2 3.8 %shard_map.146 = (bf16[3,128,768]{2,1,0:T(8,128)(2,1)}, bf16[3,128,768]{2,1,0:T(8,128)(2,1)}, bf16[3,128,768]{2,1,0:T(8,128)(2,1)}, bf16[3,128,768]{2,1,0:T(8,128)(2,1)}) custom-call(s32[12]{0:T(128)} %pad_add_fusion.table.place, bf16[1,128,3072]{2,1,0:T(8,128)(2,1)} %refs_9_.1, bf16[1,128,3072]{2,1,0:T(8,128)(2,1)} %refs_10_.1, ...), custom_call_target="tpu_custom_call" | custom-call | flops 1 | bytes 1 | tf_op jit(solution)/shard_map/pallas_call | solution.py:82
  13.0 2.5 collective-permute-start.1
  15.7 2.6 shard_map.147
  18.3 1.0 collective-permute-start.3
  19.3 44.9 %collective-permute-done.3.b_ref.refs_2_.refs_1_ = bf16[128,2048]{1,0:T(8,128)(2,1)S(1)} collective-permute-done((bf16[128,2048]{1,0:T(8,128)(2,1)}, bf16[128,2048]{1,0:T(8,128)(2,1)S(1)}, u32[]{:S(2)}, u32[]{:S(2)}) %collective-permute-start.3) | collective-permute-done | bytes 524320 | tf_op jit(solution)/shard_map/ppermute | solution.py:443
  64.2 2.3 collective-permute-done.2.refs_2_.refs_3_
  66.5 2.2 shard_map.148.refs_4_
  68.7 3.2 %collective-permute-start.6 = (bf16[256,2048]{1,0:T(8,128)(2,1)}, bf16[256,2048]{1,0:T(8,128)(2,1)}, u32[]{:S(2)}, u32[]{:S(2)}) collective-permute-start(bf16[256,2048]{1,0:T(8,128)(2,1)} %shard_map.148.refs_4_), channel_id=1, source_target_pairs={{1,2},{2,1},{5,6},{6,5},{9,10},{10,9},{13,14},{14,13},{17,18},{18,... | collective-permute-start | bytes 3145736 | tf_op jit(solution)/shard_map/ppermute | solution.py:468
  72.0 1.4 collective-permute-start.9
  74.6 9.5 %shard_map.149 = (bf16[512,768]{1,0:T(8,128)(2,1)}, bf16[768,512]{1,0:T(8,128)(2,1)}, bf16[6,512,512]{2,1,0:T(8,128)(2,1)}, bf16[768,512]{1,0:T(8,128)(2,1)}, bf...) custom-call(s32[12]{0:T(128)} %pad_add_fusion.table.place, s32[1,512]{1,0:T(1,128)} %order_ref.1, ...), custom_call_target="tpu_custom_call" | custom-call | flops 1 | bytes 1 | tf_op jit(solution)/shard_map/pallas_call | solution.py:251
  84.1 10.6 %collective-permute-done.9.b_ref.refs_1_.refs_2_ = bf16[128,2048]{1,0:T(8,128)(2,1)S(1)} collective-permute-done((bf16[128,2048]{1,0:T(8,128)(2,1)S(1)}, bf16[128,2048]{1,0:T(8,128)(2,1)S(1)}, u32[]{:S(2)}, u32[]{:S(2)}) %collective-permute-start.9) | collective-permute-done | bytes 524320 | tf_op jit(solution)/shard_map/ppermute | solution.py:443
  95.4 2.3 shard_map.154
  97.7 2.1 collective-permute-start.10
  99.8 2.3 collective-permute-start.7
  102.9 2.2 shard_map.150
  105.1 3.2 %collective-permute-start.5 = (bf16[256,2048]{1,0:T(8,128)(2,1)}, bf16[256,2048]{1,0:T(8,128)(2,1)S(1)}, u32[]{:S(2)}, u32[]{:S(2)}) collective-permute-start(bf16[256,2048]{1,0:T(8,128)(2,1)} %shard_map.150), channel_id=1, source_target_pairs={{1,2},{2,1},{5,6},{6,5},{9,10},{10,9},{13,14},{14,13},{17,18},{18,... | collective-permute-start | bytes 3145736 | tf_op jit(solution)/shard_map/ppermute | solution.py:468
  108.9 12.7 %collective-permute-done.10.refs_2_.refs_3_ = bf16[256,2048]{1,0:T(8,128)(2,1)S(1)} collective-permute-done((bf16[256,2048]{1,0:T(8,128)(2,1)}, bf16[256,2048]{1,0:T(8,128)(2,1)S(1)}, u32[]{:S(2)}, u32[]{:S(2)}) %collective-permute-start.10) | collective-permute-done | bytes 1048608 | tf_op jit(solution)/shard_map/ppermute | solution.py:468
  121.5 1.3 collective-permute-start.11
  122.9 5.8 %shard_map.152 = (bf16[4,768,384]{2,1,0:T(8,128)(2,1)}, bf16[4,768,384]{2,1,0:T(8,128)(2,1)}) custom-call(s32[8]{0:T(128)} %broadcast_xor_fusion.1.blocks, bf16[768,512]{1,0:T(8,128)(2,1)} %get-tuple-element.50.att_t_ref.refs_0_, bf16[128,2048]{1,0:T(8,128)(2,1)} %get-tuple-element.47.a_ref.refs_1_.refs_0_, bf16[128,2048]{1,0:T(8,128)(2,1)} %copy-done.7, ...), custom_call_target="tpu_custom_call" | custom-call | flops 1 | bytes 1 | tf_op jit(solution)/shard_map/pallas_call | solution.py:426
  128.7 5.9 %shard_map.151.refs_1_.refs_5_ = f32[512,768]{1,0:T(8,128)} custom-call(bf16[8,768,768]{2,1,0:T(8,128)(2,1)} %bitcast.8, bf16[128,2048]{1,0:T(8,128)(2,1)} %get-tuple-element.47.a_ref.refs_1_.refs_0_, bf16[128,2048]{1,0:T(8,128)(2,1)} %copy-done.7, bf16[256,2048]{1,0:T(8,128)(2,1)} %collective-permute-done.6.refs_3_.refs_2_, ...), custom_call_target="tpu_custom_call" | custom-call | flops 1 | bytes 1 | tf_op jit(solution)/shard_map/pallas_call | solution.py:392
  134.6 9.4 %collective-permute-done.5.refs_0_ = bf16[256,2048]{1,0:T(8,128)(2,1)S(1)} collective-permute-done((bf16[256,2048]{1,0:T(8,128)(2,1)}, bf16[256,2048]{1,0:T(8,128)(2,1)S(1)}, u32[]{:S(2)}, u32[]{:S(2)}) %collective-permute-start.5) | collective-permute-done | bytes 1048608 | tf_op jit(solution)/shard_map/ppermute | solution.py:468
  144.0 1.0 copy-done
  145.0 1.7 collective-permute-start.8
  147.2 1.0 copy-done.2
  148.2 5.6 %shard_map.155 = (bf16[4,768,384]{2,1,0:T(8,128)(2,1)}, bf16[4,768,384]{2,1,0:T(8,128)(2,1)}) custom-call(s32[8]{0:T(128)} %broadcast_xor_fusion.blocks, bf16[768,512]{1,0:T(8,128)(2,1)} %get-tuple-element.50.att_t_ref.refs_0_, bf16[128,2048]{1,0:T(8,128)(2,1)} %get-tuple-element.52.a_ref.refs_0_.refs_1_, bf16[128,2048]{1,0:T(8,128)(2,1)} %copy-done.4, ...), custom_call_target="tpu_custom_call" | custom-call | flops 1 | bytes 1 | tf_op jit(solution)/shard_map/pallas_call | solution.py:426
  153.8 6.4 %shard_map.157.refs_8_ = f32[512,768]{1,0:T(8,128)} custom-call(bf16[8,768,768]{2,1,0:T(8,128)(2,1)} %bitcast.9, bf16[128,2048]{1,0:T(8,128)(2,1)} %get-tuple-element.52.a_ref.refs_0_.refs_1_, bf16[128,2048]{1,0:T(8,128)(2,1)} %copy-done.4, bf16[256,2048]{1,0:T(8,128)(2,1)} %copy-done.1, bf16[256,2048]{1,0:T(8,128)(2,1)} %copy-done.2, ...), custom_call_target="tpu_custom_call" | custom-call | flops 1 | bytes 1 | tf_op jit(solution)/shard_map/pallas_call | solution.py:392
  160.1 5.6 %shard_map.156 = (bf16[4,768,384]{2,1,0:T(8,128)(2,1)}, bf16[4,768,384]{2,1,0:T(8,128)(2,1)}) custom-call(s32[8]{0:T(128)} %broadcast_xor_fusion.1.blocks, bf16[768,512]{1,0:T(8,128)(2,1)} %get-tuple-element.50.att_t_ref.refs_0_, bf16[128,2048]{1,0:T(8,128)(2,1)} %get-tuple-element.52.a_ref.refs_0_.refs_1_, ...), custom_call_target="tpu_custom_call", output_to_operand_aliasing={{0}: (6, {}), {1}: (7, {})} | custom-call | flops 1 | bytes 1 | tf_op jit(solution)/shard_map/pallas_call | solution.py:426
  165.7 1.0 copy-done.10
  166.7 5.8 %shard_map.158 = (bf16[4,768,384]{2,1,0:T(8,128)(2,1)}, bf16[4,768,384]{2,1,0:T(8,128)(2,1)}, bf16[4,768,384]{2,1,0:T(8,128)(2,1)}, bf16[4,768,384]{2,1,0:T(8,128)(2,1)}, f32[512,768]{1,0:T(8,128)}) custom-call(s32[8]{0:T(128)} %broadcast_xor_fusion.blocks, ...), custom_call_target="tpu_custom_call", output_to_operand_aliasing={{0}: (6, {}), {1}: (7, {}), {2}: (8, {}), {3}: (9, {}), {4}... | custom-call | flops 1 | bytes 1 | tf_op jit(solution)/shard_map/pallas_call | solution.py:426
  172.6 4.4 %collective-permute-start.12 = (bf16[4,768,384]{2,1,0:T(8,128)(2,1)}, bf16[4,768,384]{2,1,0:T(8,128)(2,1)S(1)}, u32[]{:S(2)}, u32[]{:S(2)}) collective-permute-start(bf16[4,768,384]{2,1,0:T(8,128)(2,1)} %get-tuple-element.65), channel_id=1, source_target_pairs={{0,4},{4,0},{8,12},{12,8},{16,20},{20,16},{24,28},{28,24},{1,5},{5... | collective-permute-start | bytes 7077896 | tf_op jit(solution)/shard_map/ppermute | solution.py:443
  177.0 6.0 %shard_map.159.g_ref = bf16[512,768]{1,0:T(8,128)(2,1)} custom-call(bf16[8,768,768]{2,1,0:T(8,128)(2,1)} %bitcast.10, bf16[128,2048]{1,0:T(8,128)(2,1)} %get-tuple-element.49.a_ref.refs_0_.refs_1_, bf16[128,2048]{1,0:T(8,128)(2,1)} %copy-done.9, bf16[256,2048]{1,0:T(8,128)(2,1)} %shard_map.153.refs_2_.refs_3_, bf16[256,2048]{1,0:T(8,128)(2,1)} %copy-done.10, ...), custom_call_target="tpu_custom_call" | custom-call | flops 1 | bytes 1 | tf_op jit(solution)/shard_map/pallas_call | solution.py:392
  183.0 1.3 collective-permute-done.12.refs_1_
  185.8 12.3 %shard_map.160 = (bf16[3,128,768]{2,1,0:T(8,128)(2,1)}, bf16[3,128,768]{2,1,0:T(8,128)(2,1)}, bf16[3,128,768]{2,1,0:T(8,128)(2,1)}, bf16[3,128,768]{2,1,0:T(8,12...) custom-call(s32[12]{0:T(128)} %pad_add_fusion.table.place, ...), custom_call_target="tpu_custom_call" | custom-call | flops 1 | bytes 1 | tf_op jit(solution)/shard_map/pallas_call | solution.py:333
  198.0 1.3 collective-permute-start.19
  199.3 1.2 collective-permute-start.17
  200.6 2.8 %collective-permute-start.14 = (bf16[3,128,768]{2,1,0:T(8,128)(2,1)}, bf16[3,128,768]{2,1,0:T(8,128)(2,1)}, u32[]{:S(2)}, u32[]{:S(2)}) collective-permute-start(bf16[3,128,768]{2,1,0:T(8,128)(2,1)} %get-tuple-element.67), channel_id=1, source_target_pairs={{0,2},{1,3},{2,0},{3,1},{4,6},{5,7},{6,4},{7,5},{8,10},{9,11},{10,... | collective-permute-start | bytes 1769480 | tf_op jit(solution)/shard_map/ppermute | solution.py:443
  204.5 21.0 %collective-permute-done.19 = bf16[2,768,384]{2,1,0:T(8,128)(2,1)S(1)} collective-permute-done((bf16[2,768,384]{2,1,0:T(8,128)(2,1)}, bf16[2,768,384]{2,1,0:T(8,128)(2,1)S(1)}, u32[]{:S(2)}, u32[]{:S(2)}) %collective-permute-start.19) | collective-permute-done | bytes 1179680 | tf_op jit(solution)/shard_map/ppermute | solution.py:443
  225.5 1.7 convert_add_fusion
  227.2 1.3 collective-permute-start.20
  228.8 1.4 copy-done.5
  230.2 1.3 collective-permute-start.18
  231.6 9.2 %collective-permute-done.16.refs_1_ = bf16[3,128,768]{2,1,0:T(8,128)(2,1)S(1)} collective-permute-done((bf16[3,128,768]{2,1,0:T(8,128)(2,1)}, bf16[3,128,768]{2,1,0:T(8,128)(2,1)S(1)}, u32[]{:S(2)}, u32[]{:S(2)}) %collective-permute-start.16) | collective-permute-done | bytes 589856 | tf_op jit(solution)/shard_map/ppermute | solution.py:443
  241.6 3.4 %shard_map.161 = (bf16[1,128,3072]{2,1,0:T(8,128)(2,1)}, bf16[1,128,3072]{2,1,0:T(8,128)(2,1)}, bf16[1,128,3072]{2,1,0:T(8,128)(2,1)}) custom-call(s32[12]{0:T(128)} %pad_add_fusion.table.place, bf16[3,128,768]{2,1,0:T(8,128)(2,1)} %get-tuple-element.69.refs_0_, bf16[3,128,768]{2,1,0:T(8,128)(2,1)} %copy-done.15), custom_call_target="tpu_custom_call" | custom-call | flops 1 | bytes 1 | tf_op jit(solution)/shard_map/pallas_call | solution.py:178
  245.0 10.4 %collective-permute-done.15.refs_1_ = bf16[3,128,768]{2,1,0:T(8,128)(2,1)} collective-permute-done((bf16[3,128,768]{2,1,0:T(8,128)(2,1)}, bf16[3,128,768]{2,1,0:T(8,128)(2,1)}, u32[]{:S(2)}, u32[]{:S(2)}) %collective-permute-start.15) | collective-permute-done | bytes 589856 | tf_op jit(solution)/shard_map/ppermute | solution.py:443
  255.4 3.0 %shard_map.162 = (bf16[1,128,3072]{2,1,0:T(8,128)(2,1)}, bf16[1,128,3072]{2,1,0:T(8,128)(2,1)}, bf16[1,128,3072]{2,1,0:T(8,128)(2,1)}) custom-call(s32[12]{0:T(128)} %pad_add_fusion.table.place, bf16[3,128,768]{2,1,0:T(8,128)(2,1)} %collective-permute-done.14.refs_0_, ...), custom_call_target="tpu_custom_call", output_to_operand_aliasing={{0}: (3, {}), {1}: (4, {}), {2}: (5, {})} | custom-call | flops 1 | bytes 1 | tf_op jit(solution)/shard_map/pallas_call | solution.py:191
  258.4 1.3 fusion.3
  260.2 1.2 fusion.2
  261.4 1.1 pad_maximum_fusion
  (74 shorter events, 10.4 us)
Async XLA Ops:
  7.2 121.6 %all-gather.3.cloned.1.call-start = ((), (), s32[]{:S(2)}) async-start(), calls=%async_computation | async-start | bytes 10616832 | tf_op jit(solution)/shard_map/all_gather | solution.py:500
  13.0 51.1 %collective-permute-start = (bf16[3,128,768]{2,1,0:T(8,128)(2,1)}, bf16[3,128,768]{2,1,0:T(8,128)(2,1)S(1)}, u32[]{:S(2)}, u32[]{:S(2)}) collective-permute-start(bf16[3,128,768]{2,1,0:T(8,128)(2,1)} %get-tuple-element.44), channel_id=1, source_target_pairs={{0,1},{1,0},{2,3},{3,2},{4,5},{5,4},{6,7},{7,6},{8,9},{9,8},{10,11... | collective-permute-start | bytes 1769480 | tf_op jit(solution)/shard_map/ppermute | solution.py:443
  13.0 51.1 %collective-permute-start.1 = (bf16[3,128,768]{2,1,0:T(8,128)(2,1)}, bf16[3,128,768]{2,1,0:T(8,128)(2,1)S(1)}, u32[]{:S(2)}, u32[]{:S(2)}) collective-permute-start(bf16[3,128,768]{2,1,0:T(8,128)(2,1)} %get-tuple-element.45), channel_id=1, source_target_pairs={{0,2},{1,3},{2,0},{3,1},{4,6},{5,7},{6,4},{7,5},{8,10},{9,11},{10,... | collective-permute-start | bytes 1769480 | tf_op jit(solution)/shard_map/ppermute | solution.py:443
  15.5 57.9 %copy-start.17 = (s32[1,6,4]{1,2,0:T(4,128)S(1)}, s32[1,6,4]{1,2,0:T(4,128)}, u32[]{:S(2)}) copy-start(s32[1,6,4]{1,2,0:T(4,128)} %param.18) | copy-start | bytes 292
  15.5 58.0 %copy-start.16 = (s32[1,6,4,4]{1,3,2,0:T(4,128)S(1)}, s32[1,6,4,4]{1,3,2,0:T(4,128)}, u32[]{:S(2)}) copy-start(s32[1,6,4,4]{1,3,2,0:T(4,128)} %param.17) | copy-start | bytes 1156
  15.5 50.9 %collective-permute-start.2 = (bf16[3,128,768]{2,1,0:T(8,128)(2,1)}, bf16[3,128,768]{2,1,0:T(8,128)(2,1)}, u32[]{:S(2)}, u32[]{:S(2)}) collective-permute-start(bf16[3,128,768]{2,1,0:T(8,128)(2,1)} %get-tuple-element.46), channel_id=1, source_target_pairs={{0,3},{1,2},{2,1},{3,0},{4,7},{5,6},{6,5},{7,4},{8,11},{9,10},{10,... | collective-permute-start | bytes 1769480 | tf_op jit(solution)/shard_map/ppermute | solution.py:443
  18.3 53.6 %copy-start.8 = (bf16[128,2048]{1,0:T(8,128)(2,1)S(1)}, bf16[128,2048]{1,0:T(8,128)(2,1)}, u32[]{:S(2)}) copy-start(bf16[128,2048]{1,0:T(8,128)(2,1)} %get-tuple-element.49.a_ref.refs_0_.refs_1_) | copy-start | bytes 1572868
  18.3 53.7 %copy-start.3 = (bf16[128,2048]{1,0:T(8,128)(2,1)S(1)}, bf16[128,2048]{1,0:T(8,128)(2,1)}, u32[]{:S(2)}) copy-start(bf16[128,2048]{1,0:T(8,128)(2,1)} %get-tuple-element.52.a_ref.refs_0_.refs_1_) | copy-start | bytes 1572868
  18.3 45.9 %collective-permute-start.3 = (bf16[128,2048]{1,0:T(8,128)(2,1)}, bf16[128,2048]{1,0:T(8,128)(2,1)S(1)}, u32[]{:S(2)}, u32[]{:S(2)}) collective-permute-start(bf16[128,2048]{1,0:T(8,128)(2,1)} %get-tuple-element.47.a_ref.refs_1_.refs_0_), channel_id=1, source_target_pairs={{0,1},{1,0},{2,3},{3,2},{4,5},{5,4},{6,7},{7,6},{8,9},{9,8},{10,11... | collective-permute-start | bytes 1572872 | tf_op jit(solution)/shard_map/ppermute | solution.py:443
  64.2 2.3 copy-start.7
  64.2 2.3 copy-start.12
  64.2 2.3 copy-start.13
  68.7 31.1 %collective-permute-start.6 = (bf16[256,2048]{1,0:T(8,128)(2,1)}, bf16[256,2048]{1,0:T(8,128)(2,1)}, u32[]{:S(2)}, u32[]{:S(2)}) collective-permute-start(bf16[256,2048]{1,0:T(8,128)(2,1)} %shard_map.148.refs_4_), channel_id=1, source_target_pairs={{1,2},{2,1},{5,6},{6,5},{9,10},{10,9},{13,14},{14,13},{17,18},{18,... | collective-permute-start | bytes 3145736 | tf_op jit(solution)/shard_map/ppermute | solution.py:468
  71.9 30.1 %collective-permute-start.4 = (bf16[128,2048]{1,0:T(8,128)(2,1)S(1)}, bf16[128,2048]{1,0:T(8,128)(2,1)S(1)}, u32[]{:S(2)}, u32[]{:S(2)}) collective-permute-start(bf16[128,2048]{1,0:T(8,128)(2,1)S(1)} %copy-done.8), channel_id=1, source_target_pairs={{0,1},{1,0},{2,3},{3,2},{4,5},{5,4},{6,7},{7,6},{8,9},{9,8},{10,11... | collective-permute-start | bytes 1572872 | tf_op jit(solution)/shard_map/ppermute | solution.py:443
  72.0 22.6 %collective-permute-start.9 = (bf16[128,2048]{1,0:T(8,128)(2,1)S(1)}, bf16[128,2048]{1,0:T(8,128)(2,1)S(1)}, u32[]{:S(2)}, u32[]{:S(2)}) collective-permute-start(bf16[128,2048]{1,0:T(8,128)(2,1)S(1)} %copy-done.3), channel_id=1, source_target_pairs={{0,1},{1,0},{2,3},{3,2},{4,5},{5,4},{6,7},{7,6},{8,9},{9,8},{10,11... | collective-permute-start | bytes 1572872 | tf_op jit(solution)/shard_map/ppermute | solution.py:443
  94.7 0.8 copy-start.4
  95.4 12.9 %copy-start.19 = (s32[8]{0:T(128)S(1)}, s32[8]{0:T(128)}, u32[]{:S(2)}) copy-start(s32[8]{0:T(128)} %constant.29.clone) | copy-start | bytes 100
  97.7 23.8 %collective-permute-start.10 = (bf16[256,2048]{1,0:T(8,128)(2,1)}, bf16[256,2048]{1,0:T(8,128)(2,1)S(1)}, u32[]{:S(2)}, u32[]{:S(2)}) collective-permute-start(bf16[256,2048]{1,0:T(8,128)(2,1)} %shard_map.154), channel_id=1, source_target_pairs={{1,2},{2,1},{5,6},{6,5},{9,10},{10,9},{13,14},{14,13},{17,18},{18,... | collective-permute-start | bytes 3145736 | tf_op jit(solution)/shard_map/ppermute | solution.py:468
  99.8 23.1 %collective-permute-start.7 = (bf16[256,2048]{1,0:T(8,128)(2,1)}, bf16[256,2048]{1,0:T(8,128)(2,1)}, u32[]{:S(2)}, u32[]{:S(2)}) collective-permute-start(bf16[256,2048]{1,0:T(8,128)(2,1)} %collective-permute-done.6.refs_3_.refs_2_), channel_id=1, source_target_pairs={{1,0},{2,3},{5,4},{6,7},{9,8},{10,11},{13,12},{14,15},{17,16},{18,... | collective-permute-start | bytes 3145736 | tf_op jit(solution)/shard_map/ppermute | solution.py:471
  102.1 0.8 copy-start.9
  105.1 38.9 %collective-permute-start.5 = (bf16[256,2048]{1,0:T(8,128)(2,1)}, bf16[256,2048]{1,0:T(8,128)(2,1)S(1)}, u32[]{:S(2)}, u32[]{:S(2)}) collective-permute-start(bf16[256,2048]{1,0:T(8,128)(2,1)} %shard_map.150), channel_id=1, source_target_pairs={{1,2},{2,1},{5,6},{6,5},{9,10},{10,9},{13,14},{14,13},{17,18},{18,... | collective-permute-start | bytes 3145736 | tf_op jit(solution)/shard_map/ppermute | solution.py:468
  121.5 13.1 %copy-start.1 = (bf16[256,2048]{1,0:T(8,128)(2,1)}, bf16[256,2048]{1,0:T(8,128)(2,1)S(1)}, u32[]{:S(2)}) copy-start(bf16[256,2048]{1,0:T(8,128)(2,1)S(1)} %collective-permute-done.10.refs_2_.refs_3_) | copy-start | bytes 3145732
  121.5 25.6 %collective-permute-start.11 = (bf16[256,2048]{1,0:T(8,128)(2,1)S(1)}, bf16[256,2048]{1,0:T(8,128)(2,1)S(1)}, u32[]{:S(2)}, u32[]{:S(2)}) collective-permute-start(bf16[256,2048]{1,0:T(8,128)(2,1)S(1)} %collective-permute-done.10.refs_2_.refs_3_), channel_id=1, source_target_pairs={{1,0},{2,3},{5,4},{6,7},{9,8},{10,11},{13,12},{14,15},{17,16},{18,... | collective-permute-start | bytes 3145736 | tf_op jit(solution)/shard_map/ppermute | solution.py:471
  144.0 1.0 copy-start
  145.0 1.7 copy-start.18
  145.0 20.7 %collective-permute-start.8 = (bf16[256,2048]{1,0:T(8,128)(2,1)}, bf16[256,2048]{1,0:T(8,128)(2,1)S(1)}, u32[]{:S(2)}, u32[]{:S(2)}) collective-permute-start(bf16[256,2048]{1,0:T(8,128)(2,1)} %shard_map.153.refs_2_.refs_3_), channel_id=1, source_target_pairs={{1,0},{2,3},{5,4},{6,7},{9,8},{10,11},{13,12},{14,15},{17,16},{18,... | collective-permute-start | bytes 3145736 | tf_op jit(solution)/shard_map/ppermute | solution.py:471
  147.2 1.0 copy-start.2
  165.7 1.0 copy-start.10
  172.6 11.7 %collective-permute-start.12 = (bf16[4,768,384]{2,1,0:T(8,128)(2,1)}, bf16[4,768,384]{2,1,0:T(8,128)(2,1)S(1)}, u32[]{:S(2)}, u32[]{:S(2)}) collective-permute-start(bf16[4,768,384]{2,1,0:T(8,128)(2,1)} %get-tuple-element.65), channel_id=1, source_target_pairs={{0,4},{4,0},{8,12},{12,8},{16,20},{20,16},{24,28},{28,24},{1,5},{5... | collective-permute-start | bytes 7077896 | tf_op jit(solution)/shard_map/ppermute | solution.py:443
  177.0 7.9 %collective-permute-start.13 = (bf16[4,768,384]{2,1,0:T(8,128)(2,1)}, bf16[4,768,384]{2,1,0:T(8,128)(2,1)}, u32[]{:S(2)}, u32[]{:S(2)}) collective-permute-start(bf16[4,768,384]{2,1,0:T(8,128)(2,1)} %get-tuple-element.66), channel_id=1, source_target_pairs={{0,4},{4,0},{8,12},{12,8},{16,20},{20,16},{24,28},{28,24},{1,5},{5... | collective-permute-start | bytes 7077896 | tf_op jit(solution)/shard_map/ppermute | solution.py:443
  184.3 1.4 copy-start.11
  198.0 27.5 %collective-permute-start.19 = (bf16[2,768,384]{2,1,0:T(8,128)(2,1)}, bf16[2,768,384]{2,1,0:T(8,128)(2,1)S(1)}, u32[]{:S(2)}, u32[]{:S(2)}) collective-permute-start(bf16[2,768,384]{2,1,0:T(8,128)(2,1)} %get-tuple-element.80), channel_id=1, source_target_pairs={{0,16},{4,20},{8,24},{12,28},{16,0},{20,4},{24,8},{28,12},{1,17},{... | collective-permute-start | bytes 3538952 | tf_op jit(solution)/shard_map/ppermute | solution.py:443
  199.3 29.2 %collective-permute-start.17 = (bf16[2,768,384]{2,1,0:T(8,128)(2,1)}, bf16[2,768,384]{2,1,0:T(8,128)(2,1)S(1)}, u32[]{:S(2)}, u32[]{:S(2)}) collective-permute-start(bf16[2,768,384]{2,1,0:T(8,128)(2,1)} %get-tuple-element.78), channel_id=1, source_target_pairs={{0,8},{4,12},{8,0},{12,4},{16,24},{20,28},{24,16},{28,20},{1,9},{5... | collective-permute-start | bytes 3538952 | tf_op jit(solution)/shard_map/ppermute | solution.py:443
  200.6 44.4 %collective-permute-start.14 = (bf16[3,128,768]{2,1,0:T(8,128)(2,1)}, bf16[3,128,768]{2,1,0:T(8,128)(2,1)}, u32[]{:S(2)}, u32[]{:S(2)}) collective-permute-start(bf16[3,128,768]{2,1,0:T(8,128)(2,1)} %get-tuple-element.67), channel_id=1, source_target_pairs={{0,2},{1,3},{2,0},{3,1},{4,6},{5,7},{6,4},{7,5},{8,10},{9,11},{10,... | collective-permute-start | bytes 1769480 | tf_op jit(solution)/shard_map/ppermute | solution.py:443
  203.3 52.1 %collective-permute-start.15 = (bf16[3,128,768]{2,1,0:T(8,128)(2,1)}, bf16[3,128,768]{2,1,0:T(8,128)(2,1)}, u32[]{:S(2)}, u32[]{:S(2)}) collective-permute-start(bf16[3,128,768]{2,1,0:T(8,128)(2,1)} %get-tuple-element.68), channel_id=1, source_target_pairs={{0,3},{1,2},{2,1},{3,0},{4,7},{5,6},{6,5},{7,4},{8,11},{9,10},{10,... | collective-permute-start | bytes 1769480 | tf_op jit(solution)/shard_map/ppermute | solution.py:443
  203.8 37.0 %collective-permute-start.16 = (bf16[3,128,768]{2,1,0:T(8,128)(2,1)}, bf16[3,128,768]{2,1,0:T(8,128)(2,1)S(1)}, u32[]{:S(2)}, u32[]{:S(2)}) collective-permute-start(bf16[3,128,768]{2,1,0:T(8,128)(2,1)} %get-tuple-element.70), channel_id=1, source_target_pairs={{0,1},{1,0},{2,3},{3,2},{4,5},{5,4},{6,7},{7,6},{8,9},{9,8},{10,11... | collective-permute-start | bytes 1769480 | tf_op jit(solution)/shard_map/ppermute | solution.py:443
  225.5 3.0 %copy-start.14 = (bf16[2,768,384]{2,1,0:T(8,128)(2,1)S(1)}, bf16[2,768,384]{2,1,0:T(8,128)(2,1)}, u32[]{:S(2)}) copy-start(bf16[2,768,384]{2,1,0:T(8,128)(2,1)} %get-tuple-element.77) | copy-start | bytes 3538948
  227.2 31.2 %collective-permute-start.20 = (bf16[1,768,384]{2,1,0:T(8,128)(2,1)S(1)}, bf16[1,768,384]{2,1,0:T(8,128)(2,1)}, u32[]{:S(2)}, u32[]{:S(2)}) collective-permute-start(bf16[1,768,384]{2,1,0:T(8,128)(2,1)S(1)} %slice.44), channel_id=1, source_target_pairs={{0,8},{4,12},{8,0},{12,4},{16,24},{20,28},{24,16},{28,20},{1,9},{5... | collective-permute-start | bytes 1769480 | tf_op jit(solution)/shard_map/ppermute | solution.py:443
  228.8 1.4 copy-start.5
  230.2 29.5 %collective-permute-start.18 = (bf16[1,768,384]{2,1,0:T(8,128)(2,1)S(1)}, bf16[1,768,384]{2,1,0:T(8,128)(2,1)}, u32[]{:S(2)}, u32[]{:S(2)}) collective-permute-start(bf16[1,768,384]{2,1,0:T(8,128)(2,1)S(1)} %slice.45), channel_id=1, source_target_pairs={{0,16},{4,20},{8,24},{12,28},{16,0},{20,4},{24,8},{28,12},{1,17},{... | collective-permute-start | bytes 1769480 | tf_op jit(solution)/shard_map/ppermute | solution.py:443
  240.8 0.8 copy-start.15
  258.4 1.8 copy-start.6
Sparse Core Ops, SparseCore 0:
  9.9 60.4 all-gather.2

commit v3 on v2

--- a/solution.py
+++ b/solution.py
@@ -42,7 +42,7 @@
     return lax.dot_general(a, b, dims, preferred_element_type=F32)
 
 
-def params(limit_mib=60):
+def params(limit_mib=20):
     return pltpu.CompilerParams(vmem_limit_bytes=limit_mib * 1024 * 1024)
 
 
@@ -70,27 +70,27 @@
             out[i] = ins[3 * s + i][0]
 
 
-def pack(table, q, k, v, after=()):
+def pack(table, partners, q, k, v, after=()):
     group = table.shape[0] // 3
     rows, total = q.shape[1:]
     shape = (3, rows, total // group)
     in_specs = []
-    for s in range(group):
+    for s in partners:
         in_specs += [
             pl.BlockSpec((1, rows, total // group), lambda i, t, s=s: (0, 0, t[s]))
         ] * 3
     return pl.pallas_call(
-        functools.partial(pack_kernel, group),
-        out_shape=[jax.ShapeDtypeStruct(shape, BF16)] * group,
+        functools.partial(pack_kernel, len(partners)),
+        out_shape=[jax.ShapeDtypeStruct(shape, BF16)] * len(partners),
         grid_spec=pltpu.PrefetchScalarGridSpec(
             num_scalar_prefetch=1,
             grid=(1,),
             in_specs=in_specs + awaited(after),
-            out_specs=[whole(shape)] * group,
-        ),
-        cost_estimate=light(),
-        compiler_params=params(),
-    )(table, *[q, k, v] * group, *after)
+            out_specs=[whole(shape)] * len(partners),
+        ),
+        cost_estimate=light(),
+        compiler_params=params(),
+    )(table, *[q, k, v] * len(partners), *after)
 
 
 def split_kernel(dp, g_ref, *outs):
@@ -457,8 +457,7 @@
     kept = kept.astype(F32) + swap(send, "dp", dp, masks[0]).astype(F32)
     half = kept.shape[0] // 2
     if half == 0:
-        kept = kept[0].astype(BF16)
-        return kept, kept, masks[1:]
+        return kept[0], kept[0], masks[1:]
     return kept[:half], kept[half:].astype(BF16), masks[1:]
 
 
@@ -492,8 +491,10 @@
     def blocks(order):
         return jnp.bitwise_xor(lax.axis_index("dp"), jnp.array(half_order(order), jnp.int32))
 
-    packed = pack(table, query_rows, key_rows, value_rows)
-    parts = [packed[0]] + [swap(packed[s], "head", group, s) for s in range(1, group)]
+    arrays = (query_rows, key_rows, value_rows)
+    packed = pack(table, range(1, group), *arrays)
+    parts = [swap(rows, "head", group, 1 + i) for i, rows in enumerate(packed)]
+    parts = list(pack(table, [0], *arrays, after=parts[:1])) + parts
     pieces = split(out_grad, dp)
     nears = [swap(own, "head", group, 1) for own in pieces] if group == 4 else pieces
     both = join(pieces[0], nears[0], after=parts[1:])
@@ -535,7 +536,7 @@
         states = [fold(state, dp) for state in states]
     back = [back[0]] + [swap(back[s], "head", group, s) for s in range(1, group)]
     low, high = [kept for kept, _, _ in states]
-    total = jnp.concatenate([low, high[:, part:], high[:, :part]], axis=1)
+    total = jnp.concatenate([low, high[:, part:], high[:, :part]], axis=1).astype(BF16)
     query_back, key_back, value_back = unpack(table, back)
     return (att[None], query_back, key_back, value_back, total)
 

time: 270 us -> 256 us (0.948)
  Pallas kernels: 82.4 us -> 54.5 us
  local copies, waits for them, and re-layouts: 9.31 us -> 19.6 us
  waiting for transfers between devices: 123 us -> 129 us
  other arithmetic: 8.09 us -> 2.88 us
    unnamed x40 -> x84, local copies, waits for them, and re-layouts: 8.23 us -> 19.2 us
    ppermute x15, waiting for transfers between devices: 100 us -> 108 us  [swap(): return lax.ppermute(value, axis, [(i, i ^ mask) for i in range(size)])]
    pallas_call x3, Pallas kernels: 18.3 us -> 10.8 us  [project(): pl.pallas_call(functools.partial(project_kernel, len(rows), len(at), not...]
    ppermute x3, waiting for transfers between devices: 22.1 us -> 15.3 us  [gather_rows(): lax.ppermute(join(own, near) if both is None else both, 'head', [(1, 2),...]
    pallas_call x4, Pallas kernels: 22.8 us -> 16.6 us  [outer(): pl.pallas_call(functools.partial(outer_kernel, len(rows), start, len(pass...]
    ppermute x3, waiting for transfers between devices: 0.01 us -> 4.95 us  [gather_rows(): outer = lax.ppermute(inner, 'head', [(1, 0), (2, 3)])]
    pallas_call x1, Pallas kernels: 12.3 us -> 8.39 us  [backward(): pl.pallas_call(functools.partial(backward_kernel, group, len(sums)), out_...]
  transfers between devices with their start and end apart: 22 -> 22, of which waited for: 10 -> 11; matrix products, arithmetic and copies ran while one was open for 3% -> 1% of each run, Pallas kernels for 24% -> 17%
where the time goes in v3:
time: 256 us; the launch traced here: 255 us
  waiting for transfers between devices  129 us (50%)
  Pallas kernels  54.5 us (21%)
  starting transfers between devices  34.8 us (14%)
  local copies, waits for them, and re-layouts  19.6 us (8%)
  between operations  14.5 us (6%)
  other arithmetic  2.88 us (1%)
    ppermute x15, waiting for transfers between devices, swap(): return lax.ppermute(value, axis, [(i, i ^ mask) for i in range(size)])  108 us
    ppermute x15, starting transfers between devices, swap(): return lax.ppermute(value, axis, [(i, i ^ mask) for i in range(size)])  20.7 us
    unnamed x84, local copies, waits for them, and re-layouts  19.2 us
    pallas_call x4, Pallas kernels, outer(): pl.pallas_call(functools.partial(outer_kernel, len(rows), start, len(pass...  16.6 us
    ppermute x3, waiting for transfers between devices, gather_rows(): lax.ppermute(join(own, near) if both is None else both, 'head', [(1, 2),...  15.3 us
    pallas_call x3, Pallas kernels, project(): pl.pallas_call(functools.partial(project_kernel, len(rows), len(at), not...  10.8 us
    pallas_call x1, Pallas kernels, backward(): pl.pallas_call(functools.partial(backward_kernel, group, len(sums)), out_...  8.39 us
    ppermute x3, starting transfers between devices, gather_rows(): lax.ppermute(join(own, near) if both is None else both, 'head', [(1, 2),...  8.16 us
  transfers between devices with their start and end apart: 22, of which 11 were waited for; matrix products, arithmetic and copies ran while one was open for 1% of the time, Pallas kernels for 17%

profile of v3, /device:TPU:9, one launch (start us, length us, event | category | flops | bytes accessed | tf_op | source)
XLA Modules:
  0.0 254.9 jit_solution(16331456133245259547)
XLA Ops:
  8.7 1.1 copy-done.1
  9.8 1.1 copy-done.3
  10.9 1.1 copy-done.5
  12.8 2.5 collective-permute-start.1
  15.5 1.1 shard_map.148
  17.6 46.1 %collective-permute-done.3.b_ref.refs_2_.refs_1_ = bf16[128,2048]{1,0:T(8,128)(2,1)S(1)} collective-permute-done((bf16[128,2048]{1,0:T(8,128)(2,1)S(1)}, bf16[128,2048]{1,0:T(8,128)(2,1)S(1)}, u32[]{:S(2)}, u32[]{:S(2)}) %collective-permute-start.3) | collective-permute-done | bytes 524320 | tf_op jit(solution)/shard_map/ppermute | solution.py:443
  63.7 2.3 collective-permute-done.2.refs_2_.refs_3_
  66.0 1.1 shard_map.149.refs_4_
  67.9 3.3 %collective-permute-start.6 = (bf16[256,2048]{1,0:T(8,128)(2,1)}, bf16[256,2048]{1,0:T(8,128)(2,1)}, u32[]{:S(2)}, u32[]{:S(2)}) collective-permute-start(bf16[256,2048]{1,0:T(8,128)(2,1)} %shard_map.149.refs_4_), channel_id=1, source_target_pairs={{1,2},{2,1},{5,6},{6,5},{9,10},{10,9},{13,14},{14,13},{17,18},{18,... | collective-permute-start | bytes 3145736 | tf_op jit(solution)/shard_map/ppermute | solution.py:467
  71.4 1.5 collective-permute-start.9
  74.3 1.1 copy-done.10
  75.3 7.9 %shard_map.150 = (bf16[512,768]{1,0:T(8,128)(2,1)}, bf16[768,512]{1,0:T(8,128)(2,1)S(1)}, bf16[6,512,512]{2,1,0:T(8,128)(2,1)S(1)}, bf16[768,512]{1,0:T(8,128)(2...) custom-call(s32[12]{0:T(128)S(1)} %pad_add_fusion.table.place, s32[1,512]{1,0:T(1,128)S(1)} %copy-done.34, ...), custom_call_target="tpu_custom_call" | custom-call | flops 1 | bytes 1 | tf_op jit(solution)/shard_map/pallas_call | solution.py:251
  84.1 10.2 %collective-permute-done.9.b_ref.refs_1_.refs_2_ = bf16[128,2048]{1,0:T(8,128)(2,1)} collective-permute-done((bf16[128,2048]{1,0:T(8,128)(2,1)}, bf16[128,2048]{1,0:T(8,128)(2,1)}, u32[]{:S(2)}, u32[]{:S(2)}) %collective-permute-start.9) | collective-permute-done | bytes 524320 | tf_op jit(solution)/shard_map/ppermute | solution.py:443
  94.3 1.3 shard_map.155
  95.6 2.1 collective-permute-start.10
  97.7 1.8 collective-permute-start.7
  99.5 2.2 shard_map.151
  101.8 2.8 %collective-permute-start.5 = (bf16[256,2048]{1,0:T(8,128)(2,1)}, bf16[256,2048]{1,0:T(8,128)(2,1)}, u32[]{:S(2)}, u32[]{:S(2)}) collective-permute-start(bf16[256,2048]{1,0:T(8,128)(2,1)} %shard_map.151), channel_id=1, source_target_pairs={{1,2},{2,1},{5,6},{6,5},{9,10},{10,9},{13,14},{14,13},{17,18},{18,... | collective-permute-start | bytes 3145736 | tf_op jit(solution)/shard_map/ppermute | solution.py:467
  104.6 14.8 %collective-permute-done.10.refs_2_.refs_3_ = bf16[256,2048]{1,0:T(8,128)(2,1)} collective-permute-done((bf16[256,2048]{1,0:T(8,128)(2,1)S(1)}, bf16[256,2048]{1,0:T(8,128)(2,1)}, u32[]{:S(2)}, u32[]{:S(2)}) %collective-permute-start.10) | collective-permute-done | bytes 1048608 | tf_op jit(solution)/shard_map/ppermute | solution.py:467
  119.3 2.3 collective-permute-start.11
  122.6 1.0 copy-done.12
  124.7 1.2 copy-done.18
  125.9 3.6 %shard_map.153 = (bf16[4,768,384]{2,1,0:T(8,128)(2,1)S(1)}, bf16[4,768,384]{2,1,0:T(8,128)(2,1)S(1)}) custom-call(s32[8]{0:T(128)S(1)} %broadcast_xor_fusion.1.blocks, bf16[768,512]{1,0:T(8,128)(2,1)S(1)} %get-tuple-element.48.att_t_ref.refs_0_, bf16[128,2048]{1,0:T(8,128)(2,1)S(1)} %copy-done.12, bf16[128,2048]{1,0:T(8,128)(2,1)S(1)} %copy-done.15, ...), custom_call_target="tpu_custom_call" | custom-call | flops 1 | bytes 1 | tf_op jit(solution)/shard_map/pallas_call | solution.py:426
  129.5 1.4 copy-done.7
  130.9 3.7 %copy-done = bf16[6144,768]{1,0:T(8,128)(2,1)S(1)} copy-done((bf16[6144,768]{1,0:T(8,128)(2,1)S(1)}, bf16[6144,768]{1,0:T(8,128)(2,1)}, u32[]{:S(2)}) %copy-start) | copy-done | bytes 9437208
  136.7 1.2 copy-done.19
  137.9 3.4 %shard_map.152.refs_1_.refs_5_ = f32[512,768]{1,0:T(8,128)S(1)} custom-call(bf16[8,768,768]{2,1,0:T(8,128)(2,1)S(1)} %bitcast.8, bf16[128,2048]{1,0:T(8,128)(2,1)S(1)} %copy-done.13, bf16[128,2048]{1,0:T(8,128)(2,1)S(1)} %copy-done.16, bf16[256,2048]{1,0:T(8,128)(2,1)} %collective-permute-done.6.refs_3_.refs_2_, bf16[256,2048]{1,0:T(8,128)(2,1)S(1)} %copy-done.19), custom_call_target="tpu_custom_call" | custom-call | flops 1 | bytes 1 | tf_op jit(solution)/shard_map/pallas_call | solution.py:392
  141.8 1.9 collective-permute-start.8
  143.7 4.6 %shard_map.156 = (bf16[4,768,384]{2,1,0:T(8,128)(2,1)S(1)}, bf16[4,768,384]{2,1,0:T(8,128)(2,1)S(1)}) custom-call(s32[8]{0:T(128)S(1)} %broadcast_xor_fusion.blocks, bf16[768,512]{1,0:T(8,128)(2,1)S(1)} %get-tuple-element.48.att_t_ref.refs_0_, bf16[128,2048]{1,0:T(8,128)(2,1)} %get-tuple-element.50.a_ref.refs_0_.refs_1_, ...), custom_call_target="tpu_custom_call" | custom-call | flops 1 | bytes 1 | tf_op jit(solution)/shard_map/pallas_call | solution.py:426
  148.3 3.9 %shard_map.158.refs_8_ = f32[512,768]{1,0:T(8,128)S(1)} custom-call(bf16[8,768,768]{2,1,0:T(8,128)(2,1)S(1)} %bitcast.11, bf16[128,2048]{1,0:T(8,128)(2,1)} %get-tuple-element.50.a_ref.refs_0_.refs_1_, bf16[128,2048]{1,0:T(8,128)(2,1)} %collective-permute-done.9.b_ref.refs_1_.refs_2_, bf16[256,2048]{1,0:T(8,128)(2,1)} %collective-permute-done.10.refs_2_.refs_3_, ...), custom_call_target="tpu_custom_call" | custom-call | flops 1 | bytes 1 | tf_op jit(solution)/shard_map/pallas_call | solution.py:392
  152.2 4.6 %shard_map.157 = (bf16[4,768,384]{2,1,0:T(8,128)(2,1)S(1)}, bf16[4,768,384]{2,1,0:T(8,128)(2,1)S(1)}) custom-call(s32[8]{0:T(128)S(1)} %broadcast_xor_fusion.1.blocks, bf16[768,512]{1,0:T(8,128)(2,1)S(1)} %get-tuple-element.48.att_t_ref.refs_0_, ...), custom_call_target="tpu_custom_call", output_to_operand_aliasing={{0}: (6, {}), {1}: (7, {})} | custom-call | flops 1 | bytes 1 | tf_op jit(solution)/shard_map/pallas_call | solution.py:426
  156.8 4.9 %collective-permute-done.8.refs_3_.refs_4_ = bf16[256,2048]{1,0:T(8,128)(2,1)S(1)} collective-permute-done((bf16[256,2048]{1,0:T(8,128)(2,1)}, bf16[256,2048]{1,0:T(8,128)(2,1)S(1)}, u32[]{:S(2)}, u32[]{:S(2)}) %collective-permute-start.8) | collective-permute-done | bytes 1048608 | tf_op jit(solution)/shard_map/ppermute | solution.py:470
  161.7 3.9 %shard_map.159 = (bf16[4,768,384]{2,1,0:T(8,128)(2,1)S(1)}, bf16[4,768,384]{2,1,0:T(8,128)(2,1)S(1)}, bf16[4,768,384]{2,1,0:T(8,128)(2,1)S(1)}, bf16[4,768,384]{2,1,0:T(8,128)(2,1)S(1)}, f32[512,768]{1,0:T(8,128)S(1)}) custom-call(s32[8]{0:T(128)S(1)} %broadcast_xor_fusion.blocks, ...), custom_call_target="tpu_custom_call", output_to_operand_aliasing={{0}: (6, {}), {1}: (7, {}), {2}: (8, {}), {3}: (9, {}), {4}... | custom-call | flops 1 | bytes 1 | tf_op jit(solution)/shard_map/pallas_call | solution.py:426
  165.7 6.4 %collective-permute-start.12 = (bf16[4,768,384]{2,1,0:T(8,128)(2,1)S(1)}, bf16[4,768,384]{2,1,0:T(8,128)(2,1)S(1)}, u32[]{:S(2)}, u32[]{:S(2)}) collective-permute-start(bf16[4,768,384]{2,1,0:T(8,128)(2,1)S(1)} %get-tuple-element.63), channel_id=1, source_target_pairs={{0,4},{4,0},{8,12},{12,8},{16,20},{20,16},{24,28},{28,24},{1,5},{5... | collective-permute-start | bytes 7077896 | tf_op jit(solution)/shard_map/ppermute | solution.py:443
  172.1 3.6 %shard_map.160.g_ref = bf16[512,768]{1,0:T(8,128)(2,1)S(1)} custom-call(bf16[8,768,768]{2,1,0:T(8,128)(2,1)S(1)} %bitcast.12, bf16[128,2048]{1,0:T(8,128)(2,1)} %get-tuple-element.47.a_ref.refs_0_.refs_1_, bf16[128,2048]{1,0:T(8,128)(2,1)} %collective-permute-done.4.b_ref.refs_1_.refs_2_, bf16[256,2048]{1,0:T(8,128)(2,1)} %shard_map.154.refs_2_.refs_3_, ...), custom_call_target="tpu_custom_call" | custom-call | flops 1 | bytes 1 | tf_op jit(solution)/shard_map/pallas_call | solution.py:392
  176.2 3.4 %collective-permute-done.13.refs_3_ = bf16[4,768,384]{2,1,0:T(8,128)(2,1)S(1)} collective-permute-done((bf16[4,768,384]{2,1,0:T(8,128)(2,1)S(1)}, bf16[4,768,384]{2,1,0:T(8,128)(2,1)S(1)}, u32[]{:S(2)}, u32[]{:S(2)}) %collective-permute-start.13) | collective-permute-done | bytes 2359328 | tf_op jit(solution)/shard_map/ppermute | solution.py:443
  179.6 8.4 %shard_map.161 = (bf16[3,128,768]{2,1,0:T(8,128)(2,1)S(1)}, bf16[3,128,768]{2,1,0:T(8,128)(2,1)S(1)}, bf16[3,128,768]{2,1,0:T(8,128)(2,1)S(1)}, bf16[3,128,768]{...) custom-call(s32[12]{0:T(128)S(1)} %pad_add_fusion.table.place, ...), custom_call_target="tpu_custom_call" | custom-call | flops 1 | bytes 1 | tf_op jit(solution)/shard_map/pallas_call | solution.py:333
  188.0 1.3 collective-permute-start.19
  189.3 1.2 collective-permute-start.17
  190.5 2.7 %collective-permute-start.14 = (bf16[3,128,768]{2,1,0:T(8,128)(2,1)S(1)}, bf16[3,128,768]{2,1,0:T(8,128)(2,1)S(1)}, u32[]{:S(2)}, u32[]{:S(2)}) collective-permute-start(bf16[3,128,768]{2,1,0:T(8,128)(2,1)S(1)} %get-tuple-element.65), channel_id=1, source_target_pairs={{0,2},{1,3},{2,0},{3,1},{4,6},{5,7},{6,4},{7,5},{8,10},{9,11},{10,... | collective-permute-start | bytes 1769480 | tf_op jit(solution)/shard_map/ppermute | solution.py:443
  194.4 20.9 %collective-permute-done.19 = bf16[2,768,384]{2,1,0:T(8,128)(2,1)S(1)} collective-permute-done((bf16[2,768,384]{2,1,0:T(8,128)(2,1)S(1)}, bf16[2,768,384]{2,1,0:T(8,128)(2,1)S(1)}, u32[]{:S(2)}, u32[]{:S(2)}) %collective-permute-start.19) | collective-permute-done | bytes 1179680 | tf_op jit(solution)/shard_map/ppermute | solution.py:443
  215.6 1.3 collective-permute-start.20
  217.2 1.3 collective-permute-start.18
  218.5 12.0 %collective-permute-done.16.refs_1_ = bf16[3,128,768]{2,1,0:T(8,128)(2,1)S(1)} collective-permute-done((bf16[3,128,768]{2,1,0:T(8,128)(2,1)S(1)}, bf16[3,128,768]{2,1,0:T(8,128)(2,1)S(1)}, u32[]{:S(2)}, u32[]{:S(2)}) %collective-permute-start.16) | collective-permute-done | bytes 589856 | tf_op jit(solution)/shard_map/ppermute | solution.py:443
  230.5 2.0 shard_map.162
  232.5 12.4 %collective-permute-done.15.refs_1_ = bf16[3,128,768]{2,1,0:T(8,128)(2,1)S(1)} collective-permute-done((bf16[3,128,768]{2,1,0:T(8,128)(2,1)S(1)}, bf16[3,128,768]{2,1,0:T(8,128)(2,1)S(1)}, u32[]{:S(2)}, u32[]{:S(2)}) %collective-permute-start.15) | collective-permute-done | bytes 589856 | tf_op jit(solution)/shard_map/ppermute | solution.py:443
  244.9 1.7 shard_map.163
  246.9 1.1 pad_maximum_fusion
  (120 shorter events, 14.0 us)
Async XLA Ops:
  7.2 123.7 %all-gather.3.cloned.1.call-start = ((), (), s32[]{:S(2)}) async-start(), calls=%async_computation | async-start | bytes 10616832 | tf_op jit(solution)/shard_map/all_gather | solution.py:501
  12.1 3.4 %copy-start.26 = (bf16[1,128,6144]{2,1,0:T(8,128)(2,1)S(1)}, bf16[1,128,6144]{2,1,0:T(8,128)(2,1)}, u32[]{:S(2)}) copy-start(bf16[1,128,6144]{2,1,0:T(8,128)(2,1)} %g_ref.1) | copy-start | bytes 4718596
  12.7 51.0 %collective-permute-start = (bf16[3,128,768]{2,1,0:T(8,128)(2,1)S(1)}, bf16[3,128,768]{2,1,0:T(8,128)(2,1)S(1)}, u32[]{:S(2)}, u32[]{:S(2)}) collective-permute-start(bf16[3,128,768]{2,1,0:T(8,128)(2,1)S(1)} %get-tuple-element.42), channel_id=1, source_target_pairs={{0,1},{1,0},{2,3},{3,2},{4,5},{5,4},{6,7},{7,6},{8,9},{9,8},{10,11... | collective-permute-start | bytes 1769480 | tf_op jit(solution)/shard_map/ppermute | solution.py:443
  12.8 50.9 %collective-permute-start.1 = (bf16[3,128,768]{2,1,0:T(8,128)(2,1)S(1)}, bf16[3,128,768]{2,1,0:T(8,128)(2,1)S(1)}, u32[]{:S(2)}, u32[]{:S(2)}) collective-permute-start(bf16[3,128,768]{2,1,0:T(8,128)(2,1)S(1)} %get-tuple-element.43), channel_id=1, source_target_pairs={{0,2},{1,3},{2,0},{3,1},{4,6},{5,7},{6,4},{7,5},{8,10},{9,11},{10,... | collective-permute-start | bytes 1769480 | tf_op jit(solution)/shard_map/ppermute | solution.py:443
  15.3 57.5 %copy-start.36 = (s32[1,6,4]{1,2,0:T(4,128)S(1)}, s32[1,6,4]{1,2,0:T(4,128)}, u32[]{:S(2)}) copy-start(s32[1,6,4]{1,2,0:T(4,128)} %param.18) | copy-start | bytes 292
  15.3 57.6 %copy-start.35 = (s32[1,6,4,4]{1,3,2,0:T(4,128)S(1)}, s32[1,6,4,4]{1,3,2,0:T(4,128)}, u32[]{:S(2)}) copy-start(s32[1,6,4,4]{1,3,2,0:T(4,128)} %param.17) | copy-start | bytes 1156
  15.3 50.7 %collective-permute-start.2 = (bf16[3,128,768]{2,1,0:T(8,128)(2,1)S(1)}, bf16[3,128,768]{2,1,0:T(8,128)(2,1)S(1)}, u32[]{:S(2)}, u32[]{:S(2)}) collective-permute-start(bf16[3,128,768]{2,1,0:T(8,128)(2,1)S(1)} %get-tuple-element.44), channel_id=1, source_target_pairs={{0,3},{1,2},{2,1},{3,0},{4,7},{5,6},{6,5},{7,4},{8,11},{9,10},{10,... | collective-permute-start | bytes 1769480 | tf_op jit(solution)/shard_map/ppermute | solution.py:443
  16.6 56.7 %copy-start.2 = (bf16[1,128,3072]{2,1,0:T(8,128)(2,1)S(1)}, bf16[1,128,3072]{2,1,0:T(8,128)(2,1)}, u32[]{:S(2)}) copy-start(bf16[1,128,3072]{2,1,0:T(8,128)(2,1)} %refs_0_.3) | copy-start | bytes 2359300
  16.6 56.7 %copy-start.4 = (bf16[1,128,3072]{2,1,0:T(8,128)(2,1)S(1)}, bf16[1,128,3072]{2,1,0:T(8,128)(2,1)}, u32[]{:S(2)}) copy-start(bf16[1,128,3072]{2,1,0:T(8,128)(2,1)} %refs_1_.3) | copy-start | bytes 2359300
  16.6 56.7 %copy-start.6 = (bf16[1,128,3072]{2,1,0:T(8,128)(2,1)S(1)}, bf16[1,128,3072]{2,1,0:T(8,128)(2,1)}, u32[]{:S(2)}) copy-start(bf16[1,128,3072]{2,1,0:T(8,128)(2,1)} %refs_2_.3) | copy-start | bytes 2359300
  16.6 47.1 %collective-permute-start.3 = (bf16[128,2048]{1,0:T(8,128)(2,1)S(1)}, bf16[128,2048]{1,0:T(8,128)(2,1)S(1)}, u32[]{:S(2)}, u32[]{:S(2)}) collective-permute-start(bf16[128,2048]{1,0:T(8,128)(2,1)S(1)} %get-tuple-element.45.a_ref.refs_1_.refs_0_), channel_id=1, source_target_pairs={{0,1},{1,0},{2,3},{3,2},{4,5},{5,4},{6,7},{7,6},{8,9},{9,8},{10,11... | collective-permute-start | bytes 1572872 | tf_op jit(solution)/shard_map/ppermute | solution.py:443
  63.7 3.4 %copy-start.14 = (bf16[128,2048]{1,0:T(8,128)(2,1)}, bf16[128,2048]{1,0:T(8,128)(2,1)S(1)}, u32[]{:S(2)}) copy-start(bf16[128,2048]{1,0:T(8,128)(2,1)S(1)} %collective-permute-done.3.b_ref.refs_2_.refs_1_) | copy-start | bytes 1572868
  63.7 9.6 %copy-start.9 = (bf16[3,128,768]{2,1,0:T(8,128)(2,1)}, bf16[3,128,768]{2,1,0:T(8,128)(2,1)S(1)}, u32[]{:S(2)}) copy-start(bf16[3,128,768]{2,1,0:T(8,128)(2,1)S(1)} %collective-permute-done.refs_3_.refs_0_.refs_1_) | copy-start | bytes 1769476
  63.7 7.5 %copy-start.22 = (bf16[3,128,768]{2,1,0:T(8,128)(2,1)}, bf16[3,128,768]{2,1,0:T(8,128)(2,1)S(1)}, u32[]{:S(2)}) copy-start(bf16[3,128,768]{2,1,0:T(8,128)(2,1)S(1)} %collective-permute-done.1.refs_1_.refs_2_) | copy-start | bytes 1769476
  66.0 5.3 %copy-start.24 = (bf16[3,128,768]{2,1,0:T(8,128)(2,1)}, bf16[3,128,768]{2,1,0:T(8,128)(2,1)S(1)}, u32[]{:S(2)}) copy-start(bf16[3,128,768]{2,1,0:T(8,128)(2,1)S(1)} %collective-permute-done.2.refs_2_.refs_3_) | copy-start | bytes 1769476
  67.9 6.0 %copy-start.34 = (s32[1,512]{1,0:T(1,128)S(1)}, s32[1,512]{1,0:T(1,128)}, u32[]{:S(2)}) copy-start(s32[1,512]{1,0:T(1,128)} %order_ref.1) | copy-start | bytes 6148
  67.9 29.8 %collective-permute-start.6 = (bf16[256,2048]{1,0:T(8,128)(2,1)}, bf16[256,2048]{1,0:T(8,128)(2,1)}, u32[]{:S(2)}, u32[]{:S(2)}) collective-permute-start(bf16[256,2048]{1,0:T(8,128)(2,1)} %shard_map.149.refs_4_), channel_id=1, source_target_pairs={{1,2},{2,1},{5,6},{6,5},{9,10},{10,9},{13,14},{14,13},{17,18},{18,... | collective-permute-start | bytes 3145736 | tf_op jit(solution)/shard_map/ppermute | solution.py:467
  71.3 28.2 %collective-permute-start.4 = (bf16[128,2048]{1,0:T(8,128)(2,1)}, bf16[128,2048]{1,0:T(8,128)(2,1)}, u32[]{:S(2)}, u32[]{:S(2)}) collective-permute-start(bf16[128,2048]{1,0:T(8,128)(2,1)} %get-tuple-element.47.a_ref.refs_0_.refs_1_), channel_id=1, source_target_pairs={{0,1},{1,0},{2,3},{3,2},{4,5},{5,4},{6,7},{7,6},{8,9},{9,8},{10,11... | collective-permute-start | bytes 1572872 | tf_op jit(solution)/shard_map/ppermute | solution.py:443
  71.4 23.0 %collective-permute-start.9 = (bf16[128,2048]{1,0:T(8,128)(2,1)}, bf16[128,2048]{1,0:T(8,128)(2,1)}, u32[]{:S(2)}, u32[]{:S(2)}) collective-permute-start(bf16[128,2048]{1,0:T(8,128)(2,1)} %get-tuple-element.50.a_ref.refs_0_.refs_1_), channel_id=1, source_target_pairs={{0,1},{1,0},{2,3},{3,2},{4,5},{5,4},{6,7},{7,6},{8,9},{9,8},{10,11... | collective-permute-start | bytes 1572872 | tf_op jit(solution)/shard_map/ppermute | solution.py:443
  84.1 17.6 %copy-start.20 = (bf16[6,512,512]{2,1,0:T(8,128)(2,1)}, bf16[6,512,512]{2,1,0:T(8,128)(2,1)S(1)}, u32[]{:S(2)}) copy-start(bf16[6,512,512]{2,1,0:T(8,128)(2,1)S(1)} %get-tuple-element.59.weight_ref) | copy-start | bytes 9437188
  84.1 17.6 %copy-start.28 = (bf16[768,512]{1,0:T(8,128)(2,1)}, bf16[768,512]{1,0:T(8,128)(2,1)S(1)}, u32[]{:S(2)}) copy-start(bf16[768,512]{1,0:T(8,128)(2,1)S(1)} %get-tuple-element.60.q_t_ref) | copy-start | bytes 2359300
  84.1 17.6 %copy-start.30 = (bf16[512,768]{1,0:T(8,128)(2,1)}, bf16[512,768]{1,0:T(8,128)(2,1)S(1)}, u32[]{:S(2)}) copy-start(bf16[512,768]{1,0:T(8,128)(2,1)S(1)} %get-tuple-element.61.k_ref) | copy-start | bytes 2359300
  94.3 10.2 %copy-start.38 = (s32[8]{0:T(128)S(1)}, s32[8]{0:T(128)}, u32[]{:S(2)}) copy-start(s32[8]{0:T(128)} %constant.29.clone) | copy-start | bytes 100
  95.6 23.7 %collective-permute-start.10 = (bf16[256,2048]{1,0:T(8,128)(2,1)S(1)}, bf16[256,2048]{1,0:T(8,128)(2,1)}, u32[]{:S(2)}, u32[]{:S(2)}) collective-permute-start(bf16[256,2048]{1,0:T(8,128)(2,1)S(1)} %shard_map.155), channel_id=1, source_target_pairs={{1,2},{2,1},{5,6},{6,5},{9,10},{10,9},{13,14},{14,13},{17,18},{18,... | collective-permute-start | bytes 3145736 | tf_op jit(solution)/shard_map/ppermute | solution.py:467
  97.7 23.9 %collective-permute-start.7 = (bf16[256,2048]{1,0:T(8,128)(2,1)}, bf16[256,2048]{1,0:T(8,128)(2,1)S(1)}, u32[]{:S(2)}, u32[]{:S(2)}) collective-permute-start(bf16[256,2048]{1,0:T(8,128)(2,1)} %collective-permute-done.6.refs_3_.refs_2_), channel_id=1, source_target_pairs={{1,0},{2,3},{5,4},{6,7},{9,8},{10,11},{13,12},{14,15},{17,16},{18,... | collective-permute-start | bytes 3145736 | tf_op jit(solution)/shard_map/ppermute | solution.py:470
  101.8 40.0 %collective-permute-start.5 = (bf16[256,2048]{1,0:T(8,128)(2,1)}, bf16[256,2048]{1,0:T(8,128)(2,1)}, u32[]{:S(2)}, u32[]{:S(2)}) collective-permute-start(bf16[256,2048]{1,0:T(8,128)(2,1)} %shard_map.151), channel_id=1, source_target_pairs={{1,2},{2,1},{5,6},{6,5},{9,10},{10,9},{13,14},{14,13},{17,18},{18,... | collective-permute-start | bytes 3145736 | tf_op jit(solution)/shard_map/ppermute | solution.py:467
  119.3 24.4 %collective-permute-start.11 = (bf16[256,2048]{1,0:T(8,128)(2,1)}, bf16[256,2048]{1,0:T(8,128)(2,1)}, u32[]{:S(2)}, u32[]{:S(2)}) collective-permute-start(bf16[256,2048]{1,0:T(8,128)(2,1)} %collective-permute-done.10.refs_2_.refs_3_), channel_id=1, source_target_pairs={{1,0},{2,3},{5,4},{6,7},{9,8},{10,11},{13,12},{14,15},{17,16},{18,... | collective-permute-start | bytes 3145736 | tf_op jit(solution)/shard_map/ppermute | solution.py:470
  130.9 3.7 %copy-start = (bf16[6144,768]{1,0:T(8,128)(2,1)S(1)}, bf16[6144,768]{1,0:T(8,128)(2,1)}, u32[]{:S(2)}) copy-start(bf16[6144,768]{1,0:T(8,128)(2,1)} %all-gather.3.cloned.1.call-done) | copy-start | bytes 28311556
  137.9 10.4 %slice-start = ((s8[9437184]{0:T(1024)(128)(4,1)}), s8[4194304]{0:T(1024)(128)(4,1)S(1)}, s32[]{:S(2)}) async-start(s8[9437184]{0:T(1024)(128)(4,1)} %bitcast.9), calls=%async_computation.1 | async-start | bytes 8388608
  137.9 10.4 %slice-start.1 = ((s8[9437184]{0:T(1024)(128)(4,1)}), s8[4194304]{0:T(1024)(128)(4,1)S(1)}, s32[]{:S(2)}) async-start(s8[9437184]{0:T(1024)(128)(4,1)} %bitcast.9), calls=%async_computation.2 | async-start | bytes 8388608
  141.8 1.9 copy-start.37
  141.8 6.5 %slice-start.2 = ((s8[9437184]{0:T(1024)(128)(4,1)}), s8[1048576]{0:T(1024)(128)(4,1)S(1)}, s32[]{:S(2)}) async-start(s8[9437184]{0:T(1024)(128)(4,1)} %bitcast.9), calls=%async_computation.3 | async-start | bytes 2097152
  141.8 19.9 %collective-permute-start.8 = (bf16[256,2048]{1,0:T(8,128)(2,1)}, bf16[256,2048]{1,0:T(8,128)(2,1)S(1)}, u32[]{:S(2)}, u32[]{:S(2)}) collective-permute-start(bf16[256,2048]{1,0:T(8,128)(2,1)} %shard_map.154.refs_2_.refs_3_), channel_id=1, source_target_pairs={{1,0},{2,3},{5,4},{6,7},{9,8},{10,11},{13,12},{14,15},{17,16},{18,... | collective-permute-start | bytes 3145736 | tf_op jit(solution)/shard_map/ppermute | solution.py:470
  148.3 3.9 %copy-start.8 = (bf16[4,768,384]{2,1,0:T(8,128)(2,1)S(1)}, bf16[4,768,384]{2,1,0:T(8,128)(2,1)}, u32[]{:S(2)}) copy-start(bf16[4,768,384]{2,1,0:T(8,128)(2,1)} %copy-done.7) | copy-start | bytes 7077892
  165.7 10.6 %collective-permute-start.12 = (bf16[4,768,384]{2,1,0:T(8,128)(2,1)S(1)}, bf16[4,768,384]{2,1,0:T(8,128)(2,1)S(1)}, u32[]{:S(2)}, u32[]{:S(2)}) collective-permute-start(bf16[4,768,384]{2,1,0:T(8,128)(2,1)S(1)} %get-tuple-element.63), channel_id=1, source_target_pairs={{0,4},{4,0},{8,12},{12,8},{16,20},{20,16},{24,28},{28,24},{1,5},{5... | collective-permute-start | bytes 7077896 | tf_op jit(solution)/shard_map/ppermute | solution.py:443
  172.0 7.5 %collective-permute-start.13 = (bf16[4,768,384]{2,1,0:T(8,128)(2,1)S(1)}, bf16[4,768,384]{2,1,0:T(8,128)(2,1)S(1)}, u32[]{:S(2)}, u32[]{:S(2)}) collective-permute-start(bf16[4,768,384]{2,1,0:T(8,128)(2,1)S(1)} %get-tuple-element.64), channel_id=1, source_target_pairs={{0,4},{4,0},{8,12},{12,8},{16,20},{20,16},{24,28},{28,24},{1,5},{5... | collective-permute-start | bytes 7077896 | tf_op jit(solution)/shard_map/ppermute | solution.py:443
  172.1 7.5 %copy-start.21 = (bf16[6,512,512]{2,1,0:T(8,128)(2,1)S(1)}, bf16[6,512,512]{2,1,0:T(8,128)(2,1)}, u32[]{:S(2)}) copy-start(bf16[6,512,512]{2,1,0:T(8,128)(2,1)} %copy-done.20) | copy-start | bytes 9437188
  172.1 7.5 %copy-start.27 = (bf16[512,768]{1,0:T(8,128)(2,1)S(1)}, bf16[512,768]{1,0:T(8,128)(2,1)}, u32[]{:S(2)}) copy-start(bf16[512,768]{1,0:T(8,128)(2,1)} %get-tuple-element.46.att_ref) | copy-start | bytes 2359300
  172.1 7.5 %copy-start.29 = (bf16[768,512]{1,0:T(8,128)(2,1)S(1)}, bf16[768,512]{1,0:T(8,128)(2,1)}, u32[]{:S(2)}) copy-start(bf16[768,512]{1,0:T(8,128)(2,1)} %copy-done.28) | copy-start | bytes 2359300
  172.1 7.5 %copy-start.31 = (bf16[512,768]{1,0:T(8,128)(2,1)S(1)}, bf16[512,768]{1,0:T(8,128)(2,1)}, u32[]{:S(2)}) copy-start(bf16[512,768]{1,0:T(8,128)(2,1)} %copy-done.30) | copy-start | bytes 2359300
  172.1 7.5 %copy-start.33 = (bf16[512,768]{1,0:T(8,128)(2,1)S(1)}, bf16[512,768]{1,0:T(8,128)(2,1)}, u32[]{:S(2)}) copy-start(bf16[512,768]{1,0:T(8,128)(2,1)} %copy-done.32) | copy-start | bytes 2359300
  188.0 27.2 %collective-permute-start.19 = (bf16[2,768,384]{2,1,0:T(8,128)(2,1)S(1)}, bf16[2,768,384]{2,1,0:T(8,128)(2,1)S(1)}, u32[]{:S(2)}, u32[]{:S(2)}) collective-permute-start(bf16[2,768,384]{2,1,0:T(8,128)(2,1)S(1)} %get-tuple-element.78), channel_id=1, source_target_pairs={{0,16},{4,20},{8,24},{12,28},{16,0},{20,4},{24,8},{28,12},{1,17},{... | collective-permute-start | bytes 3538952 | tf_op jit(solution)/shard_map/ppermute | solution.py:443
  189.3 27.6 %collective-permute-start.17 = (bf16[2,768,384]{2,1,0:T(8,128)(2,1)S(1)}, bf16[2,768,384]{2,1,0:T(8,128)(2,1)S(1)}, u32[]{:S(2)}, u32[]{:S(2)}) collective-permute-start(bf16[2,768,384]{2,1,0:T(8,128)(2,1)S(1)} %get-tuple-element.76), channel_id=1, source_target_pairs={{0,8},{4,12},{8,0},{12,4},{16,24},{20,28},{24,16},{28,20},{1,9},{5... | collective-permute-start | bytes 3538952 | tf_op jit(solution)/shard_map/ppermute | solution.py:443
  190.5 42.0 %collective-permute-start.14 = (bf16[3,128,768]{2,1,0:T(8,128)(2,1)S(1)}, bf16[3,128,768]{2,1,0:T(8,128)(2,1)S(1)}, u32[]{:S(2)}, u32[]{:S(2)}) collective-permute-start(bf16[3,128,768]{2,1,0:T(8,128)(2,1)S(1)} %get-tuple-element.65), channel_id=1, source_target_pairs={{0,2},{1,3},{2,0},{3,1},{4,6},{5,7},{6,4},{7,5},{8,10},{9,11},{10,... | collective-permute-start | bytes 1769480 | tf_op jit(solution)/shard_map/ppermute | solution.py:443
  193.2 51.8 %collective-permute-start.15 = (bf16[3,128,768]{2,1,0:T(8,128)(2,1)S(1)}, bf16[3,128,768]{2,1,0:T(8,128)(2,1)S(1)}, u32[]{:S(2)}, u32[]{:S(2)}) collective-permute-start(bf16[3,128,768]{2,1,0:T(8,128)(2,1)S(1)} %get-tuple-element.66), channel_id=1, source_target_pairs={{0,3},{1,2},{2,1},{3,0},{4,7},{5,6},{6,5},{7,4},{8,11},{9,10},{10,... | collective-permute-start | bytes 1769480 | tf_op jit(solution)/shard_map/ppermute | solution.py:443
  193.8 36.7 %collective-permute-start.16 = (bf16[3,128,768]{2,1,0:T(8,128)(2,1)S(1)}, bf16[3,128,768]{2,1,0:T(8,128)(2,1)S(1)}, u32[]{:S(2)}, u32[]{:S(2)}) collective-permute-start(bf16[3,128,768]{2,1,0:T(8,128)(2,1)S(1)} %get-tuple-element.68), channel_id=1, source_target_pairs={{0,1},{1,0},{2,3},{3,2},{4,5},{5,4},{6,7},{7,6},{8,9},{9,8},{10,11... | collective-permute-start | bytes 1769480 | tf_op jit(solution)/shard_map/ppermute | solution.py:443
  215.6 31.0 %collective-permute-start.20 = (bf16[1,768,384]{2,1,0:T(8,128)(2,1)S(1)}, bf16[1,768,384]{2,1,0:T(8,128)(2,1)S(1)}, u32[]{:S(2)}, u32[]{:S(2)}) collective-permute-start(bf16[1,768,384]{2,1,0:T(8,128)(2,1)S(1)} %slice.46), channel_id=1, source_target_pairs={{0,8},{4,12},{8,0},{12,4},{16,24},{20,28},{24,16},{28,20},{1,9},{5... | collective-permute-start | bytes 1769480 | tf_op jit(solution)/shard_map/ppermute | solution.py:443
  217.2 29.6 %collective-permute-start.18 = (bf16[1,768,384]{2,1,0:T(8,128)(2,1)S(1)}, bf16[1,768,384]{2,1,0:T(8,128)(2,1)S(1)}, u32[]{:S(2)}, u32[]{:S(2)}) collective-permute-start(bf16[1,768,384]{2,1,0:T(8,128)(2,1)S(1)} %slice.47), channel_id=1, source_target_pairs={{0,16},{4,20},{8,24},{12,28},{16,0},{20,4},{24,8},{28,12},{1,17},{... | collective-permute-start | bytes 1769480 | tf_op jit(solution)/shard_map/ppermute | solution.py:443
  (16 other events, 17.4 us)
Sparse Core Ops, SparseCore 0:
  9.9 60.4 all-gather.2

commit v4 on v3

--- a/solution.py
+++ b/solution.py
@@ -89,7 +89,7 @@
             out_specs=[whole(shape)] * len(partners),
         ),
         cost_estimate=light(),
-        compiler_params=params(),
+        compiler_params=params(60),
     )(table, *[q, k, v] * len(partners), *after)
 
 
@@ -291,21 +291,23 @@
     sums, refs = refs[: 2 * chains], refs[2 * chains :]
     outs, folded, held = refs[:group], refs[group:-1], refs[-1]
     rows = outs[0].shape[1]
-    grad = g_ref[...]
-    weights = weight_ref[0]
-    grad_float = grad.astype(F32)
-    att = jnp.concatenate(
-        [
-            att_ref[pl.ds(pl.multiple_of(owner(table, t) * rows, rows), rows), :]
-            for t in range(group)
-        ],
-        axis=0,
-    )
-    delta = jnp.sum(grad_float * att.astype(F32), axis=1, keepdims=True)
-    diff = (weights.astype(F32) * (dot(grad, v_ref[...], NT) - delta)).astype(BF16)
-    held[0] = (dot(diff, k_ref[...]) * scale).astype(BF16)
-    held[1] = (dot(q_t_ref[...], diff) * scale).T.astype(BF16)
-    held[2] = dot(grad_float.T.astype(BF16), weights).T.astype(BF16)
+    for i in range(weight_ref.shape[0]):
+        one = slice(i * HEAD_DIM, (i + 1) * HEAD_DIM)
+        grad = g_ref[:, one]
+        weights = weight_ref[i]
+        grad_float = grad.astype(F32)
+        att = jnp.concatenate(
+            [
+                att_ref[pl.ds(pl.multiple_of(owner(table, t) * rows, rows), rows), one]
+                for t in range(group)
+            ],
+            axis=0,
+        )
+        delta = jnp.sum(grad_float * att.astype(F32), axis=1, keepdims=True)
+        diff = (weights.astype(F32) * (dot(grad, v_ref[:, one], NT) - delta)).astype(BF16)
+        held[0, :, one] = (dot(diff, k_ref[:, one]) * scale).astype(BF16)
+        held[1, :, one] = (dot(q_t_ref[one, :], diff) * scale).T.astype(BF16)
+        held[2, :, one] = dot(grad_float.T.astype(BF16), weights).T.astype(BF16)
     for s, out in enumerate(outs):
         here = pl.ds(pl.multiple_of(slot(table, s) * rows, rows), rows)
         out[...] = held[:, here, :]
@@ -322,32 +324,34 @@
     total, width = grad.shape
     rows = total // group
     heads = width // HEAD_DIM
-    column = pl.BlockSpec((total, HEAD_DIM), lambda h, *_: (0, h))
-    row = pl.BlockSpec((HEAD_DIM, total), lambda h, *_: (h, 0))
+    per = 2 if heads % 2 == 0 else 1
+    wide = per * HEAD_DIM
+    column = pl.BlockSpec((total, wide), lambda h, *_: (0, h))
+    row = pl.BlockSpec((wide, total), lambda h, *_: (h, 0))
     sum_shapes, sum_specs, half_shapes, half_specs = [], [], [], []
     for keep, _ in sums:
         count, _, columns = keep.shape
-        sum_specs += [pl.BlockSpec((count, HEAD_DIM, columns), lambda h, *_: (0, h, 0))] * 2
-        half_specs += [pl.BlockSpec((count // 2, HEAD_DIM, columns), lambda h, *_: (0, h, 0))] * 2
+        sum_specs += [pl.BlockSpec((count, wide, columns), lambda h, *_: (0, h, 0))] * 2
+        half_specs += [pl.BlockSpec((count // 2, wide, columns), lambda h, *_: (0, h, 0))] * 2
         half_shapes += [jax.ShapeDtypeStruct((count // 2, width, columns), BF16)] * 2
     outs = pl.pallas_call(
         functools.partial(backward_kernel, group, len(sums)),
         out_shape=[jax.ShapeDtypeStruct((3, rows, width), BF16)] * group + half_shapes,
         grid_spec=pltpu.PrefetchScalarGridSpec(
             num_scalar_prefetch=1,
-            grid=(heads,),
+            grid=(heads // per,),
             in_specs=[
                 column,
                 column,
-                pl.BlockSpec((1, total, total), lambda h, *_: (h, 0, 0)),
+                pl.BlockSpec((per, total, total), lambda h, *_: (h, 0, 0)),
                 row,
                 column,
                 column,
             ]
             + sum_specs,
-            out_specs=[pl.BlockSpec((3, rows, HEAD_DIM), lambda h, *_: (0, 0, h))] * group
+            out_specs=[pl.BlockSpec((3, rows, wide), lambda h, *_: (0, 0, h))] * group
             + half_specs,
-            scratch_shapes=[pltpu.VMEM((3, total, HEAD_DIM), BF16)],
+            scratch_shapes=[pltpu.VMEM((3, total, wide), BF16)],
         ),
         cost_estimate=light(),
         compiler_params=params(),
@@ -522,10 +526,11 @@
         state = outer(order, att_t, second, 0, cut, part, part + cut, state)
     rest = part - cut
     other = outer(other_order, att_t, second, cut, rest, part, part + rest)
-    *other, keep, send, grad = outer(
-        other_order, att_t, third, 0, part, 0, part + rest, other, passed=[*state, grad]
+    keep, send = state[0], hold(state[1], [third[-1]])
+    *other, grad = outer(
+        other_order, att_t, third, 0, part, 0, part + rest, other, passed=[grad]
     )
-    grad = project(third, weights_full, 2 * part, grad, BF16, after=[other[0], keep])
+    grad = project(third, weights_full, 2 * part, grad, BF16, after=[other[0]])
     arrived = swap(send, "dp", dp, masks[0][0])
     other_arrived = swap(other[1], "dp", dp, masks[1][0])
     back, halves = backward(

time: 256 us -> 253 us (0.988)
    ppermute x15, waiting for transfers between devices: 108 us -> 101 us  [swap(): return lax.ppermute(value, axis, [(i, i ^ mask) for i in range(size)])]
    pallas_call x2, Pallas kernels: 1.24 us -> 6.07 us  [pack(): pl.pallas_call(functools.partial(pack_kernel, len(partners)), out_shape=[...]
    ppermute x3, waiting for transfers between devices: 4.95 us -> 8.09 us  [gather_rows(): outer = lax.ppermute(inner, 'head', [(1, 0), (2, 3)])]
    unnamed x84 -> x82, local copies, waits for them, and re-layouts: 19.2 us -> 16.8 us
  transfers between devices with their start and end apart: 22 -> 22, of which waited for: 11 -> 11; matrix products, arithmetic and copies ran while one was open for 1% -> 1% of each run, Pallas kernels for 17% -> 18%
where the time goes in v4:
time: 253 us; the launch traced here: 252 us
  waiting for transfers between devices  128 us (51%)
  Pallas kernels  56.1 us (22%)
  starting transfers between devices  33 us (13%)
  local copies, waits for them, and re-layouts  17.2 us (7%)
  between operations  14.5 us (6%)
  other arithmetic  3.34 us (1%)
    ppermute x15, waiting for transfers between devices, swap(): return lax.ppermute(value, axis, [(i, i ^ mask) for i in range(size)])  101 us
    ppermute x15, starting transfers between devices, swap(): return lax.ppermute(value, axis, [(i, i ^ mask) for i in range(size)])  18.2 us
    ppermute x3, waiting for transfers between devices, gather_rows(): lax.ppermute(join(own, near) if both is None else both, 'head', [(1, 2),...  17.6 us
    unnamed x82, local copies, waits for them, and re-layouts  16.8 us
    pallas_call x4, Pallas kernels, outer(): pl.pallas_call(functools.partial(outer_kernel, len(rows), start, len(pass...  16.1 us
    pallas_call x3, Pallas kernels, project(): pl.pallas_call(functools.partial(project_kernel, len(rows), len(at), not...  11 us
    ppermute x3, starting transfers between devices, gather_rows(): lax.ppermute(join(own, near) if both is None else both, 'head', [(1, 2),...  8.25 us
    ppermute x3, waiting for transfers between devices, gather_rows(): outer = lax.ppermute(inner, 'head', [(1, 0), (2, 3)])  8.09 us
  transfers between devices with their start and end apart: 22, of which 11 were waited for; matrix products, arithmetic and copies ran while one was open for 1% of the time, Pallas kernels for 18%

profile of v4, /device:TPU:9, one launch (start us, length us, event | category | flops | bytes accessed | tf_op | source)
XLA Modules:
  0.0 252.0 jit_solution(972881489020052540)
XLA Ops:
  9.2 3.4 %shard_map.146 = (bf16[3,128,768]{2,1,0:T(8,128)(2,1)}, bf16[3,128,768]{2,1,0:T(8,128)(2,1)}, bf16[3,128,768]{2,1,0:T(8,128)(2,1)}) custom-call(s32[12]{0:T(128)} %pad_add_fusion.table.place, bf16[1,128,3072]{2,1,0:T(8,128)(2,1)} %refs_0_.3, bf16[1,128,3072]{2,1,0:T(8,128)(2,1)} %refs_1_.3, bf16[1,128,3072]{2,1,0:T(8,128)(2,1)} %refs_2_.3, ...), custom_call_target="tpu_custom_call" | custom-call | flops 1 | bytes 1 | tf_op jit(solution)/shard_map/pallas_call | solution.py:82
  12.6 2.5 collective-permute-start.1
  15.3 1.4 copy-done.24
  16.8 1.1 collective-permute-start.3
  17.9 45.8 %collective-permute-done.3.b_ref.refs_2_.refs_1_ = bf16[128,2048]{1,0:T(8,128)(2,1)S(1)} collective-permute-done((bf16[128,2048]{1,0:T(8,128)(2,1)S(1)}, bf16[128,2048]{1,0:T(8,128)(2,1)S(1)}, u32[]{:S(2)}, u32[]{:S(2)}) %collective-permute-start.3) | collective-permute-done | bytes 524320 | tf_op jit(solution)/shard_map/ppermute | solution.py:447
  63.8 2.3 collective-permute-done.2.refs_2_.refs_3_
  66.0 1.1 shard_map.149.refs_4_
  67.1 3.3 %collective-permute-start.6 = (bf16[256,2048]{1,0:T(8,128)(2,1)}, bf16[256,2048]{1,0:T(8,128)(2,1)}, u32[]{:S(2)}, u32[]{:S(2)}) collective-permute-start(bf16[256,2048]{1,0:T(8,128)(2,1)} %shard_map.149.refs_4_), channel_id=1, source_target_pairs={{1,2},{2,1},{5,6},{6,5},{9,10},{10,9},{13,14},{14,13},{17,18},{18,... | collective-permute-start | bytes 3145736 | tf_op jit(solution)/shard_map/ppermute | solution.py:471
  70.6 1.4 collective-permute-start.9
  72.5 2.6 %shard_map.147.refs_0_ = bf16[3,128,768]{2,1,0:T(8,128)(2,1)} custom-call(s32[12]{0:T(128)} %pad_add_fusion.table.place, bf16[1,128,3072]{2,1,0:T(8,128)(2,1)} %refs_0_.3, bf16[1,128,3072]{2,1,0:T(8,128)(2,1)} %refs_1_.3, bf16[1,128,3072]{2,1,0:T(8,128)(2,1)} %refs_2_.3, bf16[3,128,768]{2,1,0:T(8,128)(2,1)} %copy-done.7), custom_call_target="tpu_custom_call" | custom-call | flops 1 | bytes 1 | tf_op jit(solution)/shard_map/pallas_call | solution.py:82
  76.2 1.1 copy-done.20
  77.3 1.1 copy-done.22
  78.4 1.1 copy-done.23
  79.4 7.9 %shard_map.150 = (bf16[512,768]{1,0:T(8,128)(2,1)}, bf16[768,512]{1,0:T(8,128)(2,1)S(1)}, bf16[6,512,512]{2,1,0:T(8,128)(2,1)S(1)}, bf16[768,512]{1,0:T(8,128)(2...) custom-call(s32[12]{0:T(128)S(1)} %copy-done.32, s32[1,512]{1,0:T(1,128)S(1)} %copy-done.33, ...), custom_call_target="tpu_custom_call" | custom-call | flops 1 | bytes 1 | tf_op jit(solution)/shard_map/pallas_call | solution.py:251
  89.1 4.2 %collective-permute-done.9.b_ref.refs_1_.refs_2_ = bf16[128,2048]{1,0:T(8,128)(2,1)S(1)} collective-permute-done((bf16[128,2048]{1,0:T(8,128)(2,1)S(1)}, bf16[128,2048]{1,0:T(8,128)(2,1)S(1)}, u32[]{:S(2)}, u32[]{:S(2)}) %collective-permute-start.9) | collective-permute-done | bytes 524320 | tf_op jit(solution)/shard_map/ppermute | solution.py:447
  93.3 1.1 shard_map.155
  94.4 2.1 collective-permute-start.10
  96.5 2.6 %collective-permute-start.7 = (bf16[256,2048]{1,0:T(8,128)(2,1)}, bf16[256,2048]{1,0:T(8,128)(2,1)}, u32[]{:S(2)}, u32[]{:S(2)}) collective-permute-start(bf16[256,2048]{1,0:T(8,128)(2,1)} %collective-permute-done.6.refs_3_.refs_2_), channel_id=1, source_target_pairs={{1,0},{2,3},{5,4},{6,7},{9,8},{10,11},{13,12},{14,15},{17,16},{18,... | collective-permute-start | bytes 3145736 | tf_op jit(solution)/shard_map/ppermute | solution.py:474
  99.1 2.1 shard_map.151
  101.2 2.9 %collective-permute-start.5 = (bf16[256,2048]{1,0:T(8,128)(2,1)}, bf16[256,2048]{1,0:T(8,128)(2,1)}, u32[]{:S(2)}, u32[]{:S(2)}) collective-permute-start(bf16[256,2048]{1,0:T(8,128)(2,1)} %shard_map.151), channel_id=1, source_target_pairs={{1,2},{2,1},{5,6},{6,5},{9,10},{10,9},{13,14},{14,13},{17,18},{18,... | collective-permute-start | bytes 3145736 | tf_op jit(solution)/shard_map/ppermute | solution.py:471
  104.1 14.3 %collective-permute-done.10.refs_2_.refs_3_ = bf16[256,2048]{1,0:T(8,128)(2,1)} collective-permute-done((bf16[256,2048]{1,0:T(8,128)(2,1)}, bf16[256,2048]{1,0:T(8,128)(2,1)}, u32[]{:S(2)}, u32[]{:S(2)}) %collective-permute-start.10) | collective-permute-done | bytes 1048608 | tf_op jit(solution)/shard_map/ppermute | solution.py:471
  118.5 2.3 collective-permute-start.11
  122.8 3.9 %shard_map.153 = (bf16[4,768,384]{2,1,0:T(8,128)(2,1)S(1)}, bf16[4,768,384]{2,1,0:T(8,128)(2,1)S(1)}) custom-call(s32[8]{0:T(128)S(1)} %broadcast_xor_fusion.1.blocks, bf16[768,512]{1,0:T(8,128)(2,1)S(1)} %get-tuple-element.46.att_t_ref.refs_0_, bf16[128,2048]{1,0:T(8,128)(2,1)S(1)} %copy-done.10, bf16[128,2048]{1,0:T(8,128)(2,1)S(1)} %copy-done.13, ...), custom_call_target="tpu_custom_call" | custom-call | flops 1 | bytes 1 | tf_op jit(solution)/shard_map/pallas_call | solution.py:430
  126.7 1.4 copy-done.1
  128.1 3.7 %copy-done = bf16[6144,768]{1,0:T(8,128)(2,1)S(1)} copy-done((bf16[6144,768]{1,0:T(8,128)(2,1)S(1)}, bf16[6144,768]{1,0:T(8,128)(2,1)}, u32[]{:S(2)}) %copy-start) | copy-done | bytes 9437208
  133.9 3.7 %shard_map.152.refs_1_.refs_5_ = f32[512,768]{1,0:T(8,128)S(1)} custom-call(bf16[8,768,768]{2,1,0:T(8,128)(2,1)S(1)} %bitcast.8, bf16[128,2048]{1,0:T(8,128)(2,1)S(1)} %copy-done.11, bf16[128,2048]{1,0:T(8,128)(2,1)S(1)} %copy-done.14, bf16[256,2048]{1,0:T(8,128)(2,1)} %collective-permute-done.6.refs_3_.refs_2_, ...), custom_call_target="tpu_custom_call" | custom-call | flops 1 | bytes 1 | tf_op jit(solution)/shard_map/pallas_call | solution.py:396
  137.6 3.3 %collective-permute-done.5.refs_0_ = bf16[256,2048]{1,0:T(8,128)(2,1)} collective-permute-done((bf16[256,2048]{1,0:T(8,128)(2,1)}, bf16[256,2048]{1,0:T(8,128)(2,1)}, u32[]{:S(2)}, u32[]{:S(2)}) %collective-permute-start.5) | collective-permute-done | bytes 1048608 | tf_op jit(solution)/shard_map/ppermute | solution.py:471
  141.0 1.7 collective-permute-start.8
  142.7 4.2 %shard_map.156 = (bf16[4,768,384]{2,1,0:T(8,128)(2,1)S(1)}, bf16[4,768,384]{2,1,0:T(8,128)(2,1)S(1)}) custom-call(s32[8]{0:T(128)S(1)} %broadcast_xor_fusion.blocks, bf16[768,512]{1,0:T(8,128)(2,1)S(1)} %get-tuple-element.46.att_t_ref.refs_0_, bf16[128,2048]{1,0:T(8,128)(2,1)S(1)} %copy-done.4, bf16[128,2048]{1,0:T(8,128)(2,1)S(1)} %copy-done.6, ...), custom_call_target="tpu_custom_call" | custom-call | flops 1 | bytes 1 | tf_op jit(solution)/shard_map/pallas_call | solution.py:430
  147.0 3.7 %shard_map.157.refs_6_ = f32[512,768]{1,0:T(8,128)S(1)} custom-call(bf16[8,768,768]{2,1,0:T(8,128)(2,1)S(1)} %bitcast.11, bf16[128,2048]{1,0:T(8,128)(2,1)S(1)} %copy-done.4, bf16[128,2048]{1,0:T(8,128)(2,1)S(1)} %copy-done.6, bf16[256,2048]{1,0:T(8,128)(2,1)} %collective-permute-done.10.refs_2_.refs_3_, ...), custom_call_target="tpu_custom_call" | custom-call | flops 1 | bytes 1 | tf_op jit(solution)/shard_map/pallas_call | solution.py:396
  150.7 4.2 %shard_map.160 = (bf16[4,768,384]{2,1,0:T(8,128)(2,1)S(1)}, bf16[4,768,384]{2,1,0:T(8,128)(2,1)S(1)}) custom-call(s32[8]{0:T(128)S(1)} %broadcast_xor_fusion.1.blocks, bf16[768,512]{1,0:T(8,128)(2,1)S(1)} %get-tuple-element.46.att_t_ref.refs_0_, bf16[128,2048]{1,0:T(8,128)(2,1)S(1)} %copy-done.4, ...), custom_call_target="tpu_custom_call", output_to_operand_aliasing={{0}: (6, {}), {1}: (7, {})} | custom-call | flops 1 | bytes 1 | tf_op jit(solution)/shard_map/pallas_call | solution.py:430
  155.0 8.1 %collective-permute-done.8.refs_3_.refs_4_.refs_1_ = bf16[256,2048]{1,0:T(8,128)(2,1)S(1)} collective-permute-done((bf16[256,2048]{1,0:T(8,128)(2,1)}, bf16[256,2048]{1,0:T(8,128)(2,1)S(1)}, u32[]{:S(2)}, u32[]{:S(2)}) %collective-permute-start.8) | collective-permute-done | bytes 1048608 | tf_op jit(solution)/shard_map/ppermute | solution.py:474
  163.0 3.8 %shard_map.158 = (bf16[4,768,384]{2,1,0:T(8,128)(2,1)S(1)}, bf16[4,768,384]{2,1,0:T(8,128)(2,1)S(1)}, f32[512,768]{1,0:T(8,128)S(1)}) custom-call(s32[8]{0:T(128)S(1)} %broadcast_xor_fusion.blocks, bf16[768,512]{1,0:T(8,128)(2,1)S(1)} %get-tuple-element.46.att_t_ref.refs_0_, ...), custom_call_target="tpu_custom_call", output_to_operand_aliasing={{0}: (6, {}), {1}: (7, {}), {2}: (8, {})} | custom-call | flops 1 | bytes 1 | tf_op jit(solution)/shard_map/pallas_call | solution.py:430
  166.8 3.8 %collective-permute-start.13 = (bf16[4,768,384]{2,1,0:T(8,128)(2,1)S(1)}, bf16[4,768,384]{2,1,0:T(8,128)(2,1)S(1)}, u32[]{:S(2)}, u32[]{:S(2)}) collective-permute-start(bf16[4,768,384]{2,1,0:T(8,128)(2,1)S(1)} %get-tuple-element.60), channel_id=1, source_target_pairs={{0,4},{4,0},{8,12},{12,8},{16,20},{20,16},{24,28},{28,24},{1,5},{5... | collective-permute-start | bytes 7077896 | tf_op jit(solution)/shard_map/ppermute | solution.py:447
  170.7 3.6 %shard_map.159.g_ref = bf16[512,768]{1,0:T(8,128)(2,1)S(1)} custom-call(bf16[8,768,768]{2,1,0:T(8,128)(2,1)S(1)} %bitcast.12, bf16[128,2048]{1,0:T(8,128)(2,1)S(1)} %copy-done.16, bf16[128,2048]{1,0:T(8,128)(2,1)} %collective-permute-done.4.b_ref.refs_1_.refs_2_, bf16[256,2048]{1,0:T(8,128)(2,1)} %shard_map.154.refs_2_.refs_3_, ...), custom_call_target="tpu_custom_call" | custom-call | flops 1 | bytes 1 | tf_op jit(solution)/shard_map/pallas_call | solution.py:396
  174.8 3.4 %collective-permute-done.12.refs_1_ = bf16[4,768,384]{2,1,0:T(8,128)(2,1)S(1)} collective-permute-done((bf16[4,768,384]{2,1,0:T(8,128)(2,1)S(1)}, bf16[4,768,384]{2,1,0:T(8,128)(2,1)S(1)}, u32[]{:S(2)}, u32[]{:S(2)}) %collective-permute-start.12) | collective-permute-done | bytes 2359328 | tf_op jit(solution)/shard_map/ppermute | solution.py:447
  178.2 6.8 %shard_map.162 = (bf16[3,128,768]{2,1,0:T(8,128)(2,1)S(1)}, bf16[3,128,768]{2,1,0:T(8,128)(2,1)S(1)}, bf16[3,128,768]{2,1,0:T(8,128)(2,1)S(1)}, bf16[3,128,768]{...) custom-call(s32[12]{0:T(128)S(1)} %copy-done.32, ...), custom_call_target="tpu_custom_call" | custom-call | flops 1 | bytes 1 | tf_op jit(solution)/shard_map/pallas_call | solution.py:337
  185.0 1.3 collective-permute-start.19
  186.3 1.2 collective-permute-start.17
  187.5 2.8 %collective-permute-start.14 = (bf16[3,128,768]{2,1,0:T(8,128)(2,1)S(1)}, bf16[3,128,768]{2,1,0:T(8,128)(2,1)S(1)}, u32[]{:S(2)}, u32[]{:S(2)}) collective-permute-start(bf16[3,128,768]{2,1,0:T(8,128)(2,1)S(1)} %get-tuple-element.61), channel_id=1, source_target_pairs={{0,2},{1,3},{2,0},{3,1},{4,6},{5,7},{6,4},{7,5},{8,10},{9,11},{10,... | collective-permute-start | bytes 1769480 | tf_op jit(solution)/shard_map/ppermute | solution.py:447
  191.5 20.8 %collective-permute-done.19 = bf16[2,768,384]{2,1,0:T(8,128)(2,1)S(1)} collective-permute-done((bf16[2,768,384]{2,1,0:T(8,128)(2,1)S(1)}, bf16[2,768,384]{2,1,0:T(8,128)(2,1)S(1)}, u32[]{:S(2)}, u32[]{:S(2)}) %collective-permute-start.19) | collective-permute-done | bytes 1179680 | tf_op jit(solution)/shard_map/ppermute | solution.py:447
  212.6 1.3 collective-permute-start.20
  214.2 1.3 collective-permute-start.18
  215.5 12.0 %collective-permute-done.16.refs_1_ = bf16[3,128,768]{2,1,0:T(8,128)(2,1)S(1)} collective-permute-done((bf16[3,128,768]{2,1,0:T(8,128)(2,1)S(1)}, bf16[3,128,768]{2,1,0:T(8,128)(2,1)S(1)}, u32[]{:S(2)}, u32[]{:S(2)}) %collective-permute-start.16) | collective-permute-done | bytes 589856 | tf_op jit(solution)/shard_map/ppermute | solution.py:447
  227.5 2.0 shard_map.163
  229.5 12.6 %collective-permute-done.15.refs_1_ = bf16[3,128,768]{2,1,0:T(8,128)(2,1)S(1)} collective-permute-done((bf16[3,128,768]{2,1,0:T(8,128)(2,1)S(1)}, bf16[3,128,768]{2,1,0:T(8,128)(2,1)S(1)}, u32[]{:S(2)}, u32[]{:S(2)}) %collective-permute-start.15) | collective-permute-done | bytes 589856 | tf_op jit(solution)/shard_map/ppermute | solution.py:447
  242.1 1.7 shard_map.164
  244.1 1.1 pad_maximum_fusion
  (119 shorter events, 12.6 us)
Async XLA Ops:
  7.2 121.0 %all-gather.3.cloned.1.call-start = ((), (), s32[]{:S(2)}) async-start(), calls=%async_computation | async-start | bytes 10616832 | tf_op jit(solution)/shard_map/all_gather | solution.py:505
  12.6 51.1 %collective-permute-start = (bf16[3,128,768]{2,1,0:T(8,128)(2,1)}, bf16[3,128,768]{2,1,0:T(8,128)(2,1)S(1)}, u32[]{:S(2)}, u32[]{:S(2)}) collective-permute-start(bf16[3,128,768]{2,1,0:T(8,128)(2,1)} %get-tuple-element.40), channel_id=1, source_target_pairs={{0,1},{1,0},{2,3},{3,2},{4,5},{5,4},{6,7},{7,6},{8,9},{9,8},{10,11... | collective-permute-start | bytes 1769480 | tf_op jit(solution)/shard_map/ppermute | solution.py:447
  12.6 51.1 %collective-permute-start.1 = (bf16[3,128,768]{2,1,0:T(8,128)(2,1)}, bf16[3,128,768]{2,1,0:T(8,128)(2,1)S(1)}, u32[]{:S(2)}, u32[]{:S(2)}) collective-permute-start(bf16[3,128,768]{2,1,0:T(8,128)(2,1)} %get-tuple-element.41), channel_id=1, source_target_pairs={{0,2},{1,3},{2,0},{3,1},{4,6},{5,7},{6,4},{7,5},{8,10},{9,11},{10,... | collective-permute-start | bytes 1769480 | tf_op jit(solution)/shard_map/ppermute | solution.py:447
  15.1 50.9 %collective-permute-start.2 = (bf16[3,128,768]{2,1,0:T(8,128)(2,1)}, bf16[3,128,768]{2,1,0:T(8,128)(2,1)S(1)}, u32[]{:S(2)}, u32[]{:S(2)}) collective-permute-start(bf16[3,128,768]{2,1,0:T(8,128)(2,1)} %get-tuple-element.42), channel_id=1, source_target_pairs={{0,3},{1,2},{2,1},{3,0},{4,7},{5,6},{6,5},{7,4},{8,11},{9,10},{10,... | collective-permute-start | bytes 1769480 | tf_op jit(solution)/shard_map/ppermute | solution.py:447
  16.7 55.4 %copy-start.35 = (s32[1,6,4]{1,2,0:T(4,128)S(1)}, s32[1,6,4]{1,2,0:T(4,128)}, u32[]{:S(2)}) copy-start(s32[1,6,4]{1,2,0:T(4,128)} %param.18) | copy-start | bytes 292
  16.7 55.5 %copy-start.34 = (s32[1,6,4,4]{1,3,2,0:T(4,128)S(1)}, s32[1,6,4,4]{1,3,2,0:T(4,128)}, u32[]{:S(2)}) copy-start(s32[1,6,4,4]{1,3,2,0:T(4,128)} %param.17) | copy-start | bytes 1156
  16.8 53.8 %copy-start.9 = (bf16[128,2048]{1,0:T(8,128)(2,1)}, bf16[128,2048]{1,0:T(8,128)(2,1)S(1)}, u32[]{:S(2)}) copy-start(bf16[128,2048]{1,0:T(8,128)(2,1)S(1)} %get-tuple-element.43.a_ref.refs_1_.refs_0_) | copy-start | bytes 1572868
  16.8 76.5 %copy-start.3 = (bf16[128,2048]{1,0:T(8,128)(2,1)}, bf16[128,2048]{1,0:T(8,128)(2,1)S(1)}, u32[]{:S(2)}) copy-start(bf16[128,2048]{1,0:T(8,128)(2,1)S(1)} %get-tuple-element.48.a_ref.refs_0_.refs_1_) | copy-start | bytes 1572868
  16.8 82.3 %copy-start.15 = (bf16[128,2048]{1,0:T(8,128)(2,1)}, bf16[128,2048]{1,0:T(8,128)(2,1)S(1)}, u32[]{:S(2)}) copy-start(bf16[128,2048]{1,0:T(8,128)(2,1)S(1)} %get-tuple-element.45.a_ref.refs_0_.refs_1_) | copy-start | bytes 1572868
  16.8 46.9 %collective-permute-start.3 = (bf16[128,2048]{1,0:T(8,128)(2,1)S(1)}, bf16[128,2048]{1,0:T(8,128)(2,1)S(1)}, u32[]{:S(2)}, u32[]{:S(2)}) collective-permute-start(bf16[128,2048]{1,0:T(8,128)(2,1)S(1)} %get-tuple-element.43.a_ref.refs_1_.refs_0_), channel_id=1, source_target_pairs={{0,1},{1,0},{2,3},{3,2},{4,5},{5,4},{6,7},{7,6},{8,9},{9,8},{10,11... | collective-permute-start | bytes 1572872 | tf_op jit(solution)/shard_map/ppermute | solution.py:447
  63.7 6.8 %copy-start.12 = (bf16[128,2048]{1,0:T(8,128)(2,1)}, bf16[128,2048]{1,0:T(8,128)(2,1)S(1)}, u32[]{:S(2)}) copy-start(bf16[128,2048]{1,0:T(8,128)(2,1)S(1)} %collective-permute-done.3.b_ref.refs_2_.refs_1_) | copy-start | bytes 1572868
  63.7 8.8 %copy-start.7 = (bf16[3,128,768]{2,1,0:T(8,128)(2,1)}, bf16[3,128,768]{2,1,0:T(8,128)(2,1)S(1)}, u32[]{:S(2)}) copy-start(bf16[3,128,768]{2,1,0:T(8,128)(2,1)S(1)} %collective-permute-done.refs_3_.refs_0_.refs_1_) | copy-start | bytes 1769476
  63.7 8.3 %copy-start.19 = (bf16[3,128,768]{2,1,0:T(8,128)(2,1)}, bf16[3,128,768]{2,1,0:T(8,128)(2,1)S(1)}, u32[]{:S(2)}) copy-start(bf16[3,128,768]{2,1,0:T(8,128)(2,1)S(1)} %collective-permute-done.1.refs_1_.refs_2_) | copy-start | bytes 1769476
  66.0 6.0 %copy-start.21 = (bf16[3,128,768]{2,1,0:T(8,128)(2,1)}, bf16[3,128,768]{2,1,0:T(8,128)(2,1)S(1)}, u32[]{:S(2)}) copy-start(bf16[3,128,768]{2,1,0:T(8,128)(2,1)S(1)} %collective-permute-done.2.refs_2_.refs_3_) | copy-start | bytes 1769476
  67.1 8.0 %copy-start.32 = (s32[12]{0:T(128)S(1)}, s32[12]{0:T(128)}, u32[]{:S(2)}) copy-start(s32[12]{0:T(128)} %pad_add_fusion.table.place) | copy-start | bytes 148
  67.1 8.0 %copy-start.33 = (s32[1,512]{1,0:T(1,128)S(1)}, s32[1,512]{1,0:T(1,128)}, u32[]{:S(2)}) copy-start(s32[1,512]{1,0:T(1,128)} %order_ref.1) | copy-start | bytes 6148
  67.1 29.4 %collective-permute-start.6 = (bf16[256,2048]{1,0:T(8,128)(2,1)}, bf16[256,2048]{1,0:T(8,128)(2,1)}, u32[]{:S(2)}, u32[]{:S(2)}) collective-permute-start(bf16[256,2048]{1,0:T(8,128)(2,1)} %shard_map.149.refs_4_), channel_id=1, source_target_pairs={{1,2},{2,1},{5,6},{6,5},{9,10},{10,9},{13,14},{14,13},{17,18},{18,... | collective-permute-start | bytes 3145736 | tf_op jit(solution)/shard_map/ppermute | solution.py:471
  70.5 28.7 %collective-permute-start.4 = (bf16[128,2048]{1,0:T(8,128)(2,1)S(1)}, bf16[128,2048]{1,0:T(8,128)(2,1)}, u32[]{:S(2)}, u32[]{:S(2)}) collective-permute-start(bf16[128,2048]{1,0:T(8,128)(2,1)S(1)} %get-tuple-element.45.a_ref.refs_0_.refs_1_), channel_id=1, source_target_pairs={{0,1},{1,0},{2,3},{3,2},{4,5},{5,4},{6,7},{7,6},{8,9},{9,8},{10,11... | collective-permute-start | bytes 1572872 | tf_op jit(solution)/shard_map/ppermute | solution.py:447
  70.6 22.7 %collective-permute-start.9 = (bf16[128,2048]{1,0:T(8,128)(2,1)S(1)}, bf16[128,2048]{1,0:T(8,128)(2,1)S(1)}, u32[]{:S(2)}, u32[]{:S(2)}) collective-permute-start(bf16[128,2048]{1,0:T(8,128)(2,1)S(1)} %get-tuple-element.48.a_ref.refs_0_.refs_1_), channel_id=1, source_target_pairs={{0,1},{1,0},{2,3},{3,2},{4,5},{5,4},{6,7},{7,6},{8,9},{9,8},{10,11... | collective-permute-start | bytes 1572872 | tf_op jit(solution)/shard_map/ppermute | solution.py:447
  89.1 12.1 %copy-start.17 = (bf16[6,512,512]{2,1,0:T(8,128)(2,1)}, bf16[6,512,512]{2,1,0:T(8,128)(2,1)S(1)}, u32[]{:S(2)}) copy-start(bf16[6,512,512]{2,1,0:T(8,128)(2,1)S(1)} %get-tuple-element.53.weight_ref) | copy-start | bytes 9437188
  89.1 12.1 %copy-start.26 = (bf16[768,512]{1,0:T(8,128)(2,1)}, bf16[768,512]{1,0:T(8,128)(2,1)S(1)}, u32[]{:S(2)}) copy-start(bf16[768,512]{1,0:T(8,128)(2,1)S(1)} %get-tuple-element.54.q_t_ref) | copy-start | bytes 2359300
  93.3 7.9 %copy-start.5 = (bf16[128,2048]{1,0:T(8,128)(2,1)}, bf16[128,2048]{1,0:T(8,128)(2,1)S(1)}, u32[]{:S(2)}) copy-start(bf16[128,2048]{1,0:T(8,128)(2,1)S(1)} %collective-permute-done.9.b_ref.refs_1_.refs_2_) | copy-start | bytes 1572868
  93.3 10.8 %copy-start.37 = (s32[8]{0:T(128)S(1)}, s32[8]{0:T(128)}, u32[]{:S(2)}) copy-start(s32[8]{0:T(128)} %constant.29.clone) | copy-start | bytes 100
  94.4 24.0 %collective-permute-start.10 = (bf16[256,2048]{1,0:T(8,128)(2,1)}, bf16[256,2048]{1,0:T(8,128)(2,1)}, u32[]{:S(2)}, u32[]{:S(2)}) collective-permute-start(bf16[256,2048]{1,0:T(8,128)(2,1)} %shard_map.155), channel_id=1, source_target_pairs={{1,2},{2,1},{5,6},{6,5},{9,10},{10,9},{13,14},{14,13},{17,18},{18,... | collective-permute-start | bytes 3145736 | tf_op jit(solution)/shard_map/ppermute | solution.py:471
  96.5 24.2 %collective-permute-start.7 = (bf16[256,2048]{1,0:T(8,128)(2,1)}, bf16[256,2048]{1,0:T(8,128)(2,1)}, u32[]{:S(2)}, u32[]{:S(2)}) collective-permute-start(bf16[256,2048]{1,0:T(8,128)(2,1)} %collective-permute-done.6.refs_3_.refs_2_), channel_id=1, source_target_pairs={{1,0},{2,3},{5,4},{6,7},{9,8},{10,11},{13,12},{14,15},{17,16},{18,... | collective-permute-start | bytes 3145736 | tf_op jit(solution)/shard_map/ppermute | solution.py:474
  101.2 39.7 %collective-permute-start.5 = (bf16[256,2048]{1,0:T(8,128)(2,1)}, bf16[256,2048]{1,0:T(8,128)(2,1)}, u32[]{:S(2)}, u32[]{:S(2)}) collective-permute-start(bf16[256,2048]{1,0:T(8,128)(2,1)} %shard_map.151), channel_id=1, source_target_pairs={{1,2},{2,1},{5,6},{6,5},{9,10},{10,9},{13,14},{14,13},{17,18},{18,... | collective-permute-start | bytes 3145736 | tf_op jit(solution)/shard_map/ppermute | solution.py:471
  118.5 24.2 %collective-permute-start.11 = (bf16[256,2048]{1,0:T(8,128)(2,1)}, bf16[256,2048]{1,0:T(8,128)(2,1)}, u32[]{:S(2)}, u32[]{:S(2)}) collective-permute-start(bf16[256,2048]{1,0:T(8,128)(2,1)} %collective-permute-done.10.refs_2_.refs_3_), channel_id=1, source_target_pairs={{1,0},{2,3},{5,4},{6,7},{9,8},{10,11},{13,12},{14,15},{17,16},{18,... | collective-permute-start | bytes 3145736 | tf_op jit(solution)/shard_map/ppermute | solution.py:474
  128.1 3.7 %copy-start = (bf16[6144,768]{1,0:T(8,128)(2,1)S(1)}, bf16[6144,768]{1,0:T(8,128)(2,1)}, u32[]{:S(2)}) copy-start(bf16[6144,768]{1,0:T(8,128)(2,1)} %all-gather.3.cloned.1.call-done) | copy-start | bytes 28311556
  133.9 13.0 %slice-start = ((s8[9437184]{0:T(1024)(128)(4,1)}), s8[4194304]{0:T(1024)(128)(4,1)S(1)}, s32[]{:S(2)}) async-start(s8[9437184]{0:T(1024)(128)(4,1)} %bitcast.9), calls=%async_computation.1 | async-start | bytes 8388608
  133.9 13.0 %slice-start.1 = ((s8[9437184]{0:T(1024)(128)(4,1)}), s8[4194304]{0:T(1024)(128)(4,1)S(1)}, s32[]{:S(2)}) async-start(s8[9437184]{0:T(1024)(128)(4,1)} %bitcast.9), calls=%async_computation.2 | async-start | bytes 8388608
  140.9 6.0 %slice-start.2 = ((s8[9437184]{0:T(1024)(128)(4,1)}), s8[1048576]{0:T(1024)(128)(4,1)S(1)}, s32[]{:S(2)}) async-start(s8[9437184]{0:T(1024)(128)(4,1)} %bitcast.9), calls=%async_computation.3 | async-start | bytes 2097152
  141.0 22.1 %collective-permute-start.8 = (bf16[256,2048]{1,0:T(8,128)(2,1)}, bf16[256,2048]{1,0:T(8,128)(2,1)S(1)}, u32[]{:S(2)}, u32[]{:S(2)}) collective-permute-start(bf16[256,2048]{1,0:T(8,128)(2,1)} %shard_map.154.refs_2_.refs_3_), channel_id=1, source_target_pairs={{1,0},{2,3},{5,4},{6,7},{9,8},{10,11},{13,12},{14,15},{17,16},{18,... | collective-permute-start | bytes 3145736 | tf_op jit(solution)/shard_map/ppermute | solution.py:474
  147.0 3.7 %copy-start.2 = (bf16[4,768,384]{2,1,0:T(8,128)(2,1)S(1)}, bf16[4,768,384]{2,1,0:T(8,128)(2,1)}, u32[]{:S(2)}) copy-start(bf16[4,768,384]{2,1,0:T(8,128)(2,1)} %copy-done.1) | copy-start | bytes 7077892
  150.7 12.3 %copy-start.16 = (bf16[128,2048]{1,0:T(8,128)(2,1)S(1)}, bf16[128,2048]{1,0:T(8,128)(2,1)}, u32[]{:S(2)}) copy-start(bf16[128,2048]{1,0:T(8,128)(2,1)} %copy-done.15) | copy-start | bytes 1572868
  166.8 8.0 %collective-permute-start.13 = (bf16[4,768,384]{2,1,0:T(8,128)(2,1)S(1)}, bf16[4,768,384]{2,1,0:T(8,128)(2,1)S(1)}, u32[]{:S(2)}, u32[]{:S(2)}) collective-permute-start(bf16[4,768,384]{2,1,0:T(8,128)(2,1)S(1)} %get-tuple-element.60), channel_id=1, source_target_pairs={{0,4},{4,0},{8,12},{12,8},{16,20},{20,16},{24,28},{28,24},{1,5},{5... | collective-permute-start | bytes 7077896 | tf_op jit(solution)/shard_map/ppermute | solution.py:447
  170.6 7.5 %collective-permute-start.12 = (bf16[4,768,384]{2,1,0:T(8,128)(2,1)S(1)}, bf16[4,768,384]{2,1,0:T(8,128)(2,1)S(1)}, u32[]{:S(2)}, u32[]{:S(2)}) collective-permute-start(bf16[4,768,384]{2,1,0:T(8,128)(2,1)S(1)} %shard_map.161), channel_id=1, source_target_pairs={{0,4},{4,0},{8,12},{12,8},{16,20},{20,16},{24,28},{28,24},{1,5},{5... | collective-permute-start | bytes 7077896 | tf_op jit(solution)/shard_map/ppermute | solution.py:447
  170.7 7.4 %copy-start.18 = (bf16[6,512,512]{2,1,0:T(8,128)(2,1)S(1)}, bf16[6,512,512]{2,1,0:T(8,128)(2,1)}, u32[]{:S(2)}) copy-start(bf16[6,512,512]{2,1,0:T(8,128)(2,1)} %copy-done.17) | copy-start | bytes 9437188
  170.7 7.5 %copy-start.25 = (bf16[512,768]{1,0:T(8,128)(2,1)S(1)}, bf16[512,768]{1,0:T(8,128)(2,1)}, u32[]{:S(2)}) copy-start(bf16[512,768]{1,0:T(8,128)(2,1)} %get-tuple-element.44.att_ref) | copy-start | bytes 2359300
  170.7 7.5 %copy-start.27 = (bf16[768,512]{1,0:T(8,128)(2,1)S(1)}, bf16[768,512]{1,0:T(8,128)(2,1)}, u32[]{:S(2)}) copy-start(bf16[768,512]{1,0:T(8,128)(2,1)} %copy-done.26) | copy-start | bytes 2359300
  170.7 7.5 %copy-start.29 = (bf16[512,768]{1,0:T(8,128)(2,1)S(1)}, bf16[512,768]{1,0:T(8,128)(2,1)}, u32[]{:S(2)}) copy-start(bf16[512,768]{1,0:T(8,128)(2,1)} %copy-done.28) | copy-start | bytes 2359300
  170.7 7.5 %copy-start.31 = (bf16[512,768]{1,0:T(8,128)(2,1)S(1)}, bf16[512,768]{1,0:T(8,128)(2,1)}, u32[]{:S(2)}) copy-start(bf16[512,768]{1,0:T(8,128)(2,1)} %copy-done.30) | copy-start | bytes 2359300
  185.0 27.2 %collective-permute-start.19 = (bf16[2,768,384]{2,1,0:T(8,128)(2,1)S(1)}, bf16[2,768,384]{2,1,0:T(8,128)(2,1)S(1)}, u32[]{:S(2)}, u32[]{:S(2)}) collective-permute-start(bf16[2,768,384]{2,1,0:T(8,128)(2,1)S(1)} %get-tuple-element.74), channel_id=1, source_target_pairs={{0,16},{4,20},{8,24},{12,28},{16,0},{20,4},{24,8},{28,12},{1,17},{... | collective-permute-start | bytes 3538952 | tf_op jit(solution)/shard_map/ppermute | solution.py:447
  186.3 27.5 %collective-permute-start.17 = (bf16[2,768,384]{2,1,0:T(8,128)(2,1)S(1)}, bf16[2,768,384]{2,1,0:T(8,128)(2,1)S(1)}, u32[]{:S(2)}, u32[]{:S(2)}) collective-permute-start(bf16[2,768,384]{2,1,0:T(8,128)(2,1)S(1)} %get-tuple-element.72), channel_id=1, source_target_pairs={{0,8},{4,12},{8,0},{12,4},{16,24},{20,28},{24,16},{28,20},{1,9},{5... | collective-permute-start | bytes 3538952 | tf_op jit(solution)/shard_map/ppermute | solution.py:447
  187.5 41.9 %collective-permute-start.14 = (bf16[3,128,768]{2,1,0:T(8,128)(2,1)S(1)}, bf16[3,128,768]{2,1,0:T(8,128)(2,1)S(1)}, u32[]{:S(2)}, u32[]{:S(2)}) collective-permute-start(bf16[3,128,768]{2,1,0:T(8,128)(2,1)S(1)} %get-tuple-element.61), channel_id=1, source_target_pairs={{0,2},{1,3},{2,0},{3,1},{4,6},{5,7},{6,4},{7,5},{8,10},{9,11},{10,... | collective-permute-start | bytes 1769480 | tf_op jit(solution)/shard_map/ppermute | solution.py:447
  190.3 51.8 %collective-permute-start.15 = (bf16[3,128,768]{2,1,0:T(8,128)(2,1)S(1)}, bf16[3,128,768]{2,1,0:T(8,128)(2,1)S(1)}, u32[]{:S(2)}, u32[]{:S(2)}) collective-permute-start(bf16[3,128,768]{2,1,0:T(8,128)(2,1)S(1)} %get-tuple-element.62), channel_id=1, source_target_pairs={{0,3},{1,2},{2,1},{3,0},{4,7},{5,6},{6,5},{7,4},{8,11},{9,10},{10,... | collective-permute-start | bytes 1769480 | tf_op jit(solution)/shard_map/ppermute | solution.py:447
  190.8 36.6 %collective-permute-start.16 = (bf16[3,128,768]{2,1,0:T(8,128)(2,1)S(1)}, bf16[3,128,768]{2,1,0:T(8,128)(2,1)S(1)}, u32[]{:S(2)}, u32[]{:S(2)}) collective-permute-start(bf16[3,128,768]{2,1,0:T(8,128)(2,1)S(1)} %get-tuple-element.64), channel_id=1, source_target_pairs={{0,1},{1,0},{2,3},{3,2},{4,5},{5,4},{6,7},{7,6},{8,9},{9,8},{10,11... | collective-permute-start | bytes 1769480 | tf_op jit(solution)/shard_map/ppermute | solution.py:447
  212.6 31.2 %collective-permute-start.20 = (bf16[1,768,384]{2,1,0:T(8,128)(2,1)S(1)}, bf16[1,768,384]{2,1,0:T(8,128)(2,1)S(1)}, u32[]{:S(2)}, u32[]{:S(2)}) collective-permute-start(bf16[1,768,384]{2,1,0:T(8,128)(2,1)S(1)} %slice.46), channel_id=1, source_target_pairs={{0,8},{4,12},{8,0},{12,4},{16,24},{20,28},{24,16},{28,20},{1,9},{5... | collective-permute-start | bytes 1769480 | tf_op jit(solution)/shard_map/ppermute | solution.py:447
  214.2 29.8 %collective-permute-start.18 = (bf16[1,768,384]{2,1,0:T(8,128)(2,1)S(1)}, bf16[1,768,384]{2,1,0:T(8,128)(2,1)S(1)}, u32[]{:S(2)}, u32[]{:S(2)}) collective-permute-start(bf16[1,768,384]{2,1,0:T(8,128)(2,1)S(1)} %slice.47), channel_id=1, source_target_pairs={{0,16},{4,20},{8,24},{12,28},{16,0},{20,4},{24,8},{28,12},{1,17},{... | collective-permute-start | bytes 1769480 | tf_op jit(solution)/shard_map/ppermute | solution.py:447
  (15 other events, 18.2 us)
Sparse Core Ops, SparseCore 0:
  9.9 60.4 all-gather.2

commit v5 on v4

--- a/solution.py
+++ b/solution.py
@@ -70,8 +70,8 @@
             out[i] = ins[3 * s + i][0]
 
 
-def pack(table, partners, q, k, v, after=()):
-    group = table.shape[0] // 3
+def pack(place, partners, q, k, v, after=()):
+    group = place.shape[0]
     rows, total = q.shape[1:]
     shape = (3, rows, total // group)
     in_specs = []
@@ -90,7 +90,7 @@
         ),
         cost_estimate=light(),
         compiler_params=params(60),
-    )(table, *[q, k, v] * len(partners), *after)
+    )(place, *[q, k, v] * len(partners), *after)
 
 
 def split_kernel(dp, g_ref, *outs):
@@ -496,11 +496,14 @@
         return jnp.bitwise_xor(lax.axis_index("dp"), jnp.array(half_order(order), jnp.int32))
 
     arrays = (query_rows, key_rows, value_rows)
-    packed = pack(table, range(1, group), *arrays)
+    place = jnp.bitwise_xor(lax.axis_index("head"), jnp.arange(group, dtype=jnp.int32))
+    packed = pack(place, range(1, group), *arrays)
     parts = [swap(rows, "head", group, 1 + i) for i, rows in enumerate(packed)]
-    parts = list(pack(table, [0], *arrays, after=parts[:1])) + parts
+    parts = list(pack(place, [0], *arrays, after=parts[:1])) + parts
     pieces = split(out_grad, dp)
-    nears = [swap(own, "head", group, 1) for own in pieces] if group == 4 else pieces
+    nears = [swap(own, "head", group, 1) for own in pieces[:2]] if group == 4 else pieces
+    if group == 4:
+        nears.append(swap(hold(pieces[2], [nears[1]]), "head", group, 1))
     both = join(pieces[0], nears[0], after=parts[1:])
     weights_full = lax.all_gather(out_weight, "dp", axis=0)
 

time: 253 us -> 251 us (level)
  local copies, waits for them, and re-layouts: 17.2 us -> 21.2 us
  waiting for transfers between devices: 128 us -> 124 us
    unnamed x82 -> x95, local copies, waits for them, and re-layouts: 16.8 us -> 20.8 us
  transfers between devices with their start and end apart: 22 -> 22, of which waited for: 11 -> 11; matrix products, arithmetic and copies ran while one was open for 1% -> 1% of each run, Pallas kernels for 18% -> 17%
where the time goes in v5:
time: 251 us; the launch traced here: 250 us
  waiting for transfers between devices  124 us (49%)
  Pallas kernels  54.1 us (22%)
  starting transfers between devices  33.3 us (13%)
  local copies, waits for them, and re-layouts  21.2 us (8%)
  between operations  14.5 us (6%)
  other arithmetic  2.74 us (1%)
    ppermute x15, waiting for transfers between devices, swap(): return lax.ppermute(value, axis, [(i, i ^ mask) for i in range(size)])  99.3 us
    unnamed x95, local copies, waits for them, and re-layouts  20.8 us
    ppermute x15, starting transfers between devices, swap(): return lax.ppermute(value, axis, [(i, i ^ mask) for i in range(size)])  17.8 us
    ppermute x3, waiting for transfers between devices, gather_rows(): lax.ppermute(join(own, near) if both is None else both, 'head', [(1, 2),...  17.5 us
    pallas_call x4, Pallas kernels, outer(): pl.pallas_call(functools.partial(outer_kernel, len(rows), start, len(pass...  15.6 us
    pallas_call x3, Pallas kernels, project(): pl.pallas_call(functools.partial(project_kernel, len(rows), len(at), not...  10.5 us
    ppermute x3, starting transfers between devices, gather_rows(): lax.ppermute(join(own, near) if both is None else both, 'head', [(1, 2),...  9.98 us
    pallas_call x1, Pallas kernels, forward(): pl.pallas_call(functools.partial(forward_kernel, group), out_shape=[jax.S...  7.93 us
  transfers between devices with their start and end apart: 22, of which 11 were waited for; matrix products, arithmetic and copies ran while one was open for 1% of the time, Pallas kernels for 17%

profile of v5, /device:TPU:9, one launch (start us, length us, event | category | flops | bytes accessed | tf_op | source)
XLA Modules:
  0.0 250.3 jit_solution(8799377209010124627)
XLA Ops:
  8.5 3.4 %shard_map.146 = (bf16[3,128,768]{2,1,0:T(8,128)(2,1)}, bf16[3,128,768]{2,1,0:T(8,128)(2,1)}, bf16[3,128,768]{2,1,0:T(8,128)(2,1)}) custom-call(s32[4]{0:T(128)} %iota_xor_fusion.table, bf16[1,128,3072]{2,1,0:T(8,128)(2,1)} %refs_0_.3, bf16[1,128,3072]{2,1,0:T(8,128)(2,1)} %refs_1_.3, bf16[1,128,3072]{2,1,0:T(8,128)(2,1)} %refs_2_.3, ...), custom_call_target="tpu_custom_call" | custom-call | flops 1 | bytes 1 | tf_op jit(solution)/shard_map/pallas_call | solution.py:82
  11.9 2.5 collective-permute-start.1
  14.6 1.4 copy-done.29
  16.1 1.2 collective-permute-start.3
  17.7 45.4 %collective-permute-done.3.b_ref.refs_2_.refs_1_ = bf16[128,2048]{1,0:T(8,128)(2,1)S(1)} collective-permute-done((bf16[128,2048]{1,0:T(8,128)(2,1)S(1)}, bf16[128,2048]{1,0:T(8,128)(2,1)S(1)}, u32[]{:S(2)}, u32[]{:S(2)}) %collective-permute-start.3) | collective-permute-done | bytes 524320 | tf_op jit(solution)/shard_map/ppermute | solution.py:447
  63.1 2.3 collective-permute-done.2.refs_2_.refs_3_
  65.3 1.1 shard_map.149.refs_4_
  67.3 3.3 %collective-permute-start.7 = (bf16[256,2048]{1,0:T(8,128)(2,1)}, bf16[256,2048]{1,0:T(8,128)(2,1)}, u32[]{:S(2)}, u32[]{:S(2)}) collective-permute-start(bf16[256,2048]{1,0:T(8,128)(2,1)} %shard_map.149.refs_4_), channel_id=1, source_target_pairs={{1,2},{2,1},{5,6},{6,5},{9,10},{10,9},{13,14},{14,13},{17,18},{18,... | collective-permute-start | bytes 3145736 | tf_op jit(solution)/shard_map/ppermute | solution.py:471
  71.9 2.3 collective-permute-done.4.refs_1_.b_ref.refs_2_
  74.6 2.6 %shard_map.147.refs_0_ = bf16[3,128,768]{2,1,0:T(8,128)(2,1)} custom-call(s32[4]{0:T(128)} %iota_xor_fusion.table, bf16[1,128,3072]{2,1,0:T(8,128)(2,1)} %refs_0_.3, bf16[1,128,3072]{2,1,0:T(8,128)(2,1)} %refs_1_.3, bf16[1,128,3072]{2,1,0:T(8,128)(2,1)} %refs_2_.3, bf16[3,128,768]{2,1,0:T(8,128)(2,1)} %copy-done.9), custom_call_target="tpu_custom_call" | custom-call | flops 1 | bytes 1 | tf_op jit(solution)/shard_map/pallas_call | solution.py:82
  77.2 1.1 copy-done.25
  78.3 1.1 copy-done.27
  79.3 1.1 copy-done.28
  80.4 7.9 %shard_map.150 = (bf16[512,768]{1,0:T(8,128)(2,1)}, bf16[768,512]{1,0:T(8,128)(2,1)S(1)}, bf16[6,512,512]{2,1,0:T(8,128)(2,1)S(1)}, bf16[768,512]{1,0:T(8,128)(2...) custom-call(s32[12]{0:T(128)S(1)} %pad_add_fusion.table.place, s32[1,512]{1,0:T(1,128)S(1)} %copy-done.37, ...), custom_call_target="tpu_custom_call" | custom-call | flops 1 | bytes 1 | tf_op jit(solution)/shard_map/pallas_call | solution.py:251
  90.1 1.1 shard_map.156
  91.2 4.2 %collective-permute-start.10 = (bf16[256,2048]{1,0:T(8,128)(2,1)}, bf16[256,2048]{1,0:T(8,128)(2,1)}, u32[]{:S(2)}, u32[]{:S(2)}) collective-permute-start(bf16[256,2048]{1,0:T(8,128)(2,1)} %shard_map.156), channel_id=1, source_target_pairs={{1,2},{2,1},{5,6},{6,5},{9,10},{10,9},{13,14},{14,13},{17,18},{18,... | collective-permute-start | bytes 3145736 | tf_op jit(solution)/shard_map/ppermute | solution.py:471
  95.4 1.4 collective-permute-start.8
  96.8 1.1 shard_map.152
  98.0 2.5 collective-permute-start.6
  100.5 16.9 %collective-permute-done.10.refs_2_.refs_3_ = bf16[256,2048]{1,0:T(8,128)(2,1)} collective-permute-done((bf16[256,2048]{1,0:T(8,128)(2,1)}, bf16[256,2048]{1,0:T(8,128)(2,1)}, u32[]{:S(2)}, u32[]{:S(2)}) %collective-permute-start.10) | collective-permute-done | bytes 1048608 | tf_op jit(solution)/shard_map/ppermute | solution.py:471
  117.4 2.2 collective-permute-start.11
  122.7 1.2 copy-done.20
  123.9 3.6 %shard_map.154 = (bf16[4,768,384]{2,1,0:T(8,128)(2,1)S(1)}, bf16[4,768,384]{2,1,0:T(8,128)(2,1)S(1)}) custom-call(s32[8]{0:T(128)S(1)} %broadcast_xor_fusion.1.blocks, bf16[768,512]{1,0:T(8,128)(2,1)S(1)} %get-tuple-element.47.att_t_ref.refs_0_, bf16[128,2048]{1,0:T(8,128)(2,1)S(1)} %copy-done.12, bf16[128,2048]{1,0:T(8,128)(2,1)S(1)} %copy-done.15, ...), custom_call_target="tpu_custom_call" | custom-call | flops 1 | bytes 1 | tf_op jit(solution)/shard_map/pallas_call | solution.py:430
  127.5 1.4 copy-done.3
  128.9 3.7 %copy-done = bf16[6144,768]{1,0:T(8,128)(2,1)S(1)} copy-done((bf16[6144,768]{1,0:T(8,128)(2,1)S(1)}, bf16[6144,768]{1,0:T(8,128)(2,1)}, u32[]{:S(2)}) %copy-start) | copy-done | bytes 9437208
  134.7 1.2 copy-done.21
  135.9 3.4 %shard_map.153.refs_1_.refs_5_ = f32[512,768]{1,0:T(8,128)S(1)} custom-call(bf16[8,768,768]{2,1,0:T(8,128)(2,1)S(1)} %bitcast.8, bf16[128,2048]{1,0:T(8,128)(2,1)S(1)} %copy-done.13, bf16[128,2048]{1,0:T(8,128)(2,1)S(1)} %copy-done.16, bf16[256,2048]{1,0:T(8,128)(2,1)} %collective-permute-done.7.refs_3_.refs_2_, bf16[256,2048]{1,0:T(8,128)(2,1)S(1)} %copy-done.21), custom_call_target="tpu_custom_call" | custom-call | flops 1 | bytes 1 | tf_op jit(solution)/shard_map/pallas_call | solution.py:396
  139.9 1.9 collective-permute-start.9
  141.9 4.2 %shard_map.157 = (bf16[4,768,384]{2,1,0:T(8,128)(2,1)S(1)}, bf16[4,768,384]{2,1,0:T(8,128)(2,1)S(1)}) custom-call(s32[8]{0:T(128)S(1)} %broadcast_xor_fusion.blocks, bf16[768,512]{1,0:T(8,128)(2,1)S(1)} %get-tuple-element.47.att_t_ref.refs_0_, bf16[128,2048]{1,0:T(8,128)(2,1)S(1)} %copy-done.6, bf16[128,2048]{1,0:T(8,128)(2,1)S(1)} %copy-done.2, ...), custom_call_target="tpu_custom_call" | custom-call | flops 1 | bytes 1 | tf_op jit(solution)/shard_map/pallas_call | solution.py:430
  146.1 3.7 %shard_map.158.refs_6_ = f32[512,768]{1,0:T(8,128)S(1)} custom-call(bf16[8,768,768]{2,1,0:T(8,128)(2,1)S(1)} %bitcast.11, bf16[128,2048]{1,0:T(8,128)(2,1)S(1)} %copy-done.6, bf16[128,2048]{1,0:T(8,128)(2,1)S(1)} %copy-done.2, bf16[256,2048]{1,0:T(8,128)(2,1)} %collective-permute-done.10.refs_2_.refs_3_, ...), custom_call_target="tpu_custom_call" | custom-call | flops 1 | bytes 1 | tf_op jit(solution)/shard_map/pallas_call | solution.py:396
  149.9 4.2 %shard_map.161 = (bf16[4,768,384]{2,1,0:T(8,128)(2,1)S(1)}, bf16[4,768,384]{2,1,0:T(8,128)(2,1)S(1)}) custom-call(s32[8]{0:T(128)S(1)} %broadcast_xor_fusion.1.blocks, bf16[768,512]{1,0:T(8,128)(2,1)S(1)} %get-tuple-element.47.att_t_ref.refs_0_, bf16[128,2048]{1,0:T(8,128)(2,1)S(1)} %copy-done.6, ...), custom_call_target="tpu_custom_call", output_to_operand_aliasing={{0}: (6, {}), {1}: (7, {})} | custom-call | flops 1 | bytes 1 | tf_op jit(solution)/shard_map/pallas_call | solution.py:430
  154.1 6.9 %collective-permute-done.9.refs_3_.refs_4_.refs_1_ = bf16[256,2048]{1,0:T(8,128)(2,1)S(1)} collective-permute-done((bf16[256,2048]{1,0:T(8,128)(2,1)}, bf16[256,2048]{1,0:T(8,128)(2,1)S(1)}, u32[]{:S(2)}, u32[]{:S(2)}) %collective-permute-start.9) | collective-permute-done | bytes 1048608 | tf_op jit(solution)/shard_map/ppermute | solution.py:474
  161.0 3.6 %shard_map.159 = (bf16[4,768,384]{2,1,0:T(8,128)(2,1)S(1)}, bf16[4,768,384]{2,1,0:T(8,128)(2,1)S(1)}, f32[512,768]{1,0:T(8,128)S(1)}) custom-call(s32[8]{0:T(128)S(1)} %broadcast_xor_fusion.blocks, bf16[768,512]{1,0:T(8,128)(2,1)S(1)} %get-tuple-element.47.att_t_ref.refs_0_, ...), custom_call_target="tpu_custom_call", output_to_operand_aliasing={{0}: (6, {}), {1}: (7, {}), {2}: (8, {})} | custom-call | flops 1 | bytes 1 | tf_op jit(solution)/shard_map/pallas_call | solution.py:430
  164.6 4.4 %collective-permute-start.13 = (bf16[4,768,384]{2,1,0:T(8,128)(2,1)S(1)}, bf16[4,768,384]{2,1,0:T(8,128)(2,1)S(1)}, u32[]{:S(2)}, u32[]{:S(2)}) collective-permute-start(bf16[4,768,384]{2,1,0:T(8,128)(2,1)S(1)} %get-tuple-element.60), channel_id=1, source_target_pairs={{0,4},{4,0},{8,12},{12,8},{16,20},{20,16},{24,28},{28,24},{1,5},{5... | collective-permute-start | bytes 7077896 | tf_op jit(solution)/shard_map/ppermute | solution.py:447
  169.1 3.4 %shard_map.160.g_ref = bf16[512,768]{1,0:T(8,128)(2,1)S(1)} custom-call(bf16[8,768,768]{2,1,0:T(8,128)(2,1)S(1)} %bitcast.12, bf16[128,2048]{1,0:T(8,128)(2,1)S(1)} %copy-done.8, bf16[128,2048]{1,0:T(8,128)(2,1)S(1)} %copy-done.18, bf16[256,2048]{1,0:T(8,128)(2,1)} %shard_map.155.refs_2_.refs_3_, ...), custom_call_target="tpu_custom_call" | custom-call | flops 1 | bytes 1 | tf_op jit(solution)/shard_map/pallas_call | solution.py:396
  173.2 3.4 %collective-permute-done.12.refs_1_ = bf16[4,768,384]{2,1,0:T(8,128)(2,1)S(1)} collective-permute-done((bf16[4,768,384]{2,1,0:T(8,128)(2,1)S(1)}, bf16[4,768,384]{2,1,0:T(8,128)(2,1)S(1)}, u32[]{:S(2)}, u32[]{:S(2)}) %collective-permute-start.12) | collective-permute-done | bytes 2359328 | tf_op jit(solution)/shard_map/ppermute | solution.py:447
  176.6 6.9 %shard_map.163 = (bf16[3,128,768]{2,1,0:T(8,128)(2,1)S(1)}, bf16[3,128,768]{2,1,0:T(8,128)(2,1)S(1)}, bf16[3,128,768]{2,1,0:T(8,128)(2,1)S(1)}, bf16[3,128,768]{...) custom-call(s32[12]{0:T(128)S(1)} %pad_add_fusion.table.place, ...), custom_call_target="tpu_custom_call" | custom-call | flops 1 | bytes 1 | tf_op jit(solution)/shard_map/pallas_call | solution.py:337
  183.4 1.3 collective-permute-start.19
  184.7 1.2 collective-permute-start.17
  185.9 2.6 %collective-permute-start.14 = (bf16[3,128,768]{2,1,0:T(8,128)(2,1)S(1)}, bf16[3,128,768]{2,1,0:T(8,128)(2,1)S(1)}, u32[]{:S(2)}, u32[]{:S(2)}) collective-permute-start(bf16[3,128,768]{2,1,0:T(8,128)(2,1)S(1)} %get-tuple-element.61), channel_id=1, source_target_pairs={{0,2},{1,3},{2,0},{3,1},{4,6},{5,7},{6,4},{7,5},{8,10},{9,11},{10,... | collective-permute-start | bytes 1769480 | tf_op jit(solution)/shard_map/ppermute | solution.py:447
  189.7 20.9 %collective-permute-done.19 = bf16[2,768,384]{2,1,0:T(8,128)(2,1)S(1)} collective-permute-done((bf16[2,768,384]{2,1,0:T(8,128)(2,1)S(1)}, bf16[2,768,384]{2,1,0:T(8,128)(2,1)S(1)}, u32[]{:S(2)}, u32[]{:S(2)}) %collective-permute-start.19) | collective-permute-done | bytes 1179680 | tf_op jit(solution)/shard_map/ppermute | solution.py:447
  211.0 1.3 collective-permute-start.20
  212.6 1.3 collective-permute-start.18
  213.9 12.1 %collective-permute-done.16.refs_1_ = bf16[3,128,768]{2,1,0:T(8,128)(2,1)S(1)} collective-permute-done((bf16[3,128,768]{2,1,0:T(8,128)(2,1)S(1)}, bf16[3,128,768]{2,1,0:T(8,128)(2,1)S(1)}, u32[]{:S(2)}, u32[]{:S(2)}) %collective-permute-start.16) | collective-permute-done | bytes 589856 | tf_op jit(solution)/shard_map/ppermute | solution.py:447
  225.9 2.0 shard_map.164
  228.0 12.3 %collective-permute-done.15.refs_1_ = bf16[3,128,768]{2,1,0:T(8,128)(2,1)S(1)} collective-permute-done((bf16[3,128,768]{2,1,0:T(8,128)(2,1)S(1)}, bf16[3,128,768]{2,1,0:T(8,128)(2,1)S(1)}, u32[]{:S(2)}, u32[]{:S(2)}) %collective-permute-start.15) | collective-permute-done | bytes 589856 | tf_op jit(solution)/shard_map/ppermute | solution.py:447
  240.3 1.7 shard_map.165
  242.3 1.1 pad_maximum_fusion
  (133 shorter events, 14.8 us)
Async XLA Ops:
  7.2 121.7 %all-gather.3.cloned.1.call-start = ((), (), s32[]{:S(2)}) async-start(), calls=%async_computation | async-start | bytes 10616832 | tf_op jit(solution)/shard_map/all_gather | solution.py:508
  11.9 51.1 %collective-permute-start = (bf16[3,128,768]{2,1,0:T(8,128)(2,1)}, bf16[3,128,768]{2,1,0:T(8,128)(2,1)S(1)}, u32[]{:S(2)}, u32[]{:S(2)}) collective-permute-start(bf16[3,128,768]{2,1,0:T(8,128)(2,1)} %get-tuple-element.40), channel_id=1, source_target_pairs={{0,1},{1,0},{2,3},{3,2},{4,5},{5,4},{6,7},{7,6},{8,9},{9,8},{10,11... | collective-permute-start | bytes 1769480 | tf_op jit(solution)/shard_map/ppermute | solution.py:447
  11.9 51.1 %collective-permute-start.1 = (bf16[3,128,768]{2,1,0:T(8,128)(2,1)}, bf16[3,128,768]{2,1,0:T(8,128)(2,1)S(1)}, u32[]{:S(2)}, u32[]{:S(2)}) collective-permute-start(bf16[3,128,768]{2,1,0:T(8,128)(2,1)} %get-tuple-element.41), channel_id=1, source_target_pairs={{0,2},{1,3},{2,0},{3,1},{4,6},{5,7},{6,4},{7,5},{8,10},{9,11},{10,... | collective-permute-start | bytes 1769480 | tf_op jit(solution)/shard_map/ppermute | solution.py:447
  14.4 50.9 %collective-permute-start.2 = (bf16[3,128,768]{2,1,0:T(8,128)(2,1)}, bf16[3,128,768]{2,1,0:T(8,128)(2,1)S(1)}, u32[]{:S(2)}, u32[]{:S(2)}) collective-permute-start(bf16[3,128,768]{2,1,0:T(8,128)(2,1)} %get-tuple-element.42), channel_id=1, source_target_pairs={{0,3},{1,2},{2,1},{3,0},{4,7},{5,6},{6,5},{7,4},{8,11},{9,10},{10,... | collective-permute-start | bytes 1769480 | tf_op jit(solution)/shard_map/ppermute | solution.py:447
  16.0 54.7 %copy-start.40 = (s32[1,6,4]{1,2,0:T(4,128)S(1)}, s32[1,6,4]{1,2,0:T(4,128)}, u32[]{:S(2)}) copy-start(s32[1,6,4]{1,2,0:T(4,128)} %param.18) | copy-start | bytes 292
  16.0 54.8 %copy-start.38 = (s32[1,6,4,4]{1,3,2,0:T(4,128)S(1)}, s32[1,6,4,4]{1,3,2,0:T(4,128)}, u32[]{:S(2)}) copy-start(s32[1,6,4,4]{1,3,2,0:T(4,128)} %param.17) | copy-start | bytes 1156
  16.1 74.0 %copy-start.5 = (bf16[128,2048]{1,0:T(8,128)(2,1)}, bf16[128,2048]{1,0:T(8,128)(2,1)S(1)}, u32[]{:S(2)}) copy-start(bf16[128,2048]{1,0:T(8,128)(2,1)S(1)} %get-tuple-element.46.a_ref.refs_0_.refs_1_) | copy-start | bytes 1572868
  16.1 80.7 %copy-start.7 = (bf16[128,2048]{1,0:T(8,128)(2,1)}, bf16[128,2048]{1,0:T(8,128)(2,1)S(1)}, u32[]{:S(2)}) copy-start(bf16[128,2048]{1,0:T(8,128)(2,1)S(1)} %get-tuple-element.45.a_ref.refs_0_.refs_1_) | copy-start | bytes 1572868
  16.1 46.9 %collective-permute-start.3 = (bf16[128,2048]{1,0:T(8,128)(2,1)S(1)}, bf16[128,2048]{1,0:T(8,128)(2,1)S(1)}, u32[]{:S(2)}, u32[]{:S(2)}) collective-permute-start(bf16[128,2048]{1,0:T(8,128)(2,1)S(1)} %get-tuple-element.43.a_ref.refs_1_.refs_0_), channel_id=1, source_target_pairs={{0,1},{1,0},{2,3},{3,2},{4,5},{5,4},{6,7},{7,6},{8,9},{9,8},{10,11... | collective-permute-start | bytes 1572872 | tf_op jit(solution)/shard_map/ppermute | solution.py:447
  17.3 56.8 %collective-permute-start.4 = (bf16[128,2048]{1,0:T(8,128)(2,1)S(1)}, bf16[128,2048]{1,0:T(8,128)(2,1)S(1)}, u32[]{:S(2)}, u32[]{:S(2)}) collective-permute-start(bf16[128,2048]{1,0:T(8,128)(2,1)S(1)} %get-tuple-element.46.a_ref.refs_0_.refs_1_), channel_id=1, source_target_pairs={{0,1},{1,0},{2,3},{3,2},{4,5},{5,4},{6,7},{7,6},{8,9},{9,8},{10,11... | collective-permute-start | bytes 1572872 | tf_op jit(solution)/shard_map/ppermute | solution.py:447
  63.0 3.4 %copy-start.14 = (bf16[128,2048]{1,0:T(8,128)(2,1)}, bf16[128,2048]{1,0:T(8,128)(2,1)S(1)}, u32[]{:S(2)}) copy-start(bf16[128,2048]{1,0:T(8,128)(2,1)S(1)} %collective-permute-done.3.b_ref.refs_2_.refs_1_) | copy-start | bytes 1572868
  63.0 8.6 %copy-start.9 = (bf16[3,128,768]{2,1,0:T(8,128)(2,1)}, bf16[3,128,768]{2,1,0:T(8,128)(2,1)S(1)}, u32[]{:S(2)}) copy-start(bf16[3,128,768]{2,1,0:T(8,128)(2,1)S(1)} %collective-permute-done.refs_3_.refs_0_.refs_1_) | copy-start | bytes 1769476
  67.3 7.2 %copy-start.41 = (s32[4]{0:T(128)S(1)}, s32[4]{0:T(128)}, u32[]{:S(2)}) copy-start(s32[4]{0:T(128)} %constant.28.clone) | copy-start | bytes 52
  67.3 7.2 %copy-start.39 = (s32[4]{0:T(128)S(1)}, s32[4]{0:T(128)}, u32[]{:S(2)}) copy-start(s32[4]{0:T(128)} %iota_xor_fusion.table) | copy-start | bytes 52
  67.3 28.1 %collective-permute-start.7 = (bf16[256,2048]{1,0:T(8,128)(2,1)}, bf16[256,2048]{1,0:T(8,128)(2,1)}, u32[]{:S(2)}, u32[]{:S(2)}) collective-permute-start(bf16[256,2048]{1,0:T(8,128)(2,1)} %shard_map.149.refs_4_), channel_id=1, source_target_pairs={{1,2},{2,1},{5,6},{6,5},{9,10},{10,9},{13,14},{14,13},{17,18},{18,... | collective-permute-start | bytes 3145736 | tf_op jit(solution)/shard_map/ppermute | solution.py:471
  71.9 5.3 %copy-start.10 = (bf16[3,128,768]{2,1,0:T(8,128)(2,1)S(1)}, bf16[3,128,768]{2,1,0:T(8,128)(2,1)}, u32[]{:S(2)}) copy-start(bf16[3,128,768]{2,1,0:T(8,128)(2,1)} %copy-done.9) | copy-start | bytes 1769476
  71.9 5.3 %copy-start.37 = (s32[1,512]{1,0:T(1,128)S(1)}, s32[1,512]{1,0:T(1,128)}, u32[]{:S(2)}) copy-start(s32[1,512]{1,0:T(1,128)} %order_ref.1) | copy-start | bytes 6148
  74.2 15.9 %copy-start.1 = (bf16[128,2048]{1,0:T(8,128)(2,1)}, bf16[128,2048]{1,0:T(8,128)(2,1)S(1)}, u32[]{:S(2)}) copy-start(bf16[128,2048]{1,0:T(8,128)(2,1)S(1)} %collective-permute-done.4.refs_1_.b_ref.refs_2_) | copy-start | bytes 1572868
  74.2 22.6 %collective-permute-start.5 = (bf16[128,2048]{1,0:T(8,128)(2,1)}, bf16[128,2048]{1,0:T(8,128)(2,1)S(1)}, u32[]{:S(2)}, u32[]{:S(2)}) collective-permute-start(bf16[128,2048]{1,0:T(8,128)(2,1)} %shard_map.151), channel_id=1, source_target_pairs={{0,1},{1,0},{2,3},{3,2},{4,5},{5,4},{6,7},{7,6},{8,9},{9,8},{10,11... | collective-permute-start | bytes 1572872 | tf_op jit(solution)/shard_map/ppermute | solution.py:447
  90.1 7.9 %copy-start.22 = (bf16[6,512,512]{2,1,0:T(8,128)(2,1)}, bf16[6,512,512]{2,1,0:T(8,128)(2,1)S(1)}, u32[]{:S(2)}) copy-start(bf16[6,512,512]{2,1,0:T(8,128)(2,1)S(1)} %get-tuple-element.53.weight_ref) | copy-start | bytes 9437188
  90.1 7.9 %copy-start.31 = (bf16[768,512]{1,0:T(8,128)(2,1)}, bf16[768,512]{1,0:T(8,128)(2,1)S(1)}, u32[]{:S(2)}) copy-start(bf16[768,512]{1,0:T(8,128)(2,1)S(1)} %get-tuple-element.54.q_t_ref) | copy-start | bytes 2359300
  90.1 10.4 %copy-start.43 = (s32[8]{0:T(128)S(1)}, s32[8]{0:T(128)}, u32[]{:S(2)}) copy-start(s32[8]{0:T(128)} %constant.29.clone) | copy-start | bytes 100
  91.2 26.1 %collective-permute-start.10 = (bf16[256,2048]{1,0:T(8,128)(2,1)}, bf16[256,2048]{1,0:T(8,128)(2,1)}, u32[]{:S(2)}, u32[]{:S(2)}) collective-permute-start(bf16[256,2048]{1,0:T(8,128)(2,1)} %shard_map.156), channel_id=1, source_target_pairs={{1,2},{2,1},{5,6},{6,5},{9,10},{10,9},{13,14},{14,13},{17,18},{18,... | collective-permute-start | bytes 3145736 | tf_op jit(solution)/shard_map/ppermute | solution.py:471
  95.4 24.2 %collective-permute-start.8 = (bf16[256,2048]{1,0:T(8,128)(2,1)}, bf16[256,2048]{1,0:T(8,128)(2,1)S(1)}, u32[]{:S(2)}, u32[]{:S(2)}) collective-permute-start(bf16[256,2048]{1,0:T(8,128)(2,1)} %collective-permute-done.7.refs_3_.refs_2_), channel_id=1, source_target_pairs={{1,0},{2,3},{5,4},{6,7},{9,8},{10,11},{13,12},{14,15},{17,16},{18,... | collective-permute-start | bytes 3145736 | tf_op jit(solution)/shard_map/ppermute | solution.py:474
  98.0 41.9 %collective-permute-start.6 = (bf16[256,2048]{1,0:T(8,128)(2,1)}, bf16[256,2048]{1,0:T(8,128)(2,1)}, u32[]{:S(2)}, u32[]{:S(2)}) collective-permute-start(bf16[256,2048]{1,0:T(8,128)(2,1)} %shard_map.152), channel_id=1, source_target_pairs={{1,2},{2,1},{5,6},{6,5},{9,10},{10,9},{13,14},{14,13},{17,18},{18,... | collective-permute-start | bytes 3145736 | tf_op jit(solution)/shard_map/ppermute | solution.py:471
  117.4 24.5 %collective-permute-start.11 = (bf16[256,2048]{1,0:T(8,128)(2,1)}, bf16[256,2048]{1,0:T(8,128)(2,1)}, u32[]{:S(2)}, u32[]{:S(2)}) collective-permute-start(bf16[256,2048]{1,0:T(8,128)(2,1)} %collective-permute-done.10.refs_2_.refs_3_), channel_id=1, source_target_pairs={{1,0},{2,3},{5,4},{6,7},{9,8},{10,11},{13,12},{14,15},{17,16},{18,... | collective-permute-start | bytes 3145736 | tf_op jit(solution)/shard_map/ppermute | solution.py:474
  128.9 3.7 %copy-start = (bf16[6144,768]{1,0:T(8,128)(2,1)S(1)}, bf16[6144,768]{1,0:T(8,128)(2,1)}, u32[]{:S(2)}) copy-start(bf16[6144,768]{1,0:T(8,128)(2,1)} %all-gather.3.cloned.1.call-done) | copy-start | bytes 28311556
  135.9 10.2 %slice-start = ((s8[9437184]{0:T(1024)(128)(4,1)}), s8[4194304]{0:T(1024)(128)(4,1)S(1)}, s32[]{:S(2)}) async-start(s8[9437184]{0:T(1024)(128)(4,1)} %bitcast.9), calls=%async_computation.1 | async-start | bytes 8388608
  135.9 10.2 %slice-start.1 = ((s8[9437184]{0:T(1024)(128)(4,1)}), s8[4194304]{0:T(1024)(128)(4,1)S(1)}, s32[]{:S(2)}) async-start(s8[9437184]{0:T(1024)(128)(4,1)} %bitcast.9), calls=%async_computation.2 | async-start | bytes 8388608
  139.9 6.3 %slice-start.2 = ((s8[9437184]{0:T(1024)(128)(4,1)}), s8[1048576]{0:T(1024)(128)(4,1)S(1)}, s32[]{:S(2)}) async-start(s8[9437184]{0:T(1024)(128)(4,1)} %bitcast.9), calls=%async_computation.3 | async-start | bytes 2097152
  139.9 21.2 %collective-permute-start.9 = (bf16[256,2048]{1,0:T(8,128)(2,1)}, bf16[256,2048]{1,0:T(8,128)(2,1)S(1)}, u32[]{:S(2)}, u32[]{:S(2)}) collective-permute-start(bf16[256,2048]{1,0:T(8,128)(2,1)} %shard_map.155.refs_2_.refs_3_), channel_id=1, source_target_pairs={{1,0},{2,3},{5,4},{6,7},{9,8},{10,11},{13,12},{14,15},{17,16},{18,... | collective-permute-start | bytes 3145736 | tf_op jit(solution)/shard_map/ppermute | solution.py:474
  146.1 3.7 %copy-start.4 = (bf16[4,768,384]{2,1,0:T(8,128)(2,1)S(1)}, bf16[4,768,384]{2,1,0:T(8,128)(2,1)}, u32[]{:S(2)}) copy-start(bf16[4,768,384]{2,1,0:T(8,128)(2,1)} %copy-done.3) | copy-start | bytes 7077892
  149.9 11.2 %copy-start.8 = (bf16[128,2048]{1,0:T(8,128)(2,1)S(1)}, bf16[128,2048]{1,0:T(8,128)(2,1)}, u32[]{:S(2)}) copy-start(bf16[128,2048]{1,0:T(8,128)(2,1)} %copy-done.7) | copy-start | bytes 1572868
  149.9 11.1 %copy-start.18 = (bf16[128,2048]{1,0:T(8,128)(2,1)S(1)}, bf16[128,2048]{1,0:T(8,128)(2,1)}, u32[]{:S(2)}) copy-start(bf16[128,2048]{1,0:T(8,128)(2,1)} %copy-done.17) | copy-start | bytes 1572868
  164.6 8.5 %collective-permute-start.13 = (bf16[4,768,384]{2,1,0:T(8,128)(2,1)S(1)}, bf16[4,768,384]{2,1,0:T(8,128)(2,1)S(1)}, u32[]{:S(2)}, u32[]{:S(2)}) collective-permute-start(bf16[4,768,384]{2,1,0:T(8,128)(2,1)S(1)} %get-tuple-element.60), channel_id=1, source_target_pairs={{0,4},{4,0},{8,12},{12,8},{16,20},{20,16},{24,28},{28,24},{1,5},{5... | collective-permute-start | bytes 7077896 | tf_op jit(solution)/shard_map/ppermute | solution.py:447
  169.0 7.5 %collective-permute-start.12 = (bf16[4,768,384]{2,1,0:T(8,128)(2,1)S(1)}, bf16[4,768,384]{2,1,0:T(8,128)(2,1)S(1)}, u32[]{:S(2)}, u32[]{:S(2)}) collective-permute-start(bf16[4,768,384]{2,1,0:T(8,128)(2,1)S(1)} %shard_map.162), channel_id=1, source_target_pairs={{0,4},{4,0},{8,12},{12,8},{16,20},{20,16},{24,28},{28,24},{1,5},{5... | collective-permute-start | bytes 7077896 | tf_op jit(solution)/shard_map/ppermute | solution.py:447
  169.1 7.4 %copy-start.23 = (bf16[6,512,512]{2,1,0:T(8,128)(2,1)S(1)}, bf16[6,512,512]{2,1,0:T(8,128)(2,1)}, u32[]{:S(2)}) copy-start(bf16[6,512,512]{2,1,0:T(8,128)(2,1)} %copy-done.22) | copy-start | bytes 9437188
  169.1 7.5 %copy-start.30 = (bf16[512,768]{1,0:T(8,128)(2,1)S(1)}, bf16[512,768]{1,0:T(8,128)(2,1)}, u32[]{:S(2)}) copy-start(bf16[512,768]{1,0:T(8,128)(2,1)} %get-tuple-element.44.att_ref) | copy-start | bytes 2359300
  169.1 7.5 %copy-start.32 = (bf16[768,512]{1,0:T(8,128)(2,1)S(1)}, bf16[768,512]{1,0:T(8,128)(2,1)}, u32[]{:S(2)}) copy-start(bf16[768,512]{1,0:T(8,128)(2,1)} %copy-done.31) | copy-start | bytes 2359300
  169.1 7.5 %copy-start.34 = (bf16[512,768]{1,0:T(8,128)(2,1)S(1)}, bf16[512,768]{1,0:T(8,128)(2,1)}, u32[]{:S(2)}) copy-start(bf16[512,768]{1,0:T(8,128)(2,1)} %copy-done.33) | copy-start | bytes 2359300
  169.1 7.5 %copy-start.36 = (bf16[512,768]{1,0:T(8,128)(2,1)S(1)}, bf16[512,768]{1,0:T(8,128)(2,1)}, u32[]{:S(2)}) copy-start(bf16[512,768]{1,0:T(8,128)(2,1)} %copy-done.35) | copy-start | bytes 2359300
  183.4 27.2 %collective-permute-start.19 = (bf16[2,768,384]{2,1,0:T(8,128)(2,1)S(1)}, bf16[2,768,384]{2,1,0:T(8,128)(2,1)S(1)}, u32[]{:S(2)}, u32[]{:S(2)}) collective-permute-start(bf16[2,768,384]{2,1,0:T(8,128)(2,1)S(1)} %get-tuple-element.74), channel_id=1, source_target_pairs={{0,16},{4,20},{8,24},{12,28},{16,0},{20,4},{24,8},{28,12},{1,17},{... | collective-permute-start | bytes 3538952 | tf_op jit(solution)/shard_map/ppermute | solution.py:447
  184.7 27.5 %collective-permute-start.17 = (bf16[2,768,384]{2,1,0:T(8,128)(2,1)S(1)}, bf16[2,768,384]{2,1,0:T(8,128)(2,1)S(1)}, u32[]{:S(2)}, u32[]{:S(2)}) collective-permute-start(bf16[2,768,384]{2,1,0:T(8,128)(2,1)S(1)} %get-tuple-element.72), channel_id=1, source_target_pairs={{0,8},{4,12},{8,0},{12,4},{16,24},{20,28},{24,16},{28,20},{1,9},{5... | collective-permute-start | bytes 3538952 | tf_op jit(solution)/shard_map/ppermute | solution.py:447
  185.9 42.0 %collective-permute-start.14 = (bf16[3,128,768]{2,1,0:T(8,128)(2,1)S(1)}, bf16[3,128,768]{2,1,0:T(8,128)(2,1)S(1)}, u32[]{:S(2)}, u32[]{:S(2)}) collective-permute-start(bf16[3,128,768]{2,1,0:T(8,128)(2,1)S(1)} %get-tuple-element.61), channel_id=1, source_target_pairs={{0,2},{1,3},{2,0},{3,1},{4,6},{5,7},{6,4},{7,5},{8,10},{9,11},{10,... | collective-permute-start | bytes 1769480 | tf_op jit(solution)/shard_map/ppermute | solution.py:447
  188.6 51.8 %collective-permute-start.15 = (bf16[3,128,768]{2,1,0:T(8,128)(2,1)S(1)}, bf16[3,128,768]{2,1,0:T(8,128)(2,1)S(1)}, u32[]{:S(2)}, u32[]{:S(2)}) collective-permute-start(bf16[3,128,768]{2,1,0:T(8,128)(2,1)S(1)} %get-tuple-element.62), channel_id=1, source_target_pairs={{0,3},{1,2},{2,1},{3,0},{4,7},{5,6},{6,5},{7,4},{8,11},{9,10},{10,... | collective-permute-start | bytes 1769480 | tf_op jit(solution)/shard_map/ppermute | solution.py:447
  189.2 36.7 %collective-permute-start.16 = (bf16[3,128,768]{2,1,0:T(8,128)(2,1)S(1)}, bf16[3,128,768]{2,1,0:T(8,128)(2,1)S(1)}, u32[]{:S(2)}, u32[]{:S(2)}) collective-permute-start(bf16[3,128,768]{2,1,0:T(8,128)(2,1)S(1)} %get-tuple-element.64), channel_id=1, source_target_pairs={{0,1},{1,0},{2,3},{3,2},{4,5},{5,4},{6,7},{7,6},{8,9},{9,8},{10,11... | collective-permute-start | bytes 1769480 | tf_op jit(solution)/shard_map/ppermute | solution.py:447
  211.0 31.0 %collective-permute-start.20 = (bf16[1,768,384]{2,1,0:T(8,128)(2,1)S(1)}, bf16[1,768,384]{2,1,0:T(8,128)(2,1)S(1)}, u32[]{:S(2)}, u32[]{:S(2)}) collective-permute-start(bf16[1,768,384]{2,1,0:T(8,128)(2,1)S(1)} %slice.46), channel_id=1, source_target_pairs={{0,8},{4,12},{8,0},{12,4},{16,24},{20,28},{24,16},{28,20},{1,9},{5... | collective-permute-start | bytes 1769480 | tf_op jit(solution)/shard_map/ppermute | solution.py:447
  212.6 29.6 %collective-permute-start.18 = (bf16[1,768,384]{2,1,0:T(8,128)(2,1)S(1)}, bf16[1,768,384]{2,1,0:T(8,128)(2,1)S(1)}, u32[]{:S(2)}, u32[]{:S(2)}) collective-permute-start(bf16[1,768,384]{2,1,0:T(8,128)(2,1)S(1)} %slice.47), channel_id=1, source_target_pairs={{0,16},{4,20},{8,24},{12,28},{16,0},{20,4},{24,8},{28,12},{1,17},{... | collective-permute-start | bytes 1769480 | tf_op jit(solution)/shard_map/ppermute | solution.py:447
  (21 other events, 27.8 us)
Sparse Core Ops, SparseCore 0:
  9.9 60.4 all-gather.2
